TPU v7x, 32 devices: a whole 2x2x4 slice. The times are simulated.
32 devices in a mesh: ctx: 8 (over z, y), head: 4 (over x, core).
Axes of the slice: x: 2, y: 2, z: 4, core: 2. Of those that a mesh axis runs over, the one named last changes fastest.
Arguments:
- query: bfloat16 [16384, 2048], P('ctx', 'head'), may hold values from -6 to 6
- key: bfloat16 [16384, 2048], P('ctx', 'head'), may hold values from -6 to 6
- value: bfloat16 [16384, 2048], P('ctx', 'head'), may hold values from -6 to 6
- gain: bfloat16 [2048], P('head'), may hold values from 0.099609375 to 1.8984375
- w_out: bfloat16 [2048, 2048], replicated, may hold values from -0.125 to 0.125
- d_out: bfloat16 [16384, 2048], P(('ctx', 'head')), may hold values from -6 to 6
Outputs:
- out: bfloat16 [16384, 2048], P(('ctx', 'head'))
- grad_query: bfloat16 [16384, 2048], P('ctx', 'head')
- grad_key: bfloat16 [16384, 2048], P('ctx', 'head')
- grad_value: bfloat16 [16384, 2048], P('ctx', 'head')
All inputs are finite; a program needn't handle non-finite values.
Results may differ from a plain program's by a relative error of at most 0.018.
Values may be sent and summed in bfloat16 or wider, within the bound.
No kernel may reach another device: no remote copies, remote signals or barrier semaphores. Data moves between devices by JAX's collectives and lax.ppermute only.
A program may use at most 128 MiB of HBM per device.

v0:
```python
import jax
import jax.numpy as jnp
from jax import lax
from jax.sharding import PartitionSpec as P

HDIM = 128
BLOCK = 128


epsilon = 1e-06


def earlier_states(local_total):
    position = lax.axis_index("ctx")
    piece = lax.all_gather(
        local_total[None].astype(jnp.bfloat16), "ctx", axis=0, tiled=True
    ).astype(jnp.float32)
    owners = jnp.arange(piece.shape[0], dtype=jnp.int32)
    keep = (owners < position)[:, None, None, None]
    return jnp.zeros_like(local_total) + jnp.sum(
        jnp.where(keep, piece, jnp.zeros_like(piece)), axis=0
    )


def later_states(local_total):
    position = lax.axis_index("ctx")
    piece = lax.all_gather(
        local_total[None].astype(jnp.bfloat16), "ctx", axis=0, tiled=True
    ).astype(jnp.float32)
    owners = jnp.arange(piece.shape[0], dtype=jnp.int32)
    keep = (owners > position)[:, None, None, None]
    return jnp.zeros_like(local_total) + jnp.sum(
        jnp.where(keep, piece, jnp.zeros_like(piece)), axis=0
    )


def on_device(query, key, value, gain, w_out, d_out):
    tokens, width = query.shape
    local_heads = width // HDIM
    nblocks = tokens // BLOCK
    causal = jnp.tril(jnp.ones((BLOCK, BLOCK), dtype=bool))[None, None]

    def split_blocks(array):
        return array.reshape(nblocks, BLOCK, local_heads, HDIM)

    def masked(scores):
        return jnp.where(causal, scores, jnp.zeros_like(scores)).astype(jnp.bfloat16)

    q_blocks = split_blocks(query)
    k_blocks = split_blocks(key)
    v_blocks = split_blocks(value)
    scores = masked(
        jnp.einsum("cshe,cthe->chst", q_blocks, k_blocks, preferred_element_type=jnp.float32)
    )
    block_states = jnp.einsum(
        "cshe,cshf->chef", k_blocks, v_blocks, preferred_element_type=jnp.float32
    )
    before = earlier_states(jnp.sum(block_states, axis=0))
    running = jnp.cumsum(block_states, axis=0)
    inner_before = jnp.concatenate([jnp.zeros_like(running[:1]), running[:-1]], axis=0)
    prefixes = (before[None] + inner_before).astype(jnp.bfloat16)
    attended = jnp.einsum("chst,cthf->cshf", scores, v_blocks, preferred_element_type=jnp.float32)
    attended = attended + jnp.einsum(
        "cshe,chef->cshf", q_blocks, prefixes, preferred_element_type=jnp.float32
    )
    attended = attended.reshape(tokens, local_heads, HDIM)
    inverse = lax.rsqrt(jnp.mean(attended * attended, axis=-1, keepdims=True) + epsilon)
    unit = attended * inverse
    scales = gain.astype(jnp.float32).reshape(local_heads, HDIM)
    normed = (unit * scales).astype(jnp.bfloat16).reshape(tokens, width)
    row_normed = lax.all_to_all(normed, "head", split_axis=0, concat_axis=1, tiled=True)
    out = jnp.dot(row_normed, w_out, preferred_element_type=jnp.float32).astype(jnp.bfloat16)
    grad_rows = lax.dot_general(
        d_out, w_out, (((1,), (1,)), ((), ())), preferred_element_type=jnp.float32
    )
    grad_heads = lax.all_to_all(
        grad_rows.astype(jnp.bfloat16), "head", split_axis=1, concat_axis=0, tiled=True
    )
    grad_unit = grad_heads.astype(jnp.float32).reshape(tokens, local_heads, HDIM) * scales
    grad_attended = inverse * (
        grad_unit - unit * jnp.mean(grad_unit * unit, axis=-1, keepdims=True)
    )
    g_blocks = split_blocks(grad_attended.astype(jnp.bfloat16))
    grad_scores = masked(
        jnp.einsum("cshf,cthf->chst", g_blocks, v_blocks, preferred_element_type=jnp.float32)
    )
    block_grads = jnp.einsum(
        "cshe,cshf->chef", q_blocks, g_blocks, preferred_element_type=jnp.float32
    )
    after = later_states(jnp.sum(block_grads, axis=0))
    tail_sums = jnp.cumsum(block_grads[::-1], axis=0)[::-1]
    inner_after = jnp.concatenate([tail_sums[1:], jnp.zeros_like(tail_sums[:1])], axis=0)
    suffixes = (after[None] + inner_after).astype(jnp.bfloat16)
    grad_query = jnp.einsum(
        "chst,cthe->cshe", grad_scores, k_blocks, preferred_element_type=jnp.float32
    )
    grad_query = grad_query + jnp.einsum(
        "cshf,chef->cshe", g_blocks, prefixes, preferred_element_type=jnp.float32
    )
    grad_key = jnp.einsum(
        "chst,cshe->cthe", grad_scores, q_blocks, preferred_element_type=jnp.float32
    )
    grad_key = grad_key + jnp.einsum(
        "cthf,chef->cthe", v_blocks, suffixes, preferred_element_type=jnp.float32
    )
    grad_value = jnp.einsum("chst,cshf->cthf", scores, g_blocks, preferred_element_type=jnp.float32)
    grad_value = grad_value + jnp.einsum(
        "cthe,chef->cthf", k_blocks, suffixes, preferred_element_type=jnp.float32
    )
    return (
        out,
        grad_query.reshape(tokens, width).astype(jnp.bfloat16),
        grad_key.reshape(tokens, width).astype(jnp.bfloat16),
        grad_value.reshape(tokens, width).astype(jnp.bfloat16),
    )


def solution(mesh):
    return jax.shard_map(
        on_device,
        mesh=mesh,
        in_specs=(
            P("ctx", "head"),
            P("ctx", "head"),
            P("ctx", "head"),
            P("head"),
            P(),
            P(("ctx", "head"), None),
        ),
        out_specs=(P(("ctx", "head"), None), P("ctx", "head"), P("ctx", "head"), P("ctx", "head")),
        check_vma=False,
    )
```

profile of v0, /device:TPU:0, one launch (start us, length us, event | category | flops | bytes accessed | tf_op | source)
XLA Modules:
  0.0 248.7 jit_solution(12250939265590448996)
XLA Ops:
  15.3 5.8 %fusion.31 = (bf16[4,128,128]{2,1,0:T(8,128)(2,1)}, f32[16,4,128,128]{3,2,1,0:T(8,128)}) fusion(bf16[16,128,4,128]{3,2,1,0:T(4,128)(2,1)} %reshape.122, bf16[16,128,4,128]{3,2,1,0:T(4,128)(2,1)} %reshape.121), kind=kOutput, calls=%fused_computation.59 | convolution fusion | flops 269418496 | bytes 8519680 | tf_op jit(solution)/shard_map/cshe,cshf->chef/dot_general | solution.py:55
  21.1 8.1 %convolution_convert_fusion = bf16[512,2048]{1,0:T(8,128)(2,1)S(1)} fusion(bf16[512,2048]{1,0:T(8,128)(2,1)S(1)} %copy-done, bf16[2048,2048]{1,0:T(8,128)(2,1)} %param.10), kind=kOutput, calls=%fused_computation.20 | convolution fusion | flops 4296015872 | bytes 12582912 | tf_op jit(solution)/shard_map/dot_general | solution.py:73
  30.7 4.5 %all-to-all-start.1 = ((bf16[512,4,512]{2,0,1:T(8,128)(2,1)}), bf16[512,4,512]{2,0,1:T(8,128)(2,1)}, u32[]{:S(2)}, u32[]{:S(2)}) async-start(bf16[512,4,512]{2,0,1:T(8,128)(2,1)} %bitcast.64), calls=%async_computation.1 | async-start | bytes 4194304 | tf_op jit(solution)/shard_map/all_to_all | solution.py:76
  35.7 4.8 %fusion.33 = f32[16,4,128,128]{3,2,1,0:T(8,128)} fusion(f32[16,4,128,128]{3,2,1,0:T(8,128)} %get-tuple-element.21), kind=kOutput, calls=%fused_computation.61 | output fusion | flops 15728640 | bytes 8388608 | tf_op jit(solution)/shard_map/jit(cumsum)/reduce_window_sum | solution.py:59
  43.2 4.6 %slice.12 = f32[15,4,128,128]{3,2,1,0:T(8,128)} slice(f32[16,4,128,128]{3,2,1,0:T(8,128)} %fusion.33), slice={[0:15], [0:4], [0:128], [0:128]} | slice | bytes 7864320 | tf_op jit(solution)/shard_map/slice | solution.py:60
  54.6 7.0 %all-to-all-done.1 = bf16[512,4,512]{2,0,1:T(8,128)(2,1)} async-done(((bf16[512,4,512]{2,0,1:T(8,128)(2,1)}), bf16[512,4,512]{2,0,1:T(8,128)(2,1)}, u32[]{:S(2)}, u32[]{:S(2)}) %all-to-all-start.1) | async-done | bytes 2097184 | tf_op jit(solution)/shard_map/all_to_all | solution.py:76
  65.7 5.2 %reshape.126 = f32[2048,4,128]{2,1,0:T(4,128)} reshape(f32[4,512,512]{2,1,0:T(8,128)} %convert_bitcast_fusion) | data formatting | bytes 8388608 | tf_op jit(solution)/shard_map/convert_element_type | solution.py:79
  71.0 5.2 %reshape.125 = f32[16,128,4,128]{3,2,1,0:T(4,128)} reshape(f32[4,512,512]{2,1,0:T(8,128)} %convert_bitcast_fusion) | data formatting | bytes 8388608 | tf_op jit(solution)/shard_map/convert_element_type | solution.py:79
  77.7 5.0 %multiply_reduce_fusion = (f32[16,128,4]{1,2,0:T(4,128)S(1)}, f32[16,128,4,128]{3,1,2,0:T(8,128)S(1)}) fusion(f32[15,4,128,128]{3,2,1,0:T(8,128)} %slice.12, f32[4,128,128]{2,1,0:T(8,128)S(1)} %fusion.8, bf16[16,128,4,128]{3,2,1,0:T(4,128)(2,1)S(1)} %reshape.120, f32[16,4,128,128]{3,2,1,0:T(8,128)} %fusion.14), kind=kOutput, calls=%fused_computation.17 | convolution fusion | flops 273670144 | bytes 14712832 | tf_op jit(solution)/shard_map/cshe,chef->cshf/dot_general | solution.py:63
  86.3 30.3 %fusion.3 = f32[2048,4]{1,0:T(8,128)S(1)} fusion(f32[2048,4,128]{2,0,1:T(8,128)} %bitcast.65, f32[2048,4,128]{2,1,0:T(4,128)} %reshape.126, f32[4,128]{1,0:T(4,128)S(1)} %get-tuple-element.18, f32[2048,4]{1,0:T(8,128)S(1)} %copy.105), kind=kLoop, calls=%fused_computation.7 | loop fusion | flops 4186112 | bytes 8456192 | tf_op jit(solution)/shard_map/reduce_sum | solution.py:81
  119.2 5.3 %fusion.6 = bf16[16,128,4,128]{3,1,2,0:T(8,128)(2,1)S(1)} fusion(f32[16,128,4,128]{3,2,1,0:T(4,128)} %reshape.125, f32[16,128,4,128]{3,1,2,0:T(8,128)} %copy-done.2, f32[16,128,4]{1,2,0:T(4,128)S(1)} %bitcast.74, f32[4,128]{1,0:T(4,128)S(1)} %get-tuple-element.18, f32[16,128,4]{1,2,0:T(4,128)S(1)} %get-tuple-element.16), kind=kLoop, calls=%fused_computation.11 | loop fusion | flops 6291456 | bytes 10553344 | tf_op jit(solution)/shard_map/convert_element_type | solution.py:83
  130.6 4.7 %copy.104 = f32[16,128,4,128]{3,2,1,0:T(4,128)} copy(f32[16,128,4,128]{3,1,2,0:T(8,128)S(1)} %copy-done.3) | data formatting | bytes 8388608 | tf_op jit(solution)/shard_map/add | solution.py:63
  135.3 4.7 %rev.4 = f32[16,4,128,128]{2,3,1,0:T(8,128)} reverse(f32[16,4,128,128]{2,3,1,0:T(8,128)} %get-tuple-element.25), dimensions={0} | reverse | bytes 8388608 | tf_op jit(solution)/shard_map/rev | solution.py:91
  140.0 5.3 %copy.122 = f32[16,4,128,128]{3,2,1,0:T(8,128)} copy(f32[16,4,128,128]{2,3,1,0:T(8,128)} %rev.4) | data formatting | bytes 8388608 | tf_op jit(solution)/shard_map/rev | solution.py:91
  150.5 4.5 %slice.11 = f32[15,4,128,128]{3,2,1,0:T(8,128)} reverse(f32[15,4,128,128]{3,2,1,0:T(8,128)} %slice.13), dimensions={0} | reverse | bytes 7864320 | tf_op jit(solution)/shard_map/slice | solution.py:92
  159.6 5.5 %mul.69 = f32[4,512,512]{2,1,0:T(8,128)} reshape(f32[2048,4,128]{2,1,0:T(4,128)} %mul.68) | data formatting | bytes 8388608 | tf_op jit(solution)/shard_map/mul | solution.py:68
  165.1 5.5 %reshape.123 = f32[4,512,512]{2,1,0:T(8,128)} reshape(f32[16,128,4,128]{3,2,1,0:T(4,128)} %copy.104) | data formatting | bytes 8388608 | tf_op jit(solution)/shard_map/reshape | solution.py:66
  170.6 5.9 %multiply_convert_fusion = bf16[4,512,512]{2,1,0:T(8,128)(2,1)} fusion(f32[4,512,512]{2,1,0:T(8,128)} %reshape.123, f32[4,512,512]{2,1,0:T(8,128)} %mul.69, f32[512]{0:T(512)S(1)} %copy-done.16), kind=kLoop, calls=%fused_computation.16 | loop fusion | flops 3145728 | bytes 10487808 | tf_op jit(solution)/shard_map/convert_element_type | solution.py:70
  176.5 4.7 %all-to-all-start = ((bf16[4,512,512]{2,1,0:T(8,128)(2,1)}), bf16[4,512,512]{2,1,0:T(8,128)(2,1)}, u32[]{:S(2)}, u32[]{:S(2)}) async-start(bf16[4,512,512]{2,1,0:T(8,128)(2,1)} %multiply_convert_fusion), calls=%async_computation | async-start | bytes 4194304 | tf_op jit(solution)/shard_map/all_to_all | solution.py:71
  196.6 10.3 %all-to-all-done = bf16[4,512,512]{2,1,0:T(8,128)(2,1)} async-done(((bf16[4,512,512]{2,1,0:T(8,128)(2,1)}), bf16[4,512,512]{2,1,0:T(8,128)(2,1)}, u32[]{:S(2)}, u32[]{:S(2)}) %all-to-all-start) | async-done | bytes 2097184 | tf_op jit(solution)/shard_map/all_to_all | solution.py:71
  209.7 9.3 %convolution_convert_fusion.1 = bf16[512,2048]{1,0:T(8,128)(2,1)} fusion(bf16[512,2048]{0,1:T(8,128)(2,1)S(1)} %bitcast.70, bf16[2048,2048]{1,0:T(8,128)(2,1)} %param.10), kind=kOutput, calls=%fused_computation.21 | convolution fusion | flops 4296015872 | bytes 12582912 | tf_op jit(solution)/shard_map/dot_general | solution.py:72
  220.6 5.7 %fusion = bf16[16,128,4,128]{3,1,2,0:T(8,128)(2,1)S(1)} fusion(f32[16,4,128,128]{3,2,1,0:T(8,128)} %fusion.22, bf16[16,128,4,128]{3,2,1,0:T(4,128)(2,1)} %reshape.122, f32[15,4,128,128]{3,2,1,0:T(8,128)} %slice.11, f32[4,128,128]{2,1,0:T(8,128)S(1)} %fusion.7), kind=kOutput, calls=%fused_computation.1 | convolution fusion | flops 272629760 | bytes 12582912 | tf_op jit(solution)/shard_map/cthf,chef->cthe/dot_general | solution.py:103
  232.3 4.2 %copy.141 = bf16[16,128,4,128]{3,2,1,0:T(4,128)(2,1)} copy(bf16[16,128,4,128]{1,3,2,0:T(8,128)(2,1)} %fusion.9) | data formatting | bytes 4194304
  236.6 5.1 %copy_bitcast_fusion = (bf16[2048,512]{1,0:T(8,128)(2,1)}, bf16[2048,512]{1,0:T(8,128)(2,1)}) fusion(bf16[256,8,4,128]{3,2,1,0:T(4,128)(2,1)} %bitcast.68, bf16[256,8,4,128]{3,2,1,0:T(4,128)(2,1)} %bitcast.67), kind=kLoop, calls=%fused_computation.23 | loop fusion | bytes 8388608
  (77 shorter events, 72.9 us)
Async XLA Ops:
  7.2 13.9 %copy-start = (bf16[512,2048]{1,0:T(8,128)(2,1)S(1)}, bf16[512,2048]{1,0:T(8,128)(2,1)}, u32[]{:S(2)}) copy-start(bf16[512,2048]{1,0:T(8,128)(2,1)} %param.11) | copy-start | bytes 6291460
  7.2 69.0 %all-gather.5.cloned.1.call-start = ((), (), s32[]{:S(2)}) async-start(), calls=%async_computation.2 | async-start | bytes 1179648 | tf_op jit(solution)/shard_map/all_gather | solution.py:15
  30.7 30.9 %all-to-all-start.1 = ((bf16[512,4,512]{2,0,1:T(8,128)(2,1)}), bf16[512,4,512]{2,0,1:T(8,128)(2,1)}, u32[]{:S(2)}, u32[]{:S(2)}) async-start(bf16[512,4,512]{2,0,1:T(8,128)(2,1)} %bitcast.64), calls=%async_computation.1 | async-start | bytes 4194304 | tf_op jit(solution)/shard_map/all_to_all | solution.py:76
  35.2 183.9 %all-gather.7.cloned.1.call-start = ((), (), s32[]{:S(2)}) async-start(), calls=%async_computation.3 | async-start | bytes 1179648 | tf_op jit(solution)/shard_map/all_gather | solution.py:27
  43.2 5.2 %copy-start.17 = (bf16[512]{0:T(512)(128)(2,1)S(1)}, bf16[512]{0:T(512)(128)(2,1)}, u32[]{:S(2)}) copy-start(bf16[512]{0:T(512)(128)(2,1)} %param.9) | copy-start | bytes 3076
  43.2 5.8 %copy-start.6 = (bf16[16,128,4,128]{3,2,1,0:T(4,128)(2,1)S(1)}, bf16[16,128,4,128]{3,2,1,0:T(4,128)(2,1)}, u32[]{:S(2)}) copy-start(bf16[16,128,4,128]{3,2,1,0:T(4,128)(2,1)} %reshape.121) | copy-start | bytes 6291460
  49.0 2.9 %copy-start.8 = (bf16[16,128,4,128]{3,2,1,0:T(4,128)(2,1)S(1)}, bf16[16,128,4,128]{3,2,1,0:T(4,128)(2,1)}, u32[]{:S(2)}) copy-start(bf16[16,128,4,128]{3,2,1,0:T(4,128)(2,1)} %reshape.122) | copy-start | bytes 6291460
  50.5 1.3 copy-start.13
  82.7 3.2 %copy-start.2 = (f32[16,128,4,128]{3,1,2,0:T(8,128)}, f32[16,128,4,128]{3,1,2,0:T(8,128)S(1)}, u32[]{:S(2)}) copy-start(f32[16,128,4,128]{3,1,2,0:T(8,128)S(1)} %get-tuple-element.23) | copy-start | bytes 12582916
  124.5 2.9 %copy-start.10 = (bf16[16,128,4,128]{3,1,2,0:T(8,128)(2,1)}, bf16[16,128,4,128]{3,1,2,0:T(8,128)(2,1)S(1)}, u32[]{:S(2)}) copy-start(bf16[16,128,4,128]{3,1,2,0:T(8,128)(2,1)S(1)} %fusion.6) | copy-start | bytes 6291460
  124.5 3.2 %copy-start.9 = (bf16[16,128,4,128]{3,2,1,0:T(4,128)(2,1)S(1)}, bf16[16,128,4,128]{3,2,1,0:T(4,128)(2,1)}, u32[]{:S(2)}) copy-start(bf16[16,128,4,128]{3,2,1,0:T(4,128)(2,1)} %reshape.122) | copy-start | bytes 6291460
  127.7 2.9 %copy-start.3 = (f32[16,128,4,128]{3,1,2,0:T(8,128)S(1)}, f32[16,128,4,128]{3,1,2,0:T(8,128)}, u32[]{:S(2)}) copy-start(f32[16,128,4,128]{3,1,2,0:T(8,128)} %copy-done.2) | copy-start | bytes 12582916
  165.1 5.5 %copy-start.16 = (f32[512]{0:T(512)S(1)}, f32[512]{0:T(512)}, u32[]{:S(2)}) copy-start(f32[512]{0:T(512)} %get-tuple-element.19) | copy-start | bytes 6148
  176.5 30.4 %all-to-all-start = ((bf16[4,512,512]{2,1,0:T(8,128)(2,1)}), bf16[4,512,512]{2,1,0:T(8,128)(2,1)}, u32[]{:S(2)}, u32[]{:S(2)}) async-start(bf16[4,512,512]{2,1,0:T(8,128)(2,1)} %multiply_convert_fusion), calls=%async_computation | async-start | bytes 4194304 | tf_op jit(solution)/shard_map/all_to_all | solution.py:71
  181.2 3.4 %copy-start.4 = (f32[15,4,128,128]{3,2,1,0:T(8,128)S(1)}, f32[15,4,128,128]{3,2,1,0:T(8,128)}, u32[]{:S(2)}) copy-start(f32[15,4,128,128]{3,2,1,0:T(8,128)} %slice.12) | copy-start | bytes 11796484
  181.2 4.1 %copy-start.11 = (bf16[16,128,4,128]{3,1,2,0:T(8,128)(2,1)S(1)}, bf16[16,128,4,128]{3,1,2,0:T(8,128)(2,1)}, u32[]{:S(2)}) copy-start(bf16[16,128,4,128]{3,1,2,0:T(8,128)(2,1)} %copy-done.10) | copy-start | bytes 6291460
  188.7 2.2 copy-start.15
  191.0 2.8 %copy-start.14 = (bf16[16,4,128,128]{3,2,1,0:T(8,128)(2,1)S(1)}, bf16[16,4,128,128]{3,2,1,0:T(8,128)(2,1)}, u32[]{:S(2)}) copy-start(bf16[16,4,128,128]{3,2,1,0:T(8,128)(2,1)} %copy-done.13) | copy-start | bytes 6291460
  209.7 9.4 %copy-start.18 = (pred[8]{0:T(512)(128)(4,1)S(1)}, pred[8]{0:T(512)(128)(4,1)}, u32[]{:S(2)}) copy-start(pred[8]{0:T(512)(128)(4,1)} %iota_compare_fusion.1) | copy-start | bytes 28
  220.6 8.8 %copy-start.7 = (bf16[16,128,4,128]{3,2,1,0:T(4,128)(2,1)S(1)}, bf16[16,128,4,128]{3,2,1,0:T(4,128)(2,1)}, u32[]{:S(2)}) copy-start(bf16[16,128,4,128]{3,2,1,0:T(4,128)(2,1)} %reshape.121) | copy-start | bytes 6291460
  220.6 8.8 %copy-start.12 = (f32[16,4,128,128]{3,2,1,0:T(8,128)S(1)}, f32[16,4,128,128]{3,2,1,0:T(8,128)}, u32[]{:S(2)}) copy-start(f32[16,4,128,128]{3,2,1,0:T(8,128)} %fusion.35) | copy-start | bytes 12582916
  226.3 3.1 %copy-start.5 = (f32[15,4,128,128]{3,2,1,0:T(8,128)S(1)}, f32[15,4,128,128]{3,2,1,0:T(8,128)}, u32[]{:S(2)}) copy-start(f32[15,4,128,128]{3,2,1,0:T(8,128)} %slice.11) | copy-start | bytes 11796484
  236.6 5.1 %copy-start.1 = (bf16[512,2048]{1,0:T(8,128)(2,1)S(1)}, bf16[512,2048]{1,0:T(8,128)(2,1)}, u32[]{:S(2)}) copy-start(bf16[512,2048]{1,0:T(8,128)(2,1)} %param.11) | copy-start | bytes 6291460
Sparse Core Ops, SparseCore 0:
  21.2 42.8 all-gather.4
  155.9 41.2 all-gather.6
where the time goes:
time: 254 us; the launch traced here: 249 us
  local copies, waits for them, and re-layouts  91.3 us (36%)
  other arithmetic  58.5 us (23%)
  matrix products  57.3 us (23%)
  waiting for transfers between devices  17.4 us (7%)
  between operations  14.6 us (6%)
  starting transfers between devices  9.71 us (4%)
    reduce_sum x1, other arithmetic, on_device(): jnp.mean(grad_unit * unit, axis=-1, keepdims=True)  30.3 us
    unnamed x44, local copies, waits for them, and re-layouts  21 us
    reshape x3, local copies, waits for them, and re-layouts, split_blocks(): return array.reshape(nblocks, BLOCK, local_heads, HDIM)  10.6 us
    convert_element_type x2, local copies, waits for them, and re-layouts, on_device(): grad_heads.astype(jnp.float32).reshape(tokens, local_heads, HDIM) * scales  10.5 us
    all_to_all x1, waiting for transfers between devices, on_device(): lax.all_to_all(normed, 'head', split_axis=0, concat_axis=1, tiled=True)  10.3 us
    rev x2, local copies, waits for them, and re-layouts, on_device(): tail_sums = jnp.cumsum(block_grads[::-1], axis=0)[::-1]  10.1 us
    dot_general x1, matrix products, on_device(): jnp.dot(row_normed, w_out, preferred_element_type=jnp.float32)  9.35 us
    mul x2, local copies, waits for them, and re-layouts, on_device(): unit = attended * inverse  9.32 us
  transfers between devices with their start and end apart: 4, of which 2 were waited for; matrix products, arithmetic and copies ran while one was open for 36% of the time, Pallas kernels for 0%

commit v1 on v0

v1 whole, which is shorter than its diff:
```python
import functools

import jax
import jax.numpy as jnp
from jax import lax
from jax.experimental import pallas as pl
from jax.experimental.pallas import tpu as pltpu
from jax.sharding import PartitionSpec as P

HDIM = 128
BLOCK = 128
epsilon = 1e-06
f32 = jnp.float32
bf16 = jnp.bfloat16
MIB = 1 << 20


def mm(a, b, ca, cb):
    return lax.dot_general(a, b, (((ca,), (cb,)), ((), ())), preferred_element_type=f32)


def params(mib, dims=1):
    return pltpu.CompilerParams(
        vmem_limit_bytes=mib * MIB, dimension_semantics=("arbitrary",) * dims
    )


def keep_causal(scores):
    row = lax.broadcasted_iota(jnp.int32, (BLOCK, BLOCK), 0)
    col = lax.broadcasted_iota(jnp.int32, (BLOCK, BLOCK), 1)
    return jnp.where(col <= row, scores, 0.0).astype(bf16)


def grad_rows_kernel(npieces, me_ref, d_ref, *refs):
    w_refs, o_refs, acc_refs = refs[:npieces], refs[npieces : 2 * npieces], refs[2 * npieces :]
    step, last = pl.program_id(0), pl.num_programs(0) - 1
    for w_ref, o_ref, acc_ref in zip(w_refs, o_refs, acc_refs):
        part = mm(d_ref[...], w_ref[...], 1, 1)

        @pl.when(step == 0)
        def _():
            acc_ref[...] = part

        @pl.when((step > 0) & (step < last))
        def _():
            acc_ref[...] += part

        @pl.when(step == last)
        def _():
            o_ref[...] = (acc_ref[...] + part).astype(bf16)


def grad_rows(me, d_out, w_out, pieces, chunks, cols):
    rows, model = d_out.shape
    tile = min(512, model)
    n = len(pieces)

    def w_spec(dist, chunk):
        return pl.BlockSpec((cols, tile), lambda k, m: ((m[0] ^ dist) * chunks + chunk, k))

    return pl.pallas_call(
        functools.partial(grad_rows_kernel, n),
        grid_spec=pltpu.PrefetchScalarGridSpec(
            num_scalar_prefetch=1,
            grid=(model // tile,),
            in_specs=[pl.BlockSpec((rows, tile), lambda k, m: (0, k))]
            + [w_spec(*piece) for piece in pieces],
            out_specs=[pl.BlockSpec((rows, cols), lambda k, m: (0, 0))] * n,
            scratch_shapes=[pltpu.VMEM((rows, cols), f32)] * n,
        ),
        out_shape=[jax.ShapeDtypeStruct((rows, cols), bf16)] * n,
        compiler_params=params(24),
        name="grad_rows",
    )(me, d_out, *([w_out] * n))


def total_kernel(k_ref, v_ref, o_ref):
    @pl.when(pl.program_id(0) == 0)
    def _():
        o_ref[...] = jnp.zeros_like(o_ref)

    for h in range(o_ref.shape[0]):
        cols = slice(h * HDIM, (h + 1) * HDIM)
        o_ref[h] += mm(k_ref[:, cols], v_ref[:, cols], 0, 0)


def total_state(key, value):
    tokens, width = key.shape
    tile = min(512, tokens)
    spec = pl.BlockSpec((tile, width), lambda i: (i, 0))
    heads = width // HDIM
    return pl.pallas_call(
        total_kernel,
        grid=(tokens // tile,),
        in_specs=[spec, spec],
        out_specs=pl.BlockSpec((heads, HDIM, HDIM), lambda i: (0, 0, 0)),
        out_shape=jax.ShapeDtypeStruct((heads, HDIM, HDIM), f32),
        compiler_params=params(24),
        name="total_state",
    )(key, value)


def forward_kernel(nhead, me_ref, q_ref, k_ref, v_ref, gain_ref, before_ref, *refs):
    n_refs = refs[:nhead]
    att_ref, s_ref, st_ref, run_ref, row_ref = refs[nhead:]
    step = pl.program_id(0)
    heads = before_ref.shape[0]

    @pl.when(step == 0)
    def _():
        run_ref[...] = before_ref[...]

    for h in range(heads):
        cols = slice(h * HDIM, (h + 1) * HDIM)
        gain = gain_ref[:, cols].astype(f32)
        run = run_ref[h]
        for b in range(q_ref.shape[0] // BLOCK):
            rows = slice(b * BLOCK, (b + 1) * BLOCK)
            q, k, v = q_ref[rows, cols], k_ref[rows, cols], v_ref[rows, cols]
            scores = keep_causal(mm(q, k, 1, 1))
            state = run.astype(bf16)
            attended = mm(scores, v, 1, 0) + mm(q, state, 1, 0)
            run = run + mm(k, v, 0, 0)
            inverse = lax.rsqrt(jnp.mean(attended * attended, axis=-1, keepdims=True) + epsilon)
            row_ref[rows, cols] = (attended * inverse * gain).astype(bf16)
            att_ref[rows, cols] = attended
            s_ref[rows, cols] = scores
            st_ref[rows, cols] = state
        run_ref[h] = run

    owner = step ^ me_ref[0]
    for dist, n_ref in enumerate(n_refs):

        @pl.when(owner == dist)
        def _():
            n_ref[...] = row_ref[...]


def forward(me, query, key, value, gain, before, chunk, cols, nhead):
    tokens, width = query.shape
    tile = tokens // nhead
    heads = cols // HDIM
    spec = pl.BlockSpec((tile, cols), lambda i, m: (i, chunk))
    local = pl.BlockSpec((tile, cols), lambda i, m: (i, 0))
    whole = pl.BlockSpec((tile, cols), lambda i, m: (0, 0))
    outs = pl.pallas_call(
        functools.partial(forward_kernel, nhead),
        grid_spec=pltpu.PrefetchScalarGridSpec(
            num_scalar_prefetch=1,
            grid=(nhead,),
            in_specs=[
                spec,
                spec,
                spec,
                pl.BlockSpec((1, cols), lambda i, m: (0, chunk)),
                pl.BlockSpec((heads, HDIM, HDIM), lambda i, m: (chunk, 0, 0)),
            ],
            out_specs=[whole] * nhead + [local] * 3,
            scratch_shapes=[pltpu.VMEM((heads, HDIM, HDIM), f32), pltpu.VMEM((tile, cols), bf16)],
        ),
        out_shape=[jax.ShapeDtypeStruct((tile, cols), bf16)] * nhead
        + [jax.ShapeDtypeStruct((tokens, cols), kind) for kind in (f32, bf16, bf16)],
        compiler_params=params(32),
        name="forward",
    )(me, query, key, value, gain, before)
    return outs[:nhead], outs[nhead:]


def backward_kernel(nhead, aliased, me_ref, *refs):
    p_refs = refs[:nhead]
    q_ref, k_ref, v_ref, gain_ref, att_ref, st_ref = refs[nhead : nhead + 6]
    gq_ref, g_ref, gs_ref, tot_ref, row_ref = refs[nhead + 6 + aliased :]
    step = pl.program_id(0)
    heads = tot_ref.shape[0]

    @pl.when(step == 0)
    def _():
        tot_ref[...] = jnp.zeros_like(tot_ref)

    for dist, p_ref in enumerate(p_refs):

        @pl.when(step == dist)
        def _():
            row_ref[...] = p_ref[...]

    for h in range(heads):
        cols = slice(h * HDIM, (h + 1) * HDIM)
        gain = gain_ref[:, cols].astype(f32)
        total = tot_ref[h]
        for b in range(q_ref.shape[0] // BLOCK):
            rows = slice(b * BLOCK, (b + 1) * BLOCK)
            q, k, v = q_ref[rows, cols], k_ref[rows, cols], v_ref[rows, cols]
            attended = att_ref[rows, cols]
            inverse = lax.rsqrt(jnp.mean(attended * attended, axis=-1, keepdims=True) + epsilon)
            unit = attended * inverse
            grad_unit = row_ref[rows, cols].astype(f32) * gain
            along = jnp.mean(grad_unit * unit, axis=-1, keepdims=True)
            g = (inverse * (grad_unit - unit * along)).astype(bf16)
            grad_scores = keep_causal(mm(g, v, 1, 1))
            grad_q = mm(grad_scores, k, 1, 0) + mm(g, st_ref[rows, cols], 1, 1)
            total = total + mm(q, g, 0, 0)
            gq_ref[rows, cols] = grad_q.astype(bf16)
            g_ref[rows, cols] = g
            gs_ref[rows, cols] = grad_scores
        tot_ref[h] = total


def backward(me, pieces, query, key, value, gain, attended, states, into, chunk, cols, nhead):
    tokens, width = query.shape
    tile = tokens // nhead
    heads = cols // HDIM
    spec = pl.BlockSpec((tile, cols), lambda i, m: (i ^ m[0], chunk))
    local = pl.BlockSpec((tile, cols), lambda i, m: (i ^ m[0], 0))
    whole = pl.BlockSpec((tile, cols), lambda i, m: (0, 0))
    in_specs = (
        [whole] * nhead
        + [spec] * 3
        + [pl.BlockSpec((1, cols), lambda i, m: (0, chunk)), local, local]
    )
    extra = [] if into is None else [into]
    return pl.pallas_call(
        functools.partial(backward_kernel, nhead, len(extra)),
        grid_spec=pltpu.PrefetchScalarGridSpec(
            num_scalar_prefetch=1,
            grid=(nhead,),
            in_specs=in_specs + [pl.BlockSpec(memory_space=pl.ANY)] * len(extra),
            out_specs=[
                spec,
                local,
                local,
                pl.BlockSpec((heads, HDIM, HDIM), lambda i, m: (0, 0, 0)),
            ],
            scratch_shapes=[pltpu.VMEM((tile, cols), bf16)],
        ),
        out_shape=[
            jax.ShapeDtypeStruct((tokens, width), bf16),
            jax.ShapeDtypeStruct((tokens, cols), bf16),
            jax.ShapeDtypeStruct((tokens, cols), bf16),
            jax.ShapeDtypeStruct((heads, HDIM, HDIM), f32),
        ],
        input_output_aliases={1 + len(in_specs): 0} if extra else {},
        compiler_params=params(32),
        name="backward",
    )(me, *pieces, query, key, value, gain, attended, states, *extra)


def later_kernel(aliased, q_ref, k_ref, v_ref, g_ref, s_ref, gs_ref, after_ref, *refs):
    gk_ref, gv_ref, run_ref = refs[aliased:]
    heads = after_ref.shape[0]

    @pl.when(pl.program_id(0) == 0)
    def _():
        run_ref[...] = after_ref[...]

    for h in range(heads):
        cols = slice(h * HDIM, (h + 1) * HDIM)
        run = run_ref[h]
        for b in reversed(range(q_ref.shape[0] // BLOCK)):
            rows = slice(b * BLOCK, (b + 1) * BLOCK)
            q, k, v, g = q_ref[rows, cols], k_ref[rows, cols], v_ref[rows, cols], g_ref[rows, cols]
            later = run.astype(bf16)
            grad_k = mm(gs_ref[rows, cols], q, 0, 0) + mm(v, later, 1, 1)
            grad_v = mm(s_ref[rows, cols], g, 0, 0) + mm(k, later, 1, 0)
            run = run + mm(q, g, 0, 0)
            gk_ref[rows, cols] = grad_k.astype(bf16)
            gv_ref[rows, cols] = grad_v.astype(bf16)
        run_ref[h] = run


def later_grads(query, key, value, g, scores, grad_scores, after, into, chunk, cols, tile):
    tokens, width = query.shape
    heads = cols // HDIM
    steps = tokens // tile
    spec = pl.BlockSpec((tile, cols), lambda i: (steps - 1 - i, chunk))
    local = pl.BlockSpec((tile, cols), lambda i: (steps - 1 - i, 0))
    extra = [] if into is None else list(into)
    return pl.pallas_call(
        functools.partial(later_kernel, len(extra)),
        grid=(steps,),
        in_specs=[spec] * 3
        + [local] * 3
        + [pl.BlockSpec((heads, HDIM, HDIM), lambda i: (0, 0, 0))]
        + [pl.BlockSpec(memory_space=pl.ANY)] * len(extra),
        out_specs=[spec, spec],
        scratch_shapes=[pltpu.VMEM((heads, HDIM, HDIM), f32)],
        out_shape=[jax.ShapeDtypeStruct((tokens, width), bf16)] * 2,
        input_output_aliases={7: 0, 8: 1} if extra else {},
        compiler_params=params(32),
        name="later_grads",
    )(query, key, value, g, scores, grad_scores, after, *extra)


def project_kernel(n, with_acc, me_ref, *refs):
    x_refs, w_refs = refs[:n], refs[n : 2 * n]
    o_ref = refs[-1]
    total = refs[2 * n][...] if with_acc else None
    for x_ref, w_ref in zip(x_refs, w_refs):
        part = mm(x_ref[...], w_ref[...], 1, 0)
        total = part if total is None else total + part
    o_ref[...] = total.astype(o_ref.dtype)


def project(me, pieces, xs, w_out, acc, chunks, kind):
    rows, cols = xs[0].shape
    model = w_out.shape[1]
    tile = min(512, model)
    n = len(pieces)

    def w_spec(dist, chunk):
        return pl.BlockSpec((cols, tile), lambda j, m: ((m[0] ^ dist) * chunks + chunk, j))

    wide = pl.BlockSpec((rows, tile), lambda j, m: (0, j))
    extra = [] if acc is None else [acc]
    return pl.pallas_call(
        functools.partial(project_kernel, n, len(extra)),
        grid_spec=pltpu.PrefetchScalarGridSpec(
            num_scalar_prefetch=1,
            grid=(model // tile,),
            in_specs=[pl.BlockSpec((rows, cols), lambda j, m: (0, 0))] * n
            + [w_spec(*piece) for piece in pieces]
            + [wide] * len(extra),
            out_specs=wide,
        ),
        out_shape=jax.ShapeDtypeStruct((rows, model), kind),
        compiler_params=params(32),
        name="project",
    )(me, *xs, *([w_out] * n), *extra)


def on_device(nctx, nhead, query, key, value, gain, w_out, d_out):
    tokens, width = query.shape
    local_heads = width // HDIM
    chunks = 2 if local_heads % 2 == 0 else 1
    cols = width // chunks
    me = lax.axis_index("head").astype(jnp.int32).reshape(1)
    place = lax.axis_index("ctx")
    gain = gain.reshape(1, width)

    def swap(array, dist):
        if dist == 0:
            return array
        return lax.ppermute(array, "head", [(i, i ^ dist) for i in range(nhead)])

    def others(total, later):
        outside = jnp.zeros_like(total)
        dist = 1
        while dist < nctx:
            got = lax.ppermute(
                total.astype(bf16), "ctx", [(i, i ^ dist) for i in range(nctx)]
            ).astype(f32)
            wanted = ((place & dist) == 0) == later
            outside = outside + jnp.where(wanted, got, 0.0)
            total = total + got
            dist *= 2
        return outside

    far = [d for d in range(nhead - 1, 0, -1) if d > 1] or []
    near = [d for d in range(nhead) if d <= 1]
    sent = {}
    for c in range(chunks):
        if far:
            pieces = [(d, c) for d in far]
            sent.update(zip(pieces, grad_rows(me, d_out, w_out, pieces, chunks, cols)))
    pieces = [(d, c) for d in near for c in range(chunks)]
    sent.update(zip(pieces, grad_rows(me, d_out, w_out, pieces, chunks, cols)))
    got = {(d, c): swap(sent[d, c], d) for c in range(chunks) for d in reversed(range(nhead))}

    before = others(total_state(key, value), False)

    kept, normed = [], {}
    for c in range(chunks):
        parts, saved = forward(me, query, key, value, gain, before, c, cols, nhead)
        kept.append(saved)
        for d in reversed(range(nhead)):
            normed[d, c] = swap(parts[d], d)

    grad_query, carried = None, []
    for c in range(chunks):
        attended, scores, states = kept[c]
        grad_query, g, grad_scores, total = backward(
            me,
            [got[d, c] for d in range(nhead)],
            query,
            key,
            value,
            gain,
            attended,
            states,
            grad_query,
            c,
            cols,
            nhead,
        )
        carried.append((g, scores, grad_scores, others(total, True)))
    grads = None
    for c in range(chunks):
        grads = later_grads(
            query, key, value, *carried[c], grads, c, cols, tokens // nhead
        )

    last = [(d, chunks - 1) for d in far]
    first = [p for p in normed if p not in last]
    acc = project(
        me, first, [normed[p] for p in first], w_out, None, chunks, f32 if last else bf16
    )
    if last:
        acc = project(me, last, [normed[p] for p in last], w_out, acc, chunks, bf16)
    return acc, grad_query, grads[0], grads[1]


def solution(mesh):
    nctx, nhead = mesh.shape["ctx"], mesh.shape["head"]
    return jax.shard_map(
        functools.partial(on_device, nctx, nhead),
        mesh=mesh,
        in_specs=(
            P("ctx", "head"),
            P("ctx", "head"),
            P("ctx", "head"),
            P("head"),
            P(),
            P(("ctx", "head"), None),
        ),
        out_specs=(P(("ctx", "head"), None), P("ctx", "head"), P("ctx", "head"), P("ctx", "head")),
        check_vma=False,
    )
```

time: 254 us -> 114 us (0.45); the launches traced: 249 us -> 114 us
  local copies, waits for them, and re-layouts: 91.3 us -> 9.77 us
  Pallas kernels: 0 us -> 68.2 us
  matrix products: 57.3 us -> 0 us
  other arithmetic: 58.5 us -> 1.33 us
  between operations: 14.6 us -> 0.84 us
  starting transfers between devices: 9.71 us -> 18.1 us
    pallas_call x0 -> x12, Pallas kernels: none -> 68.2 us  [the longest x3 19.5 us: grad_rows(): pl.pallas_call(functools.partial(grad_rows_kernel, n), grid_spec=pltpu.Pr...]
    dot_general x14 -> x0, matrix products: 57.3 us -> none  [the longest x1 9.35 us: on_device(): jnp.dot(row_normed, w_out, preferred_element_type=jnp.float32)]
    reduce_sum x3 -> x0, other arithmetic: 33.3 us -> none  [the longest x1 30.3 us: on_device(): jnp.mean(grad_unit * unit, axis=-1, keepdims=True)]
    ppermute x0 -> x21, starting transfers between devices: none -> 18.1 us  [the longest x9 11.2 us: others(): lax.ppermute(total.astype(bf16), 'ctx', [(i, i ^ dist) for i in range(nct...]
    all_to_all x2 -> x0, waiting for transfers between devices: 17.3 us -> none  [the longest x1 10.3 us: on_device(): lax.all_to_all(normed, 'head', split_axis=0, concat_axis=1, tiled=True)]
    reshape x4 -> x1, local copies, waits for them, and re-layouts: 16.1 us -> 0.01 us  [on_device(): gain = gain.reshape(1, width)]
    ppermute x0 -> x21, waiting for transfers between devices: none -> 15.3 us  [the longest x9 15.3 us: others(): lax.ppermute(total.astype(bf16), 'ctx', [(i, i ^ dist) for i in range(nct...]
    convert_element_type x3 -> x9, other arithmetic: 15.3 us -> 0.22 us  [others(): total.astype(bf16)]
  transfers between devices with their start and end apart: 4 -> 21, of which waited for: 2 -> 7; matrix products, arithmetic and copies ran while one was open for 36% -> 1% of each run, Pallas kernels for 0% -> 50%
where the time goes in v1:
time: 114 us
  Pallas kernels  68.2 us (60%)
  starting transfers between devices  18.1 us (16%)
  waiting for transfers between devices  15.3 us (13%)
  local copies, waits for them, and re-layouts  9.77 us (9%)
  other arithmetic  1.33 us (1%)
    pallas_call x3, Pallas kernels, grad_rows(): pl.pallas_call(functools.partial(grad_rows_kernel, n), grid_spec=pltpu.Pr...  19.5 us
    ppermute x9, waiting for transfers between devices, others(): lax.ppermute(total.astype(bf16), 'ctx', [(i, i ^ dist) for i in range(nct...  15.3 us
    pallas_call x2, Pallas kernels, backward(): pl.pallas_call(functools.partial(backward_kernel, nhead, len(extra)), gri...  13.5 us
    pallas_call x2, Pallas kernels, later_grads(): pl.pallas_call(functools.partial(later_kernel, len(extra)), grid=(steps,)...  12.8 us
    pallas_call x2, Pallas kernels, forward(): pl.pallas_call(functools.partial(forward_kernel, nhead), grid_spec=pltpu....  12.7 us
    ppermute x9, starting transfers between devices, others(): lax.ppermute(total.astype(bf16), 'ctx', [(i, i ^ dist) for i in range(nct...  11.2 us
    unnamed x24, local copies, waits for them, and re-layouts  9.76 us
    pallas_call x2, Pallas kernels, project(): pl.pallas_call(functools.partial(project_kernel, n, len(extra)), grid_spe...  8.19 us
  transfers between devices with their start and end apart: 21, of which 7 were waited for; matrix products, arithmetic and copies ran while one was open for 1% of the time, Pallas kernels for 50%

profile of v1, /device:TPU:0, one launch (start us, length us, event | category | flops | bytes accessed | tf_op | source)
XLA Modules:
  0.0 113.6 jit_solution(1053129659966109889)
XLA Ops:
  0.6 1.6 %copy-done.1 = bf16[2048,512]{1,0:T(8,128)(2,1)S(1)} copy-done((bf16[2048,512]{1,0:T(8,128)(2,1)S(1)}, bf16[2048,512]{1,0:T(8,128)(2,1)}, u32[]{:S(2)}) %copy-start.1) | copy-done | bytes 2097176
  2.2 1.6 %copy-done.3 = bf16[2048,512]{1,0:T(8,128)(2,1)S(1)} copy-done((bf16[2048,512]{1,0:T(8,128)(2,1)S(1)}, bf16[2048,512]{1,0:T(8,128)(2,1)}, u32[]{:S(2)}) %copy-start.3) | copy-done | bytes 2097176
  5.3 3.0 %collective-permute-start = (bf16[4,128,128]{2,1,0:T(8,128)(2,1)S(1)}, bf16[4,128,128]{2,1,0:T(8,128)(2,1)S(1)}, u32[]{:S(2)}, u32[]{:S(2)}) collective-permute-start(bf16[4,128,128]{2,1,0:T(8,128)(2,1)S(1)} %convert_element_type.54), channel_id=1, source_target_pairs={{0,4},{4,0},{8,12},{12,8},{16,20},{20,16},{24,28},{28,24},{1,5},{5... | collective-permute-start | bytes 393224 | tf_op jit(solution)/shard_map/ppermute | solution.py:348
  8.3 3.5 %collective-permute-done = bf16[4,128,128]{2,1,0:T(8,128)(2,1)S(1)} collective-permute-done((bf16[4,128,128]{2,1,0:T(8,128)(2,1)S(1)}, bf16[4,128,128]{2,1,0:T(8,128)(2,1)S(1)}, u32[]{:S(2)}, u32[]{:S(2)}) %collective-permute-start) | collective-permute-done | bytes 131104 | tf_op jit(solution)/shard_map/ppermute | solution.py:348
  11.9 1.9 %collective-permute-start.1 = (bf16[4,128,128]{2,1,0:T(8,128)(2,1)S(1)}, bf16[4,128,128]{2,1,0:T(8,128)(2,1)S(1)}, u32[]{:S(2)}, u32[]{:S(2)}) collective-permute-start(bf16[4,128,128]{2,1,0:T(8,128)(2,1)S(1)} %fusion.3), channel_id=1, source_target_pairs={{0,8},{4,12},{8,0},{12,4},{16,24},{20,28},{24,16},{28,20},{1,9},{5... | collective-permute-start | bytes 393224 | tf_op jit(solution)/shard_map/ppermute | solution.py:348
  13.7 3.4 %copy-done = bf16[2048,2048]{1,0:T(8,128)(2,1)S(1)} copy-done((bf16[2048,2048]{1,0:T(8,128)(2,1)S(1)}, bf16[2048,2048]{1,0:T(8,128)(2,1)}, u32[]{:S(2)}) %copy-start) | copy-done | bytes 8388632
  17.1 9.2 %grad_rows.3 = (bf16[512,256]{1,0:T(8,128)(2,1)S(1)}, bf16[512,256]{1,0:T(8,128)(2,1)S(1)}, bf16[512,256]{1,0:T(8,128)(2,1)S(1)}, bf16[512,256]{1,0:T(8,128)(2,1)}) custom-call(s32[1]{0:T(128)} %bitcast.me_ref, bf16[512,2048]{1,0:T(8,128)(2,1)S(1)} %copy-done.6, bf16[2048,2048]{1,0:T(8,128)(2,1)S(1)} %copy-done, bf16[2048,2048]{1,0:T(8,128)(2,1)S(1)} %copy-done, ...), custom_call_target="tpu_custom_call" | custom-call | tf_op jit(solution)/shard_map/grad_rows/pallas_call | solution.py:61
  26.4 2.7 %collective-permute-start.2 = (bf16[4,128,128]{2,1,0:T(8,128)(2,1)S(1)}, bf16[4,128,128]{2,1,0:T(8,128)(2,1)}, u32[]{:S(2)}, u32[]{:S(2)}) collective-permute-start(bf16[4,128,128]{2,1,0:T(8,128)(2,1)S(1)} %fusion.2), channel_id=1, source_target_pairs={{0,16},{4,20},{8,24},{12,28},{16,0},{20,4},{24,8},{28,12},{1,17},{... | collective-permute-start | bytes 393224 | tf_op jit(solution)/shard_map/ppermute | solution.py:348
  29.3 5.1 %grad_rows.5 = (bf16[512,256]{1,0:T(8,128)(2,1)}, bf16[512,256]{1,0:T(8,128)(2,1)}) custom-call(s32[1]{0:T(128)} %bitcast.me_ref, bf16[512,2048]{1,0:T(8,128)(2,1)S(1)} %copy-done.6, bf16[2048,2048]{1,0:T(8,128)(2,1)S(1)} %copy-done, bf16[2048,2048]{1,0:T(8,128)(2,1)S(1)} %copy-done), custom_call_target="tpu_custom_call" | custom-call | tf_op jit(solution)/shard_map/grad_rows/pallas_call | solution.py:61
  36.1 5.1 %grad_rows.4 = (bf16[512,256]{1,0:T(8,128)(2,1)}, bf16[512,256]{1,0:T(8,128)(2,1)}) custom-call(s32[1]{0:T(128)} %bitcast.me_ref, bf16[512,2048]{1,0:T(8,128)(2,1)S(1)} %copy-done.7, bf16[2048,2048]{1,0:T(8,128)(2,1)S(1)} %copy-done, bf16[2048,2048]{1,0:T(8,128)(2,1)S(1)} %copy-done), custom_call_target="tpu_custom_call" | custom-call | tf_op jit(solution)/shard_map/grad_rows/pallas_call | solution.py:61
  45.7 1.6 %copy-done.5 = bf16[2048,512]{1,0:T(8,128)(2,1)S(1)} copy-done((bf16[2048,512]{1,0:T(8,128)(2,1)S(1)}, bf16[2048,512]{1,0:T(8,128)(2,1)}, u32[]{:S(2)}) %copy-start.5) | copy-done | bytes 2097176
  47.3 6.4 %forward.2 = (bf16[512,256]{1,0:T(8,128)(2,1)S(1)}, bf16[512,256]{1,0:T(8,128)(2,1)S(1)}, bf16[512,256]{1,0:T(8,128)(2,1)S(1)}, bf16[512,256]{1,0:T(8,128)(2,1)S...) custom-call(s32[1]{0:T(128)} %bitcast.me_ref, ...), custom_call_target="tpu_custom_call" | custom-call | tf_op jit(solution)/shard_map/forward/pallas_call | solution.py:146
  53.7 6.4 %forward.3 = (bf16[512,256]{1,0:T(8,128)(2,1)S(1)}, bf16[512,256]{1,0:T(8,128)(2,1)S(1)}, bf16[512,256]{1,0:T(8,128)(2,1)S(1)}, bf16[512,256]{1,0:T(8,128)(2,1)S...) custom-call(s32[1]{0:T(128)} %bitcast.me_ref, ...), custom_call_target="tpu_custom_call" | custom-call | tf_op jit(solution)/shard_map/forward/pallas_call | solution.py:146
  60.1 6.8 %backward.2 = (bf16[2048,512]{1,0:T(8,128)(2,1)}, bf16[2048,256]{1,0:T(8,128)(2,1)S(1)}, bf16[2048,256]{1,0:T(8,128)(2,1)S(1)}, f32[2,128,128]{2,1,0:T(8,128)S(1)}) custom-call(s32[1]{0:T(128)} %bitcast.me_ref, bf16[512,256]{1,0:T(8,128)(2,1)S(1)} %get-tuple-element.52.refs_0_, bf16[512,256]{1,0:T(8,128)(2,1)S(1)} %collective-permute-done.12.refs_1_, ...), custom_call_target="tpu_custom_call" | custom-call | tf_op jit(solution)/shard_map/backward/pallas_call | solution.py:221
  66.9 6.7 %backward.3 = (bf16[2048,512]{1,0:T(8,128)(2,1)}, bf16[2048,256]{1,0:T(8,128)(2,1)S(1)}, bf16[2048,256]{1,0:T(8,128)(2,1)S(1)}, f32[2,128,128]{2,1,0:T(8,128)S(1)}) custom-call(s32[1]{0:T(128)} %bitcast.me_ref, bf16[512,256]{1,0:T(8,128)(2,1)S(1)} %get-tuple-element.46.refs_0_, ...), custom_call_target="tpu_custom_call", output_to_operand_aliasing={{0}: (11, {})} | custom-call | tf_op jit(solution)/shard_map/backward/pallas_call | solution.py:221
  73.7 1.6 %collective-permute-start.15 = (bf16[2,128,128]{2,1,0:T(8,128)(2,1)S(1)}, bf16[2,128,128]{2,1,0:T(8,128)(2,1)S(1)}, u32[]{:S(2)}, u32[]{:S(2)}) collective-permute-start(bf16[2,128,128]{2,1,0:T(8,128)(2,1)S(1)} %convert_element_type.60), channel_id=1, source_target_pairs={{0,4},{4,0},{8,12},{12,8},{16,20},{20,16},{24,28},{28,24},{1,5},{5... | collective-permute-start | bytes 196616 | tf_op jit(solution)/shard_map/ppermute | solution.py:348
  78.5 2.4 %collective-permute-done.18 = bf16[2,128,128]{2,1,0:T(8,128)(2,1)S(1)} collective-permute-done((bf16[2,128,128]{2,1,0:T(8,128)(2,1)S(1)}, bf16[2,128,128]{2,1,0:T(8,128)(2,1)S(1)}, u32[]{:S(2)}, u32[]{:S(2)}) %collective-permute-start.18) | collective-permute-done | bytes 65568 | tf_op jit(solution)/shard_map/ppermute | solution.py:348
  82.8 3.1 %collective-permute-done.19 = bf16[2,128,128]{2,1,0:T(8,128)(2,1)S(1)} collective-permute-done((bf16[2,128,128]{2,1,0:T(8,128)(2,1)S(1)}, bf16[2,128,128]{2,1,0:T(8,128)(2,1)S(1)}, u32[]{:S(2)}, u32[]{:S(2)}) %collective-permute-start.19) | collective-permute-done | bytes 65568 | tf_op jit(solution)/shard_map/ppermute | solution.py:348
  87.0 2.5 %collective-permute-done.17 = bf16[2,128,128]{2,1,0:T(8,128)(2,1)S(1)} collective-permute-done((bf16[2,128,128]{2,1,0:T(8,128)(2,1)S(1)}, bf16[2,128,128]{2,1,0:T(8,128)(2,1)S(1)}, u32[]{:S(2)}, u32[]{:S(2)}) %collective-permute-start.17) | collective-permute-done | bytes 65568 | tf_op jit(solution)/shard_map/ppermute | solution.py:348
  89.5 1.8 %collective-permute-done.20 = bf16[2,128,128]{2,1,0:T(8,128)(2,1)S(1)} collective-permute-done((bf16[2,128,128]{2,1,0:T(8,128)(2,1)S(1)}, bf16[2,128,128]{2,1,0:T(8,128)(2,1)S(1)}, u32[]{:S(2)}, u32[]{:S(2)}) %collective-permute-start.20) | collective-permute-done | bytes 65568 | tf_op jit(solution)/shard_map/ppermute | solution.py:348
  92.5 6.4 %later_grads.2 = (bf16[2048,512]{1,0:T(8,128)(2,1)}, bf16[2048,512]{1,0:T(8,128)(2,1)}) custom-call(bf16[2048,512]{1,0:T(8,128)(2,1)S(1)} %copy-done.5, bf16[2048,512]{1,0:T(8,128)(2,1)S(1)} %copy-done.2, bf16[2048,512]{1,0:T(8,128)(2,1)S(1)} %copy-done.4, bf16[2048,256]{1,0:T(8,128)(2,1)S(1)} %get-tuple-element.64.g_ref, ...), custom_call_target="tpu_custom_call" | custom-call | tf_op jit(solution)/shard_map/later_grads/pallas_call | solution.py:277
  98.9 6.4 %later_grads.3 = (bf16[2048,512]{1,0:T(8,128)(2,1)}, bf16[2048,512]{1,0:T(8,128)(2,1)}) custom-call(bf16[2048,512]{1,0:T(8,128)(2,1)S(1)} %copy-done.5, bf16[2048,512]{1,0:T(8,128)(2,1)S(1)} %copy-done.2, bf16[2048,512]{1,0:T(8,128)(2,1)S(1)} %copy-done.4, ...), custom_call_target="tpu_custom_call", output_to_operand_aliasing={{0}: (7, {}), {1}: (8, {})} | custom-call | tf_op jit(solution)/shard_map/later_grads/pallas_call | solution.py:277
  105.4 4.9 %project.2.refs_4_ = f32[512,2048]{1,0:T(8,128)S(1)} custom-call(s32[1]{0:T(128)} %bitcast.me_ref, bf16[512,256]{1,0:T(8,128)(2,1)S(1)} %collective-permute-done.5.refs_0_, bf16[512,256]{1,0:T(8,128)(2,1)S(1)} %collective-permute-done.6.refs_1_, bf16[512,256]{1,0:T(8,128)(2,1)S(1)} %collective-permute-done.7.refs_2_, ...), custom_call_target="tpu_custom_call" | custom-call | tf_op jit(solution)/shard_map/project/pallas_call | solution.py:314
  110.3 3.3 %project.3 = bf16[512,2048]{1,0:T(8,128)(2,1)} custom-call(s32[1]{0:T(128)} %bitcast.me_ref, bf16[512,256]{1,0:T(8,128)(2,1)S(1)} %collective-permute-done.3.refs_0_, bf16[512,256]{1,0:T(8,128)(2,1)S(1)} %collective-permute-done.4.refs_1_, bf16[2048,2048]{1,0:T(8,128)(2,1)S(1)} %bitcast.2, bf16[2048,2048]{1,0:T(8,128)(2,1)S(1)} %bitcast.2, ...), custom_call_target="tpu_custom_call" | custom-call | tf_op jit(solution)/shard_map/project/pallas_call | solution.py:314
  (67 shorter events, 15.4 us)
Async XLA Ops:
  3.8 9.9 %copy-start.6 = (bf16[512,2048]{1,0:T(8,128)(2,1)S(1)}, bf16[512,2048]{1,0:T(8,128)(2,1)}, u32[]{:S(2)}) copy-start(bf16[512,2048]{1,0:T(8,128)(2,1)} %d_ref.5) | copy-start | bytes 6291460
  5.3 6.5 %collective-permute-start = (bf16[4,128,128]{2,1,0:T(8,128)(2,1)S(1)}, bf16[4,128,128]{2,1,0:T(8,128)(2,1)S(1)}, u32[]{:S(2)}, u32[]{:S(2)}) collective-permute-start(bf16[4,128,128]{2,1,0:T(8,128)(2,1)S(1)} %convert_element_type.54), channel_id=1, source_target_pairs={{0,4},{4,0},{8,12},{12,8},{16,20},{20,16},{24,28},{28,24},{1,5},{5... | collective-permute-start | bytes 393224 | tf_op jit(solution)/shard_map/ppermute | solution.py:348
  11.9 14.5 %collective-permute-start.1 = (bf16[4,128,128]{2,1,0:T(8,128)(2,1)S(1)}, bf16[4,128,128]{2,1,0:T(8,128)(2,1)S(1)}, u32[]{:S(2)}, u32[]{:S(2)}) collective-permute-start(bf16[4,128,128]{2,1,0:T(8,128)(2,1)S(1)} %fusion.3), channel_id=1, source_target_pairs={{0,8},{4,12},{8,0},{12,4},{16,24},{20,28},{24,16},{28,20},{1,9},{5... | collective-permute-start | bytes 393224 | tf_op jit(solution)/shard_map/ppermute | solution.py:348
  26.3 14.9 %collective-permute-start.12 = (bf16[512,256]{1,0:T(8,128)(2,1)S(1)}, bf16[512,256]{1,0:T(8,128)(2,1)S(1)}, u32[]{:S(2)}, u32[]{:S(2)}) collective-permute-start(bf16[512,256]{1,0:T(8,128)(2,1)S(1)} %get-tuple-element.53), channel_id=1, source_target_pairs={{0,1},{1,0},{2,3},{3,2},{4,5},{5,4},{6,7},{7,6},{8,9},{9,8},{10,11... | collective-permute-start | bytes 786440 | tf_op jit(solution)/shard_map/ppermute | solution.py:342
  26.4 8.1 %copy-start.8 = (bf16[4,128,128]{2,1,0:T(8,128)(2,1)}, bf16[4,128,128]{2,1,0:T(8,128)(2,1)S(1)}, u32[]{:S(2)}) copy-start(bf16[4,128,128]{2,1,0:T(8,128)(2,1)S(1)} %collective-permute-done.1) | copy-start | bytes 393220
  26.4 16.3 %collective-permute-start.2 = (bf16[4,128,128]{2,1,0:T(8,128)(2,1)S(1)}, bf16[4,128,128]{2,1,0:T(8,128)(2,1)}, u32[]{:S(2)}, u32[]{:S(2)}) collective-permute-start(bf16[4,128,128]{2,1,0:T(8,128)(2,1)S(1)} %fusion.2), channel_id=1, source_target_pairs={{0,16},{4,20},{8,24},{12,28},{16,0},{20,4},{24,8},{28,12},{1,17},{... | collective-permute-start | bytes 393224 | tf_op jit(solution)/shard_map/ppermute | solution.py:348
  29.1 37.8 %collective-permute-start.9 = (bf16[512,256]{1,0:T(8,128)(2,1)}, bf16[512,256]{1,0:T(8,128)(2,1)S(1)}, u32[]{:S(2)}, u32[]{:S(2)}) collective-permute-start(bf16[512,256]{1,0:T(8,128)(2,1)} %get-tuple-element.47), channel_id=1, source_target_pairs={{0,1},{1,0},{2,3},{3,2},{4,5},{5,4},{6,7},{7,6},{8,9},{9,8},{10,11... | collective-permute-start | bytes 786440 | tf_op jit(solution)/shard_map/ppermute | solution.py:342
  34.4 25.6 %collective-permute-start.13 = (bf16[512,256]{1,0:T(8,128)(2,1)}, bf16[512,256]{1,0:T(8,128)(2,1)}, u32[]{:S(2)}, u32[]{:S(2)}) collective-permute-start(bf16[512,256]{1,0:T(8,128)(2,1)} %get-tuple-element.54), channel_id=1, source_target_pairs={{0,2},{1,3},{2,0},{3,1},{4,6},{5,7},{6,4},{7,5},{8,10},{9,11},{10,... | collective-permute-start | bytes 786440 | tf_op jit(solution)/shard_map/ppermute | solution.py:342
  35.9 24.2 %collective-permute-start.14 = (bf16[512,256]{1,0:T(8,128)(2,1)}, bf16[512,256]{1,0:T(8,128)(2,1)}, u32[]{:S(2)}, u32[]{:S(2)}) collective-permute-start(bf16[512,256]{1,0:T(8,128)(2,1)} %get-tuple-element.55), channel_id=1, source_target_pairs={{0,3},{1,2},{2,1},{3,0},{4,7},{5,6},{6,5},{7,4},{8,11},{9,10},{10,... | collective-permute-start | bytes 786440 | tf_op jit(solution)/shard_map/ppermute | solution.py:342
  41.2 25.7 %collective-permute-start.10 = (bf16[512,256]{1,0:T(8,128)(2,1)}, bf16[512,256]{1,0:T(8,128)(2,1)S(1)}, u32[]{:S(2)}, u32[]{:S(2)}) collective-permute-start(bf16[512,256]{1,0:T(8,128)(2,1)} %get-tuple-element.48), channel_id=1, source_target_pairs={{0,2},{1,3},{2,0},{3,1},{4,6},{5,7},{6,4},{7,5},{8,10},{9,11},{10,... | collective-permute-start | bytes 786440 | tf_op jit(solution)/shard_map/ppermute | solution.py:342
  42.7 24.2 %collective-permute-start.11 = (bf16[512,256]{1,0:T(8,128)(2,1)}, bf16[512,256]{1,0:T(8,128)(2,1)}, u32[]{:S(2)}, u32[]{:S(2)}) collective-permute-start(bf16[512,256]{1,0:T(8,128)(2,1)} %get-tuple-element.49), channel_id=1, source_target_pairs={{0,3},{1,2},{2,1},{3,0},{4,7},{5,6},{6,5},{7,4},{8,11},{9,10},{10,... | collective-permute-start | bytes 786440 | tf_op jit(solution)/shard_map/ppermute | solution.py:342
  73.7 4.3 %collective-permute-start.15 = (bf16[2,128,128]{2,1,0:T(8,128)(2,1)S(1)}, bf16[2,128,128]{2,1,0:T(8,128)(2,1)S(1)}, u32[]{:S(2)}, u32[]{:S(2)}) collective-permute-start(bf16[2,128,128]{2,1,0:T(8,128)(2,1)S(1)} %convert_element_type.60), channel_id=1, source_target_pairs={{0,4},{4,0},{8,12},{12,8},{16,20},{20,16},{24,28},{28,24},{1,5},{5... | collective-permute-start | bytes 196616 | tf_op jit(solution)/shard_map/ppermute | solution.py:348
  75.2 16.6 %collective-permute-start.5 = (bf16[512,256]{1,0:T(8,128)(2,1)S(1)}, bf16[512,256]{1,0:T(8,128)(2,1)S(1)}, u32[]{:S(2)}, u32[]{:S(2)}) collective-permute-start(bf16[512,256]{1,0:T(8,128)(2,1)S(1)} %get-tuple-element.40), channel_id=1, source_target_pairs={{0,3},{1,2},{2,1},{3,0},{4,7},{5,6},{6,5},{7,4},{8,11},{9,10},{10,... | collective-permute-start | bytes 786440 | tf_op jit(solution)/shard_map/ppermute | solution.py:342
  76.4 4.6 %collective-permute-start.18 = (bf16[2,128,128]{2,1,0:T(8,128)(2,1)S(1)}, bf16[2,128,128]{2,1,0:T(8,128)(2,1)S(1)}, u32[]{:S(2)}, u32[]{:S(2)}) collective-permute-start(bf16[2,128,128]{2,1,0:T(8,128)(2,1)S(1)} %convert_element_type.66), channel_id=1, source_target_pairs={{0,4},{4,0},{8,12},{12,8},{16,20},{20,16},{24,28},{28,24},{1,5},{5... | collective-permute-start | bytes 196616 | tf_op jit(solution)/shard_map/ppermute | solution.py:348
  78.0 4.3 %collective-permute-start.16 = (bf16[2,128,128]{2,1,0:T(8,128)(2,1)S(1)}, bf16[2,128,128]{2,1,0:T(8,128)(2,1)S(1)}, u32[]{:S(2)}, u32[]{:S(2)}) collective-permute-start(bf16[2,128,128]{2,1,0:T(8,128)(2,1)S(1)} %fusion.10), channel_id=1, source_target_pairs={{0,8},{4,12},{8,0},{12,4},{16,24},{20,28},{24,16},{28,20},{1,9},{5... | collective-permute-start | bytes 196616 | tf_op jit(solution)/shard_map/ppermute | solution.py:348
  80.9 5.0 %collective-permute-start.19 = (bf16[2,128,128]{2,1,0:T(8,128)(2,1)S(1)}, bf16[2,128,128]{2,1,0:T(8,128)(2,1)S(1)}, u32[]{:S(2)}, u32[]{:S(2)}) collective-permute-start(bf16[2,128,128]{2,1,0:T(8,128)(2,1)S(1)} %fusion.11), channel_id=1, source_target_pairs={{0,8},{4,12},{8,0},{12,4},{16,24},{20,28},{24,16},{28,20},{1,9},{5... | collective-permute-start | bytes 196616 | tf_op jit(solution)/shard_map/ppermute | solution.py:348
  82.4 7.1 %collective-permute-start.17 = (bf16[2,128,128]{2,1,0:T(8,128)(2,1)S(1)}, bf16[2,128,128]{2,1,0:T(8,128)(2,1)S(1)}, u32[]{:S(2)}, u32[]{:S(2)}) collective-permute-start(bf16[2,128,128]{2,1,0:T(8,128)(2,1)S(1)} %fusion.6), channel_id=1, source_target_pairs={{0,16},{4,20},{8,24},{12,28},{16,0},{20,4},{24,8},{28,12},{1,17},{... | collective-permute-start | bytes 196616 | tf_op jit(solution)/shard_map/ppermute | solution.py:348
  85.9 5.4 %collective-permute-start.20 = (bf16[2,128,128]{2,1,0:T(8,128)(2,1)S(1)}, bf16[2,128,128]{2,1,0:T(8,128)(2,1)S(1)}, u32[]{:S(2)}, u32[]{:S(2)}) collective-permute-start(bf16[2,128,128]{2,1,0:T(8,128)(2,1)S(1)} %fusion.9), channel_id=1, source_target_pairs={{0,16},{4,20},{8,24},{12,28},{16,0},{20,4},{24,8},{28,12},{1,17},{... | collective-permute-start | bytes 196616 | tf_op jit(solution)/shard_map/ppermute | solution.py:348
  86.0 19.3 %collective-permute-start.6 = (bf16[512,256]{1,0:T(8,128)(2,1)S(1)}, bf16[512,256]{1,0:T(8,128)(2,1)S(1)}, u32[]{:S(2)}, u32[]{:S(2)}) collective-permute-start(bf16[512,256]{1,0:T(8,128)(2,1)S(1)} %get-tuple-element.41), channel_id=1, source_target_pairs={{0,2},{1,3},{2,0},{3,1},{4,6},{5,7},{6,4},{7,5},{8,10},{9,11},{10,... | collective-permute-start | bytes 786440 | tf_op jit(solution)/shard_map/ppermute | solution.py:342
  87.0 18.4 %collective-permute-start.7 = (bf16[512,256]{1,0:T(8,128)(2,1)S(1)}, bf16[512,256]{1,0:T(8,128)(2,1)S(1)}, u32[]{:S(2)}, u32[]{:S(2)}) collective-permute-start(bf16[512,256]{1,0:T(8,128)(2,1)S(1)} %get-tuple-element.42), channel_id=1, source_target_pairs={{0,1},{1,0},{2,3},{3,2},{4,5},{5,4},{6,7},{7,6},{8,9},{9,8},{10,11... | collective-permute-start | bytes 786440 | tf_op jit(solution)/shard_map/ppermute | solution.py:342
  89.5 15.9 %collective-permute-start.8 = (bf16[512,256]{1,0:T(8,128)(2,1)S(1)}, bf16[512,256]{1,0:T(8,128)(2,1)S(1)}, u32[]{:S(2)}, u32[]{:S(2)}) collective-permute-start(bf16[512,256]{1,0:T(8,128)(2,1)S(1)} %get-tuple-element.44), channel_id=1, source_target_pairs={{0,1},{1,0},{2,3},{3,2},{4,5},{5,4},{6,7},{7,6},{8,9},{9,8},{10,11... | collective-permute-start | bytes 786440 | tf_op jit(solution)/shard_map/ppermute | solution.py:342
  91.3 19.0 %collective-permute-start.3 = (bf16[512,256]{1,0:T(8,128)(2,1)S(1)}, bf16[512,256]{1,0:T(8,128)(2,1)S(1)}, u32[]{:S(2)}, u32[]{:S(2)}) collective-permute-start(bf16[512,256]{1,0:T(8,128)(2,1)S(1)} %get-tuple-element.38), channel_id=1, source_target_pairs={{0,3},{1,2},{2,1},{3,0},{4,7},{5,6},{6,5},{7,4},{8,11},{9,10},{10,... | collective-permute-start | bytes 786440 | tf_op jit(solution)/shard_map/ppermute | solution.py:342
  91.8 18.5 %collective-permute-start.4 = (bf16[512,256]{1,0:T(8,128)(2,1)S(1)}, bf16[512,256]{1,0:T(8,128)(2,1)S(1)}, u32[]{:S(2)}, u32[]{:S(2)}) collective-permute-start(bf16[512,256]{1,0:T(8,128)(2,1)S(1)} %get-tuple-element.39), channel_id=1, source_target_pairs={{0,2},{1,3},{2,0},{3,1},{4,6},{5,7},{6,4},{7,5},{8,10},{9,11},{10,... | collective-permute-start | bytes 786440 | tf_op jit(solution)/shard_map/ppermute | solution.py:342
  92.5 12.8 %slice-start = ((s8[8388608]{0:T(1024)(128)(4,1)}), s8[4194304]{0:T(1024)(128)(4,1)S(1)}, s32[]{:S(2)}) async-start(s8[8388608]{0:T(1024)(128)(4,1)} %bitcast.1), calls=%async_computation | async-start | bytes 8388608
  (9 other events, 38.4 us)

commit v2 on v0

v2 whole, which is shorter than its diff:
```python
import functools

import jax
import jax.numpy as jnp
from jax import lax
from jax.experimental import pallas as pl
from jax.experimental.pallas import tpu as pltpu
from jax.sharding import PartitionSpec as P

HDIM = 128
BLOCK = 128
epsilon = 1e-06
f32 = jnp.float32
bf16 = jnp.bfloat16
VMEM_LIMIT = 16 << 20


def mm(a, b, ca, cb):
    return lax.dot_general(a, b, (((ca,), (cb,)), ((), ())), preferred_element_type=f32)


def both(a0, a1, b0, b1):
    return mm(jnp.concatenate([a0, a1], 1), jnp.concatenate([b0, b1], 0), 1, 0)


def causal_mask():
    row = lax.broadcasted_iota(jnp.int32, (BLOCK, BLOCK), 0)
    col = lax.broadcasted_iota(jnp.int32, (BLOCK, BLOCK), 1)
    return col <= row


def masked(mask, scores):
    return jnp.where(mask, scores, 0.0).astype(bf16)


def pairs(tile, heads, order=list):
    return [
        (h, (slice(b * BLOCK, (b + 1) * BLOCK), slice(h * HDIM, (h + 1) * HDIM)))
        for b in order(range(tile // BLOCK))
        for h in range(heads)
    ]


def backwards(blocks):
    return list(reversed(blocks))


class Copies:
    def __init__(self, sems):
        self.sems, self.used = sems, 0

    def start(self, src, dst):
        copy = pltpu.make_async_copy(src, dst, self.sems.at[self.used])
        self.used += 1
        copy.start()
        return copy


def span(index, size):
    return pl.ds(pl.multiple_of(index * size, size), size)


def run_kernel(body, args, outs, scratch=(), ncopies=0, name=None, into=None, sent=0):
    here, anywhere = pl.BlockSpec(memory_space=pltpu.VMEM), pl.BlockSpec(memory_space=pl.ANY)
    into = list(into or [])
    return pl.pallas_call(
        body,
        in_specs=[here] * len(args) + [anywhere] * len(into),
        out_specs=[anywhere] * sent + [here] * (len(outs) - sent),
        out_shape=[jax.ShapeDtypeStruct(*out) for out in outs],
        scratch_shapes=[pltpu.VMEM(*s) for s in scratch]
        + ([pltpu.SemaphoreType.DMA((ncopies,))] if ncopies else []),
        input_output_aliases={len(args) + i: i for i in range(len(into))},
        compiler_params=pltpu.CompilerParams(vmem_limit_bytes=VMEM_LIMIT),
        name=name,
    )(*args, *into)


def grad_rows(d_out, w_out, pieces, chunks, cols):
    rows = d_out.shape[0]

    def body(d, w, *outs):
        me = lax.axis_index("head")
        for (dist, c), out in zip(pieces, outs):
            piece = span((me ^ dist) * chunks + c, cols)
            out[...] = mm(d[...], w[piece], 1, 1).astype(bf16)

    return run_kernel(
        body, (d_out, w_out), [((rows, cols), bf16)] * len(pieces), name="grad_rows"
    )


def total_state(key, value):
    heads = key.shape[1] // HDIM
    shape = (heads, HDIM, HDIM)

    def body(k, v, o, ob):
        for h in range(heads):
            cols = slice(h * HDIM, (h + 1) * HDIM)
            total = mm(k[:, cols], v[:, cols], 0, 0)
            o[h] = total
            ob[h] = total.astype(bf16)

    return run_kernel(body, (key, value), [(shape, f32), (shape, bf16)], name="total_state")


def forward(query, key, value, gain, before, chunks, nhead):
    tokens, width = query.shape
    tile, cols = tokens // nhead, width // chunks
    heads = width // HDIM
    n = nhead * chunks

    def body(q, k, v, gain, before, *refs):
        normed, (att, s, st, rows) = refs[:n], refs[n:]
        me = lax.axis_index("head")
        mask = causal_mask()
        run = [before[h] for h in range(heads)]
        for t in range(nhead):
            work = [
                (h, (slice(t * tile + r.start, t * tile + r.stop), c))
                for h, (r, c) in pairs(tile, heads)
            ]
            scores = [masked(mask, mm(q[at], k[at], 1, 1)) for _, at in work]
            for (_, at), x in zip(work, scores):
                s[at] = x
            products = [mm(k[at], v[at], 0, 0) for _, at in work]
            states = []
            for (h, at), product in zip(work, products):
                states.append(run[h].astype(bf16))
                st[at] = states[-1]
                run[h] = run[h] + product
            attended = [both(x, q[at], v[at], y) for (_, at), x, y in zip(work, scores, states)]
            for (_, at), x in zip(work, attended):
                att[at] = x
                inverse = lax.rsqrt(jnp.mean(x * x, axis=-1, keepdims=True) + epsilon)
                rows[at] = (x * inverse * gain[:, at[1]].astype(f32)).astype(bf16)
        for dist in range(nhead):
            part = span(me ^ dist, tile)
            for c in range(chunks):
                normed[dist * chunks + c][...] = rows[part, c * cols : (c + 1) * cols]

    whole = (tokens, width)
    outs = run_kernel(
        body,
        (query, key, value, gain, before),
        [((tile, cols), bf16)] * n + [(whole, f32), (whole, bf16), (whole, bf16)],
        [(whole, bf16)],
        name="forward",
    )
    normed = {(d, c): outs[d * chunks + c] for d in range(nhead) for c in range(chunks)}
    return normed, outs[n:]


def backward(pieces, query, key, value, gain, attended, states, into, chunk, cols):
    tokens, width = query.shape
    nhead = len(pieces)
    tile = tokens // nhead
    heads = cols // HDIM
    shape = (heads, HDIM, HDIM)
    first = chunk * cols

    def body(*refs):
        p, refs = refs[:nhead], refs[nhead:]
        q, k, v, gain, att, st = refs[:6]
        gq_hbm, g, gs, tot, totb, gq, sems = refs[6 + (into is not None) :]
        me = lax.axis_index("head")
        copies = Copies(sems)
        mask = causal_mask()
        stores, sums = [], [0.0] * heads
        for t in range(nhead):
            base = (me ^ t) * tile
            work = [
                (
                    h,
                    (r, c),
                    (span(base // BLOCK + r.start // BLOCK, BLOCK), c),
                    (
                        span(base // BLOCK + r.start // BLOCK, BLOCK),
                        slice(first + c.start, first + c.stop),
                    ),
                )
                for h, (r, c) in pairs(tile, heads)
            ]
            grads = []
            for _, here, near, wide in work:
                x = att[wide]
                inverse = lax.rsqrt(jnp.mean(x * x, axis=-1, keepdims=True) + epsilon)
                unit = x * inverse
                grad_unit = p[t][here].astype(f32) * gain[:, wide[1]].astype(f32)
                along = jnp.mean(grad_unit * unit, axis=-1, keepdims=True)
                grads.append((inverse * (grad_unit - unit * along)).astype(bf16))
                g[near] = grads[-1]
            products = [mm(q[wide], x, 0, 0) for (*_, wide), x in zip(work, grads)]
            for (h, *_), product in zip(work, products):
                sums[h] = sums[h] + product
            grad_scores = [
                masked(mask, mm(x, v[wide], 1, 1)) for (*_, wide), x in zip(work, grads)
            ]
            for (_, _, near, _), x in zip(work, grad_scores):
                gs[near] = x
            for (_, _, near, wide), x, y in zip(work, grad_scores, grads):
                gq[near] = both(x, y, k[wide], st[wide].T).astype(bf16)
            part = span(me ^ t, tile)
            stores.append(copies.start(gq.at[part], gq_hbm.at[part, first : first + cols]))
        for h in range(heads):
            tot[h] = sums[h]
            totb[h] = sums[h].astype(bf16)
        for copy in stores:
            copy.wait()

    local = (tokens, cols)
    return run_kernel(
        body,
        (*pieces, query, key, value, gain, attended, states),
        [((tokens, width), bf16), (local, bf16), (local, bf16), (shape, f32), (shape, bf16)],
        [(local, bf16)],
        nhead,
        "backward",
        into,
        1,
    )


def later_grads(query, key, value, scores, g, grad_scores, after, into, chunk, cols, steps):
    tokens, width = query.shape
    tile, heads = tokens // steps, cols // HDIM
    first = chunk * cols

    def body(*refs):
        q, k, v, s, g, gs, after = refs[:7]
        gk_hbm, gv_hbm, gk, gv, sems = refs[7 + (2 if into else 0) :]
        copies = Copies(sems)
        stores, run = [], [after[h] for h in range(heads)]
        for t in reversed(range(steps)):
            part = pl.ds(t * tile, tile)
            work = []
            for h, (r, c) in pairs(tile, heads, backwards):
                rows = slice(t * tile + r.start, t * tile + r.stop)
                work.append((h, (rows, c), (rows, slice(first + c.start, first + c.stop))))
            products = [mm(q[wide], g[near], 0, 0) for _, near, wide in work]
            laters = []
            for (h, *_), product in zip(work, products):
                laters.append(run[h].astype(bf16))
                run[h] = run[h] + product
            for (_, near, wide), x in zip(work, laters):
                gk[near] = both(gs[near].T, v[wide], q[wide], x.T).astype(bf16)
            mine = slice(first, first + cols)
            stores.append(copies.start(gk.at[part], gk_hbm.at[part, mine]))
            for (_, near, wide), x in zip(work, laters):
                gv[near] = both(s[wide].T, k[wide], g[near], x).astype(bf16)
            stores.append(copies.start(gv.at[part], gv_hbm.at[part, mine]))
        for copy in stores:
            copy.wait()

    local = (tokens, cols)
    return run_kernel(
        body,
        (query, key, value, scores, g, grad_scores, after),
        [((tokens, width), bf16)] * 2,
        [(local, bf16)] * 2,
        2 * steps,
        "later_grads",
        into,
        2,
    )


def project(pieces, xs, w_out, acc, chunks, kind):
    rows, cols = xs[0].shape
    model = w_out.shape[1]
    tile = min(512, model)
    steps, n = model // tile, len(pieces)

    def body(*refs):
        x, w, refs = refs[:n], refs[n], refs[n + 1 :]
        me = lax.axis_index("head")
        deep = jnp.concatenate([ref[...] for ref in x], axis=1)
        rows_of = [span((me ^ dist) * chunks + c, cols) for dist, c in pieces]
        stores = []
        for j in range(steps):
            at = slice(j * tile, (j + 1) * tile)
            total = mm(deep, jnp.concatenate([w[r, at] for r in rows_of], axis=0), 1, 0)
            if acc is not None:
                total = total + refs[0][:, at]
            if kind == f32:
                refs[-1][:, at] = total
            else:
                o_hbm, o, sems = refs[-3:]
                o[:, at] = total.astype(kind)
                stores.append(pltpu.make_async_copy(o.at[:, at], o_hbm.at[:, at], sems.at[j]))
                stores[-1].start()
        for copy in stores:
            copy.wait()

    final = kind == bf16
    return run_kernel(
        body,
        (*xs, w_out) + (() if acc is None else (acc,)),
        [((rows, model), kind)],
        [((rows, model), kind)] if final else [],
        steps if final else 0,
        "project",
        sent=int(final),
    )[0]


def on_device(nctx, nhead, query, key, value, gain, w_out, d_out):
    tokens, width = query.shape
    local_heads = width // HDIM
    chunks = 2 if local_heads % 2 == 0 else 1
    cols = width // chunks
    place = lax.axis_index("ctx")
    gain = gain.reshape(1, width)

    def swap(array, dist):
        if dist == 0:
            return array
        return lax.ppermute(array, "head", [(i, i ^ dist) for i in range(nhead)])

    def others(total, rounded, later):
        outside = jnp.zeros_like(total)
        dist = 1
        while dist < nctx:
            got = lax.ppermute(rounded, "ctx", [(i, i ^ dist) for i in range(nctx)]).astype(f32)
            wanted = ((place & dist) == 0) == later
            outside = outside + jnp.where(wanted, got, 0.0)
            total = total + got
            rounded = total.astype(bf16)
            dist *= 2
        return outside

    far = [d for d in range(nhead - 1, 0, -1) if d > 1]
    near = [d for d in range(nhead) if d <= 1]
    sent = {}
    for c in range(chunks):
        pieces = [(d, c) for d in far]
        if far:
            sent.update(zip(pieces, grad_rows(d_out, w_out, pieces, chunks, cols)))
    pieces = [(d, c) for d in near for c in range(chunks)]
    sent.update(zip(pieces, grad_rows(d_out, w_out, pieces, chunks, cols)))
    got = {(d, c): swap(sent[d, c], d) for c in range(chunks) for d in reversed(range(nhead))}

    before = others(*total_state(key, value), False)

    normed, (attended, scores, states) = forward(query, key, value, gain, before, chunks, nhead)
    normed = {(d, c): swap(normed[d, c], d) for c in range(chunks) for d in reversed(range(nhead))}

    grad_query, carried = None, []
    for c in range(chunks):
        grad_query, g, grad_scores, total, rounded = backward(
            [got[d, c] for d in range(nhead)],
            query,
            key,
            value,
            gain,
            attended,
            states,
            grad_query,
            c,
            cols,
        )
        grad_query = [grad_query]
        carried.append((g, grad_scores, others(total, rounded, True)))
    grads = None
    for c in range(chunks):
        grads = later_grads(query, key, value, scores, *carried[c], grads, c, cols, nhead)

    last = [(d, chunks - 1) for d in far]
    first = [p for p in normed if p not in last]
    out = project(first, [normed[p] for p in first], w_out, None, chunks, f32 if last else bf16)
    if last:
        out = project(last, [normed[p] for p in last], w_out, out, chunks, bf16)
    return out, grad_query[0], grads[0], grads[1]


def solution(mesh):
    nctx, nhead = mesh.shape["ctx"], mesh.shape["head"]
    return jax.shard_map(
        functools.partial(on_device, nctx, nhead),
        mesh=mesh,
        in_specs=(
            P("ctx", "head"),
            P("ctx", "head"),
            P("ctx", "head"),
            P("head"),
            P(),
            P(("ctx", "head"), None),
        ),
        out_specs=(P(("ctx", "head"), None), P("ctx", "head"), P("ctx", "head"), P("ctx", "head")),
        check_vma=False,
    )
```

time: 254 us -> 81.1 us (0.32); the launches traced: 249 us -> 80.8 us
  local copies, waits for them, and re-layouts: 91.3 us -> 9.78 us
  matrix products: 57.3 us -> 0 us
  other arithmetic: 58.5 us -> 1.28 us
  Pallas kernels: 0 us -> 31.6 us
  between operations: 14.6 us -> 1.04 us
  starting transfers between devices: 9.71 us -> 19.7 us
    dot_general x14 -> x0, matrix products: 57.3 us -> none  [the longest x1 9.35 us: on_device(): jnp.dot(row_normed, w_out, preferred_element_type=jnp.float32)]
    reduce_sum x3 -> x0, other arithmetic: 33.3 us -> none  [the longest x1 30.3 us: on_device(): jnp.mean(grad_unit * unit, axis=-1, keepdims=True)]
    pallas_call x0 -> x11, Pallas kernels: none -> 31.6 us  [run_kernel(): pl.pallas_call(body, in_specs=[here] * len(args) + [anywhere] * len(into)...]
    ppermute x0 -> x21, starting transfers between devices: none -> 19.7 us  [the longest x9 12.2 us: others(): lax.ppermute(rounded, 'ctx', [(i, i ^ dist) for i in range(nctx)])]
    all_to_all x2 -> x0, waiting for transfers between devices: 17.3 us -> none  [the longest x1 10.3 us: on_device(): lax.all_to_all(normed, 'head', split_axis=0, concat_axis=1, tiled=True)]
    ppermute x0 -> x21, waiting for transfers between devices: none -> 17.3 us  [the longest x9 14.2 us: others(): lax.ppermute(rounded, 'ctx', [(i, i ^ dist) for i in range(nctx)])]
    reshape x4 -> x1, local copies, waits for them, and re-layouts: 16.1 us -> 0.01 us  [on_device(): gain = gain.reshape(1, width)]
    convert_element_type x3 -> x6, other arithmetic: 15.3 us -> 0.17 us  [others(): rounded = total.astype(bf16)]
  transfers between devices with their start and end apart: 4 -> 21, of which waited for: 2 -> 8; matrix products, arithmetic and copies ran while one was open for 36% -> 2% of each run, Pallas kernels for 0% -> 31%
where the time goes in v2:
time: 81.1 us; the launch traced here: 80.8 us
  Pallas kernels  31.6 us (39%)
  starting transfers between devices  19.7 us (24%)
  waiting for transfers between devices  17.3 us (21%)
  local copies, waits for them, and re-layouts  9.78 us (12%)
  other arithmetic  1.28 us (2%)
  between operations  1.04 us (1%)
    pallas_call x11, Pallas kernels, run_kernel(): pl.pallas_call(body, in_specs=[here] * len(args) + [anywhere] * len(into)...  31.6 us
    ppermute x9, waiting for transfers between devices, others(): lax.ppermute(rounded, 'ctx', [(i, i ^ dist) for i in range(nctx)])  14.2 us
    ppermute x9, starting transfers between devices, others(): lax.ppermute(rounded, 'ctx', [(i, i ^ dist) for i in range(nctx)])  12.2 us
    unnamed x26, local copies, waits for them, and re-layouts  9.77 us
    ppermute x12, starting transfers between devices, swap(): return lax.ppermute(array, 'head', [(i, i ^ dist) for i in range(nhead)])  7.53 us
    ppermute x12, waiting for transfers between devices, swap(): return lax.ppermute(array, 'head', [(i, i ^ dist) for i in range(nhead)])  3.05 us
  transfers between devices with their start and end apart: 21, of which 8 were waited for; matrix products, arithmetic and copies ran while one was open for 2% of the time, Pallas kernels for 31%

profile of v2, /device:TPU:0, one launch (start us, length us, event | category | flops | bytes accessed | tf_op | source)
XLA Modules:
  0.0 80.8 jit_solution(12580733373024511823)
XLA Ops:
  0.6 1.6 %copy-done.1 = bf16[2048,512]{1,0:T(8,128)(2,1)S(1)} copy-done((bf16[2048,512]{1,0:T(8,128)(2,1)S(1)}, bf16[2048,512]{1,0:T(8,128)(2,1)}, u32[]{:S(2)}) %copy-start.1) | copy-done | bytes 2097176
  2.2 1.6 %copy-done.3 = bf16[2048,512]{1,0:T(8,128)(2,1)S(1)} copy-done((bf16[2048,512]{1,0:T(8,128)(2,1)S(1)}, bf16[2048,512]{1,0:T(8,128)(2,1)}, u32[]{:S(2)}) %copy-start.3) | copy-done | bytes 2097176
  4.6 3.0 %collective-permute-start = (bf16[4,128,128]{2,1,0:T(8,128)(2,1)S(1)}, bf16[4,128,128]{2,1,0:T(8,128)(2,1)S(1)}, u32[]{:S(2)}, u32[]{:S(2)}) collective-permute-start(bf16[4,128,128]{2,1,0:T(8,128)(2,1)S(1)} %get-tuple-element.39), channel_id=1, source_target_pairs={{0,4},{4,0},{8,12},{12,8},{16,20},{20,16},{24,28},{28,24},{1,5},{5... | collective-permute-start | bytes 393224 | tf_op jit(solution)/shard_map/ppermute | solution.py:324
  7.6 3.5 %collective-permute-done = bf16[4,128,128]{2,1,0:T(8,128)(2,1)S(1)} collective-permute-done((bf16[4,128,128]{2,1,0:T(8,128)(2,1)S(1)}, bf16[4,128,128]{2,1,0:T(8,128)(2,1)S(1)}, u32[]{:S(2)}, u32[]{:S(2)}) %collective-permute-start) | collective-permute-done | bytes 131104 | tf_op jit(solution)/shard_map/ppermute | solution.py:324
  11.2 1.9 %collective-permute-start.1 = (bf16[4,128,128]{2,1,0:T(8,128)(2,1)S(1)}, bf16[4,128,128]{2,1,0:T(8,128)(2,1)S(1)}, u32[]{:S(2)}, u32[]{:S(2)}) collective-permute-start(bf16[4,128,128]{2,1,0:T(8,128)(2,1)S(1)} %fusion.3), channel_id=1, source_target_pairs={{0,8},{4,12},{8,0},{12,4},{16,24},{20,28},{24,16},{28,20},{1,9},{5... | collective-permute-start | bytes 393224 | tf_op jit(solution)/shard_map/ppermute | solution.py:324
  13.0 3.4 %copy-done = bf16[2048,2048]{1,0:T(8,128)(2,1)S(1)} copy-done((bf16[2048,2048]{1,0:T(8,128)(2,1)S(1)}, bf16[2048,2048]{1,0:T(8,128)(2,1)}, u32[]{:S(2)}) %copy-start) | copy-done | bytes 8388632
  16.4 2.0 %grad_rows.5 = (bf16[512,256]{1,0:T(8,128)(2,1)}, bf16[512,256]{1,0:T(8,128)(2,1)S(1)}) custom-call(bf16[512,2048]{1,0:T(8,128)(2,1)S(1)} %copy-done.6, bf16[2048,2048]{1,0:T(8,128)(2,1)S(1)} %copy-done), custom_call_target="tpu_custom_call" | custom-call | tf_op jit(solution)/shard_map/grad_rows/pallas_call | solution.py:66
  19.9 2.7 %collective-permute-start.2 = (bf16[4,128,128]{2,1,0:T(8,128)(2,1)S(1)}, bf16[4,128,128]{2,1,0:T(8,128)(2,1)}, u32[]{:S(2)}, u32[]{:S(2)}) collective-permute-start(bf16[4,128,128]{2,1,0:T(8,128)(2,1)S(1)} %fusion.2), channel_id=1, source_target_pairs={{0,16},{4,20},{8,24},{12,28},{16,0},{20,4},{24,8},{28,12},{1,17},{... | collective-permute-start | bytes 393224 | tf_op jit(solution)/shard_map/ppermute | solution.py:324
  22.6 3.2 %grad_rows.3 = (bf16[512,256]{1,0:T(8,128)(2,1)S(1)}, bf16[512,256]{1,0:T(8,128)(2,1)S(1)}, bf16[512,256]{1,0:T(8,128)(2,1)}, bf16[512,256]{1,0:T(8,128)(2,1)}) custom-call(bf16[512,2048]{1,0:T(8,128)(2,1)S(1)} %copy-done.6, bf16[2048,2048]{1,0:T(8,128)(2,1)S(1)} %copy-done), custom_call_target="tpu_custom_call" | custom-call | tf_op jit(solution)/shard_map/grad_rows/pallas_call | solution.py:66
  26.5 2.1 %grad_rows.4 = (bf16[512,256]{1,0:T(8,128)(2,1)}, bf16[512,256]{1,0:T(8,128)(2,1)}) custom-call(bf16[512,2048]{1,0:T(8,128)(2,1)S(1)} %copy-done.6, bf16[2048,2048]{1,0:T(8,128)(2,1)S(1)} %copy-done), custom_call_target="tpu_custom_call" | custom-call | tf_op jit(solution)/shard_map/grad_rows/pallas_call | solution.py:66
  33.4 1.6 %copy-done.5 = bf16[2048,512]{1,0:T(8,128)(2,1)S(1)} copy-done((bf16[2048,512]{1,0:T(8,128)(2,1)S(1)}, bf16[2048,512]{1,0:T(8,128)(2,1)}, u32[]{:S(2)}) %copy-start.5) | copy-done | bytes 2097176
  34.9 4.0 %forward.1 = (bf16[512,256]{1,0:T(8,128)(2,1)S(1)}, bf16[512,256]{1,0:T(8,128)(2,1)S(1)}, bf16[512,256]{1,0:T(8,128)(2,1)S(1)}, bf16[512,256]{1,0:T(8,128)(2,1)S...) custom-call(bf16[2048,512]{1,0:T(8,128)(2,1)S(1)} %copy-done.5, ...), custom_call_target="tpu_custom_call" | custom-call | tf_op jit(solution)/shard_map/forward/pallas_call | solution.py:66
  38.9 4.7 %backward.2 = (bf16[2048,512]{1,0:T(8,128)(2,1)}, bf16[2048,256]{1,0:T(8,128)(2,1)S(1)}, bf16[2048,256]{1,0:T(8,128)(2,1)S(1)}, f32[2,128,128]{2,1,0:T(8,128)S(1)}, bf16[2,128,128]{2,1,0:T(8,128)(2,1)S(1)}) custom-call(bf16[512,256]{1,0:T(8,128)(2,1)S(1)} %copy-done.8, bf16[512,256]{1,0:T(8,128)(2,1)} %collective-permute-done.12.refs_1_, ...), custom_call_target="tpu_custom_call" | custom-call | tf_op jit(solution)/shard_map/backward/pallas_call | solution.py:66
  43.6 3.8 %backward.3 = (bf16[2048,512]{1,0:T(8,128)(2,1)}, bf16[2048,256]{1,0:T(8,128)(2,1)S(1)}, bf16[2048,256]{1,0:T(8,128)(2,1)S(1)}, f32[2,128,128]{2,1,0:T(8,128)S(1)}, bf16[2,128,128]{2,1,0:T(8,128)(2,1)S(1)}) custom-call(bf16[512,256]{1,0:T(8,128)(2,1)S(1)} %get-tuple-element.49.refs_0_, ...), custom_call_target="tpu_custom_call", output_to_operand_aliasing={{0}: (10, {})} | custom-call | tf_op jit(solution)/shard_map/backward/pallas_call | solution.py:66
  47.4 1.6 %collective-permute-start.15 = (bf16[2,128,128]{2,1,0:T(8,128)(2,1)S(1)}, bf16[2,128,128]{2,1,0:T(8,128)(2,1)S(1)}, u32[]{:S(2)}, u32[]{:S(2)}) collective-permute-start(bf16[2,128,128]{2,1,0:T(8,128)(2,1)S(1)} %get-tuple-element.64), channel_id=1, source_target_pairs={{0,4},{4,0},{8,12},{12,8},{16,20},{20,16},{24,28},{28,24},{1,5},{5... | collective-permute-start | bytes 196616 | tf_op jit(solution)/shard_map/ppermute | solution.py:324
  52.3 2.3 %collective-permute-done.18 = bf16[2,128,128]{2,1,0:T(8,128)(2,1)S(1)} collective-permute-done((bf16[2,128,128]{2,1,0:T(8,128)(2,1)S(1)}, bf16[2,128,128]{2,1,0:T(8,128)(2,1)S(1)}, u32[]{:S(2)}, u32[]{:S(2)}) %collective-permute-start.18) | collective-permute-done | bytes 65568 | tf_op jit(solution)/shard_map/ppermute | solution.py:324
  57.6 2.0 %collective-permute-done.19 = bf16[2,128,128]{2,1,0:T(8,128)(2,1)S(1)} collective-permute-done((bf16[2,128,128]{2,1,0:T(8,128)(2,1)S(1)}, bf16[2,128,128]{2,1,0:T(8,128)(2,1)S(1)}, u32[]{:S(2)}, u32[]{:S(2)}) %collective-permute-start.19) | collective-permute-done | bytes 65568 | tf_op jit(solution)/shard_map/ppermute | solution.py:324
  61.1 2.2 %collective-permute-done.17 = bf16[2,128,128]{2,1,0:T(8,128)(2,1)S(1)} collective-permute-done((bf16[2,128,128]{2,1,0:T(8,128)(2,1)S(1)}, bf16[2,128,128]{2,1,0:T(8,128)(2,1)S(1)}, u32[]{:S(2)}, u32[]{:S(2)}) %collective-permute-start.17) | collective-permute-done | bytes 65568 | tf_op jit(solution)/shard_map/ppermute | solution.py:324
  63.3 1.8 %collective-permute-done.20 = bf16[2,128,128]{2,1,0:T(8,128)(2,1)S(1)} collective-permute-done((bf16[2,128,128]{2,1,0:T(8,128)(2,1)S(1)}, bf16[2,128,128]{2,1,0:T(8,128)(2,1)S(1)}, u32[]{:S(2)}, u32[]{:S(2)}) %collective-permute-start.20) | collective-permute-done | bytes 65568 | tf_op jit(solution)/shard_map/ppermute | solution.py:324
  66.2 2.9 %later_grads.2 = (bf16[2048,512]{1,0:T(8,128)(2,1)}, bf16[2048,512]{1,0:T(8,128)(2,1)}) custom-call(bf16[2048,512]{1,0:T(8,128)(2,1)S(1)} %copy-done.5, bf16[2048,512]{1,0:T(8,128)(2,1)S(1)} %copy-done.2, bf16[2048,512]{1,0:T(8,128)(2,1)S(1)} %copy-done.4, bf16[2048,512]{1,0:T(8,128)(2,1)S(1)} %get-tuple-element.61.refs_3_, ...), custom_call_target="tpu_custom_call" | custom-call | tf_op jit(solution)/shard_map/later_grads/pallas_call | solution.py:66
  69.1 2.9 %later_grads.3 = (bf16[2048,512]{1,0:T(8,128)(2,1)}, bf16[2048,512]{1,0:T(8,128)(2,1)}) custom-call(bf16[2048,512]{1,0:T(8,128)(2,1)S(1)} %copy-done.5, bf16[2048,512]{1,0:T(8,128)(2,1)S(1)} %copy-done.2, bf16[2048,512]{1,0:T(8,128)(2,1)S(1)} %copy-done.4, ...), custom_call_target="tpu_custom_call", output_to_operand_aliasing={{0}: (7, {}), {1}: (8, {})} | custom-call | tf_op jit(solution)/shard_map/later_grads/pallas_call | solution.py:66
  72.0 3.4 %project.2.refs_3_ = f32[512,2048]{1,0:T(8,128)S(1)} custom-call(bf16[512,256]{1,0:T(8,128)(2,1)S(1)} %collective-permute-done.5.refs_0_, bf16[512,256]{1,0:T(8,128)(2,1)S(1)} %collective-permute-done.6.refs_1_, bf16[512,256]{1,0:T(8,128)(2,1)S(1)} %collective-permute-done.7.refs_2_, bf16[512,256]{1,0:T(8,128)(2,1)S(1)} %get-tuple-element.46.refs_3_, ...), custom_call_target="tpu_custom_call" | custom-call | tf_op jit(solution)/shard_map/project/pallas_call | solution.py:66
  75.5 3.0 %collective-permute-done.4.refs_1_ = bf16[512,256]{1,0:T(8,128)(2,1)S(1)} collective-permute-done((bf16[512,256]{1,0:T(8,128)(2,1)S(1)}, bf16[512,256]{1,0:T(8,128)(2,1)S(1)}, u32[]{:S(2)}, u32[]{:S(2)}) %collective-permute-start.4) | collective-permute-done | bytes 262176 | tf_op jit(solution)/shard_map/ppermute | solution.py:318
  78.5 2.1 %project.3 = bf16[512,2048]{1,0:T(8,128)(2,1)} custom-call(bf16[512,256]{1,0:T(8,128)(2,1)S(1)} %collective-permute-done.3.refs_0_, bf16[512,256]{1,0:T(8,128)(2,1)S(1)} %collective-permute-done.4.refs_1_, bf16[2048,2048]{1,0:T(8,128)(2,1)S(1)} %bitcast.1, f32[512,2048]{1,0:T(8,128)S(1)} %project.2.refs_3_), custom_call_target="tpu_custom_call" | custom-call | tf_op jit(solution)/shard_map/project/pallas_call | solution.py:66
  (65 shorter events, 16.7 us)
Async XLA Ops:
  3.8 9.2 %copy-start.6 = (bf16[512,2048]{1,0:T(8,128)(2,1)S(1)}, bf16[512,2048]{1,0:T(8,128)(2,1)}, u32[]{:S(2)}) copy-start(bf16[512,2048]{1,0:T(8,128)(2,1)} %d.5) | copy-start | bytes 6291460
  4.6 6.5 %collective-permute-start = (bf16[4,128,128]{2,1,0:T(8,128)(2,1)S(1)}, bf16[4,128,128]{2,1,0:T(8,128)(2,1)S(1)}, u32[]{:S(2)}, u32[]{:S(2)}) collective-permute-start(bf16[4,128,128]{2,1,0:T(8,128)(2,1)S(1)} %get-tuple-element.39), channel_id=1, source_target_pairs={{0,4},{4,0},{8,12},{12,8},{16,20},{20,16},{24,28},{28,24},{1,5},{5... | collective-permute-start | bytes 393224 | tf_op jit(solution)/shard_map/ppermute | solution.py:324
  11.2 8.7 %collective-permute-start.1 = (bf16[4,128,128]{2,1,0:T(8,128)(2,1)S(1)}, bf16[4,128,128]{2,1,0:T(8,128)(2,1)S(1)}, u32[]{:S(2)}, u32[]{:S(2)}) collective-permute-start(bf16[4,128,128]{2,1,0:T(8,128)(2,1)S(1)} %fusion.3), channel_id=1, source_target_pairs={{0,8},{4,12},{8,0},{12,4},{16,24},{20,28},{24,16},{28,20},{1,9},{5... | collective-permute-start | bytes 393224 | tf_op jit(solution)/shard_map/ppermute | solution.py:324
  18.4 11.6 %collective-permute-start.13 = (bf16[512,256]{1,0:T(8,128)(2,1)S(1)}, bf16[512,256]{1,0:T(8,128)(2,1)S(1)}, u32[]{:S(2)}, u32[]{:S(2)}) collective-permute-start(bf16[512,256]{1,0:T(8,128)(2,1)S(1)} %get-tuple-element.57), channel_id=1, source_target_pairs={{0,2},{1,3},{2,0},{3,1},{4,6},{5,7},{6,4},{7,5},{8,10},{9,11},{10,... | collective-permute-start | bytes 786440 | tf_op jit(solution)/shard_map/ppermute | solution.py:318
  19.9 5.9 %copy-start.9 = (bf16[4,128,128]{2,1,0:T(8,128)(2,1)}, bf16[4,128,128]{2,1,0:T(8,128)(2,1)S(1)}, u32[]{:S(2)}) copy-start(bf16[4,128,128]{2,1,0:T(8,128)(2,1)S(1)} %collective-permute-done.1) | copy-start | bytes 393220
  19.9 10.1 %collective-permute-start.2 = (bf16[4,128,128]{2,1,0:T(8,128)(2,1)S(1)}, bf16[4,128,128]{2,1,0:T(8,128)(2,1)}, u32[]{:S(2)}, u32[]{:S(2)}) collective-permute-start(bf16[4,128,128]{2,1,0:T(8,128)(2,1)S(1)} %fusion.2), channel_id=1, source_target_pairs={{0,16},{4,20},{8,24},{12,28},{16,0},{20,4},{24,8},{28,12},{1,17},{... | collective-permute-start | bytes 393224 | tf_op jit(solution)/shard_map/ppermute | solution.py:324
  22.6 16.3 %collective-permute-start.14 = (bf16[512,256]{1,0:T(8,128)(2,1)}, bf16[512,256]{1,0:T(8,128)(2,1)}, u32[]{:S(2)}, u32[]{:S(2)}) collective-permute-start(bf16[512,256]{1,0:T(8,128)(2,1)} %get-tuple-element.58), channel_id=1, source_target_pairs={{0,3},{1,2},{2,1},{3,0},{4,7},{5,6},{6,5},{7,4},{8,11},{9,10},{10,... | collective-permute-start | bytes 786440 | tf_op jit(solution)/shard_map/ppermute | solution.py:318
  25.8 13.2 %collective-permute-start.12 = (bf16[512,256]{1,0:T(8,128)(2,1)}, bf16[512,256]{1,0:T(8,128)(2,1)}, u32[]{:S(2)}, u32[]{:S(2)}) collective-permute-start(bf16[512,256]{1,0:T(8,128)(2,1)} %get-tuple-element.56), channel_id=1, source_target_pairs={{0,1},{1,0},{2,3},{3,2},{4,5},{5,4},{6,7},{7,6},{8,9},{9,8},{10,11... | collective-permute-start | bytes 786440 | tf_op jit(solution)/shard_map/ppermute | solution.py:318
  28.5 15.1 %collective-permute-start.10 = (bf16[512,256]{1,0:T(8,128)(2,1)}, bf16[512,256]{1,0:T(8,128)(2,1)S(1)}, u32[]{:S(2)}, u32[]{:S(2)}) collective-permute-start(bf16[512,256]{1,0:T(8,128)(2,1)} %get-tuple-element.51), channel_id=1, source_target_pairs={{0,2},{1,3},{2,0},{3,1},{4,6},{5,7},{6,4},{7,5},{8,10},{9,11},{10,... | collective-permute-start | bytes 786440 | tf_op jit(solution)/shard_map/ppermute | solution.py:318
  30.0 13.6 %collective-permute-start.11 = (bf16[512,256]{1,0:T(8,128)(2,1)}, bf16[512,256]{1,0:T(8,128)(2,1)S(1)}, u32[]{:S(2)}, u32[]{:S(2)}) collective-permute-start(bf16[512,256]{1,0:T(8,128)(2,1)} %get-tuple-element.52), channel_id=1, source_target_pairs={{0,3},{1,2},{2,1},{3,0},{4,7},{5,6},{6,5},{7,4},{8,11},{9,10},{10,... | collective-permute-start | bytes 786440 | tf_op jit(solution)/shard_map/ppermute | solution.py:318
  30.0 13.6 %collective-permute-start.9 = (bf16[512,256]{1,0:T(8,128)(2,1)}, bf16[512,256]{1,0:T(8,128)(2,1)S(1)}, u32[]{:S(2)}, u32[]{:S(2)}) collective-permute-start(bf16[512,256]{1,0:T(8,128)(2,1)} %get-tuple-element.50), channel_id=1, source_target_pairs={{0,1},{1,0},{2,3},{3,2},{4,5},{5,4},{6,7},{7,6},{8,9},{9,8},{10,11... | collective-permute-start | bytes 786440 | tf_op jit(solution)/shard_map/ppermute | solution.py:318
  47.4 4.3 %collective-permute-start.15 = (bf16[2,128,128]{2,1,0:T(8,128)(2,1)S(1)}, bf16[2,128,128]{2,1,0:T(8,128)(2,1)S(1)}, u32[]{:S(2)}, u32[]{:S(2)}) collective-permute-start(bf16[2,128,128]{2,1,0:T(8,128)(2,1)S(1)} %get-tuple-element.64), channel_id=1, source_target_pairs={{0,4},{4,0},{8,12},{12,8},{16,20},{20,16},{24,28},{28,24},{1,5},{5... | collective-permute-start | bytes 196616 | tf_op jit(solution)/shard_map/ppermute | solution.py:324
  49.0 16.5 %collective-permute-start.5 = (bf16[512,256]{1,0:T(8,128)(2,1)S(1)}, bf16[512,256]{1,0:T(8,128)(2,1)S(1)}, u32[]{:S(2)}, u32[]{:S(2)}) collective-permute-start(bf16[512,256]{1,0:T(8,128)(2,1)S(1)} %get-tuple-element.43), channel_id=1, source_target_pairs={{0,3},{1,2},{2,1},{3,0},{4,7},{5,6},{6,5},{7,4},{8,11},{9,10},{10,... | collective-permute-start | bytes 786440 | tf_op jit(solution)/shard_map/ppermute | solution.py:318
  49.9 4.8 %collective-permute-start.18 = (bf16[2,128,128]{2,1,0:T(8,128)(2,1)S(1)}, bf16[2,128,128]{2,1,0:T(8,128)(2,1)S(1)}, u32[]{:S(2)}, u32[]{:S(2)}) collective-permute-start(bf16[2,128,128]{2,1,0:T(8,128)(2,1)S(1)} %get-tuple-element.68), channel_id=1, source_target_pairs={{0,4},{4,0},{8,12},{12,8},{16,20},{20,16},{24,28},{28,24},{1,5},{5... | collective-permute-start | bytes 196616 | tf_op jit(solution)/shard_map/ppermute | solution.py:324
  51.8 4.3 %collective-permute-start.16 = (bf16[2,128,128]{2,1,0:T(8,128)(2,1)S(1)}, bf16[2,128,128]{2,1,0:T(8,128)(2,1)S(1)}, u32[]{:S(2)}, u32[]{:S(2)}) collective-permute-start(bf16[2,128,128]{2,1,0:T(8,128)(2,1)S(1)} %fusion.10), channel_id=1, source_target_pairs={{0,8},{4,12},{8,0},{12,4},{16,24},{20,28},{24,16},{28,20},{1,9},{5... | collective-permute-start | bytes 196616 | tf_op jit(solution)/shard_map/ppermute | solution.py:324
  54.6 5.0 %collective-permute-start.19 = (bf16[2,128,128]{2,1,0:T(8,128)(2,1)S(1)}, bf16[2,128,128]{2,1,0:T(8,128)(2,1)S(1)}, u32[]{:S(2)}, u32[]{:S(2)}) collective-permute-start(bf16[2,128,128]{2,1,0:T(8,128)(2,1)S(1)} %fusion.11), channel_id=1, source_target_pairs={{0,8},{4,12},{8,0},{12,4},{16,24},{20,28},{24,16},{28,20},{1,9},{5... | collective-permute-start | bytes 196616 | tf_op jit(solution)/shard_map/ppermute | solution.py:324
  56.1 7.2 %collective-permute-start.17 = (bf16[2,128,128]{2,1,0:T(8,128)(2,1)S(1)}, bf16[2,128,128]{2,1,0:T(8,128)(2,1)S(1)}, u32[]{:S(2)}, u32[]{:S(2)}) collective-permute-start(bf16[2,128,128]{2,1,0:T(8,128)(2,1)S(1)} %fusion.6), channel_id=1, source_target_pairs={{0,16},{4,20},{8,24},{12,28},{16,0},{20,4},{24,8},{28,12},{1,17},{... | collective-permute-start | bytes 196616 | tf_op jit(solution)/shard_map/ppermute | solution.py:324
  59.7 5.4 %collective-permute-start.20 = (bf16[2,128,128]{2,1,0:T(8,128)(2,1)S(1)}, bf16[2,128,128]{2,1,0:T(8,128)(2,1)S(1)}, u32[]{:S(2)}, u32[]{:S(2)}) collective-permute-start(bf16[2,128,128]{2,1,0:T(8,128)(2,1)S(1)} %fusion.9), channel_id=1, source_target_pairs={{0,16},{4,20},{8,24},{12,28},{16,0},{20,4},{24,8},{28,12},{1,17},{... | collective-permute-start | bytes 196616 | tf_op jit(solution)/shard_map/ppermute | solution.py:324
  59.8 12.2 %collective-permute-start.6 = (bf16[512,256]{1,0:T(8,128)(2,1)S(1)}, bf16[512,256]{1,0:T(8,128)(2,1)S(1)}, u32[]{:S(2)}, u32[]{:S(2)}) collective-permute-start(bf16[512,256]{1,0:T(8,128)(2,1)S(1)} %get-tuple-element.44), channel_id=1, source_target_pairs={{0,2},{1,3},{2,0},{3,1},{4,6},{5,7},{6,4},{7,5},{8,10},{9,11},{10,... | collective-permute-start | bytes 786440 | tf_op jit(solution)/shard_map/ppermute | solution.py:318
  61.1 10.9 %collective-permute-start.7 = (bf16[512,256]{1,0:T(8,128)(2,1)S(1)}, bf16[512,256]{1,0:T(8,128)(2,1)S(1)}, u32[]{:S(2)}, u32[]{:S(2)}) collective-permute-start(bf16[512,256]{1,0:T(8,128)(2,1)S(1)} %get-tuple-element.45), channel_id=1, source_target_pairs={{0,1},{1,0},{2,3},{3,2},{4,5},{5,4},{6,7},{7,6},{8,9},{9,8},{10,11... | collective-permute-start | bytes 786440 | tf_op jit(solution)/shard_map/ppermute | solution.py:318
  63.3 8.7 %collective-permute-start.8 = (bf16[512,256]{1,0:T(8,128)(2,1)S(1)}, bf16[512,256]{1,0:T(8,128)(2,1)S(1)}, u32[]{:S(2)}, u32[]{:S(2)}) collective-permute-start(bf16[512,256]{1,0:T(8,128)(2,1)S(1)} %get-tuple-element.47), channel_id=1, source_target_pairs={{0,1},{1,0},{2,3},{3,2},{4,5},{5,4},{6,7},{7,6},{8,9},{9,8},{10,11... | collective-permute-start | bytes 786440 | tf_op jit(solution)/shard_map/ppermute | solution.py:318
  65.1 10.3 %collective-permute-start.3 = (bf16[512,256]{1,0:T(8,128)(2,1)S(1)}, bf16[512,256]{1,0:T(8,128)(2,1)S(1)}, u32[]{:S(2)}, u32[]{:S(2)}) collective-permute-start(bf16[512,256]{1,0:T(8,128)(2,1)S(1)} %get-tuple-element.41), channel_id=1, source_target_pairs={{0,3},{1,2},{2,1},{3,0},{4,7},{5,6},{6,5},{7,4},{8,11},{9,10},{10,... | collective-permute-start | bytes 786440 | tf_op jit(solution)/shard_map/ppermute | solution.py:318
  65.5 13.0 %collective-permute-start.4 = (bf16[512,256]{1,0:T(8,128)(2,1)S(1)}, bf16[512,256]{1,0:T(8,128)(2,1)S(1)}, u32[]{:S(2)}, u32[]{:S(2)}) collective-permute-start(bf16[512,256]{1,0:T(8,128)(2,1)S(1)} %get-tuple-element.42), channel_id=1, source_target_pairs={{0,2},{1,3},{2,0},{3,1},{4,6},{5,7},{6,4},{7,5},{8,10},{9,11},{10,... | collective-permute-start | bytes 786440 | tf_op jit(solution)/shard_map/ppermute | solution.py:318
  66.2 5.8 %slice-start = ((s8[8388608]{0:T(1024)(128)(4,1)}), s8[4194304]{0:T(1024)(128)(4,1)S(1)}, s32[]{:S(2)}) async-start(s8[8388608]{0:T(1024)(128)(4,1)} %bitcast), calls=%async_computation | async-start | bytes 8388608
  (10 other events, 29.7 us)

commit v3 on v2

--- a/solution.py
+++ b/solution.py
@@ -13,6 +13,7 @@
 f32 = jnp.float32
 bf16 = jnp.bfloat16
 VMEM_LIMIT = 16 << 20
+COST = {'grad_rows': 553680000, 'total_state': 276840000, 'forward': 1349595000, 'backward': 1280385000, 'later_grads': 986242500, 'project': 692100000, 'second_part': 69210000, 'held_back': 103815000}
 
 
 def mm(a, b, ca, cb):
@@ -60,37 +61,61 @@
     return pl.ds(pl.multiple_of(index * size, size), size)
 
 
-def run_kernel(body, args, outs, scratch=(), ncopies=0, name=None, into=None, sent=0):
+def run_kernel(body, args, outs, scratch=(), ncopies=0, name=None, into=(), sent=0, after=()):
     here, anywhere = pl.BlockSpec(memory_space=pltpu.VMEM), pl.BlockSpec(memory_space=pl.ANY)
-    into = list(into or [])
+    skip = len(after)
     return pl.pallas_call(
-        body,
-        in_specs=[here] * len(args) + [anywhere] * len(into),
+        lambda *refs: body(*refs[skip:]),
+        in_specs=[anywhere] * skip + [here] * len(args) + [anywhere] * len(into),
         out_specs=[anywhere] * sent + [here] * (len(outs) - sent),
         out_shape=[jax.ShapeDtypeStruct(*out) for out in outs],
         scratch_shapes=[pltpu.VMEM(*s) for s in scratch]
         + ([pltpu.SemaphoreType.DMA((ncopies,))] if ncopies else []),
-        input_output_aliases={len(args) + i: i for i in range(len(into))},
+        input_output_aliases={skip + len(args) + i: i for i in range(len(into))},
         compiler_params=pltpu.CompilerParams(vmem_limit_bytes=VMEM_LIMIT),
+        cost_estimate=pl.CostEstimate(flops=COST[name], bytes_accessed=0, transcendentals=0),
         name=name,
-    )(*args, *into)
-
-
-def grad_rows(d_out, w_out, pieces, chunks, cols):
-    rows = d_out.shape[0]
+    )(*after, *args, *into)
+
+
+def grad_rows(d_out, w_out, groups, width, chunks, after=(), beside=()):
+    rows, cols = d_out.shape[0], width // chunks
 
     def body(d, w, *outs):
-        me = lax.axis_index("head")
-        for (dist, c), out in zip(pieces, outs):
-            piece = span((me ^ dist) * chunks + c, cols)
-            out[...] = mm(d[...], w[piece], 1, 1).astype(bf16)
+        me, outs = lax.axis_index("head"), outs[len(beside) :]
+        for c in range(chunks):
+            for group, out in zip(groups, outs[c * len(groups) :]):
+                for i, dist in enumerate(group):
+                    piece = span((me ^ dist) * chunks + c, cols)
+                    out[i] = mm(d[...], w[piece], 1, 1).astype(bf16)
 
     return run_kernel(
-        body, (d_out, w_out), [((rows, cols), bf16)] * len(pieces), name="grad_rows"
-    )
-
-
-def total_state(key, value):
+        body,
+        (d_out, w_out, *beside),
+        [((len(group), rows, cols), bf16) for _ in range(chunks) for group in groups],
+        name="grad_rows",
+        after=after,
+    )
+
+
+def held_back(array, after):
+    def body(array, out):
+        out[...] = array[...]
+
+    return run_kernel(body, (array,), [(array.shape, array.dtype)], name="held_back", after=after)[0]
+
+
+def second_part(got, after):
+    def body(got, out):
+        out[0] = got[1]
+
+    (out,) = run_kernel(
+        body, (got,), [((1,) + got.shape[1:], got.dtype)], name="second_part", after=after
+    )
+    return out
+
+
+def total_state(key, value, after):
     heads = key.shape[1] // HDIM
     shape = (heads, HDIM, HDIM)
 
@@ -101,16 +126,25 @@
             o[h] = total
             ob[h] = total.astype(bf16)
 
-    return run_kernel(body, (key, value), [(shape, f32), (shape, bf16)], name="total_state")
-
-
-def forward(query, key, value, gain, before, chunks, nhead):
+    return run_kernel(body, (key, value), [(shape, f32), (shape, bf16)], name="total_state", after=after)
+
+
+def outside(arrived, later):
+    place = lax.axis_index("ctx")
+    total = 0.0
+    for step, got in enumerate(arrived):
+        wanted = (((place >> step) & 1) == 0) == later
+        total = total + jnp.where(wanted, got[...].astype(f32), 0.0)
+    return total
+
+
+def forward(query, key, value, gain, arrived, groups, after):
     tokens, width = query.shape
-    tile, cols = tokens // nhead, width // chunks
-    heads = width // HDIM
-    n = nhead * chunks
-
-    def body(q, k, v, gain, before, *refs):
+    nhead, n = sum(map(len, groups)), len(groups)
+    tile, heads = tokens // nhead, width // HDIM
+
+    def body(q, k, v, gain, *refs):
+        before, refs = outside(refs[: len(arrived)], False), refs[len(arrived) :]
         normed, (att, s, st, rows) = refs[:n], refs[n:]
         me = lax.axis_index("head")
         mask = causal_mask()
@@ -134,21 +168,21 @@
                 att[at] = x
                 inverse = lax.rsqrt(jnp.mean(x * x, axis=-1, keepdims=True) + epsilon)
                 rows[at] = (x * inverse * gain[:, at[1]].astype(f32)).astype(bf16)
-        for dist in range(nhead):
-            part = span(me ^ dist, tile)
-            for c in range(chunks):
-                normed[dist * chunks + c][...] = rows[part, c * cols : (c + 1) * cols]
+        for group, out in zip(groups, normed):
+            for i, dist in enumerate(group):
+                out[i] = rows[span(me ^ dist, tile)]
 
     whole = (tokens, width)
     outs = run_kernel(
         body,
-        (query, key, value, gain, before),
-        [((tile, cols), bf16)] * n + [(whole, f32), (whole, bf16), (whole, bf16)],
+        (query, key, value, gain, *arrived),
+        [((len(group), tile, width), bf16) for group in groups]
+        + [(whole, f32), (whole, bf16), (whole, bf16)],
         [(whole, bf16)],
         name="forward",
-    )
-    normed = {(d, c): outs[d * chunks + c] for d in range(nhead) for c in range(chunks)}
-    return normed, outs[n:]
+        after=after,
+    )
+    return outs[:n], outs[n:]
 
 
 def backward(pieces, query, key, value, gain, attended, states, into, chunk, cols):
@@ -158,11 +192,12 @@
     heads = cols // HDIM
     shape = (heads, HDIM, HDIM)
     first = chunk * cols
+    shifts = [first if piece.shape[2] == width else 0 for piece in pieces]
 
     def body(*refs):
         p, refs = refs[:nhead], refs[nhead:]
         q, k, v, gain, att, st = refs[:6]
-        gq_hbm, g, gs, tot, totb, gq, sems = refs[6 + (into is not None) :]
+        gq_hbm, g, gs, tot, totb, gq, sems = refs[6 + len(into) :]
         me = lax.axis_index("head")
         copies = Copies(sems)
         mask = causal_mask()
@@ -186,7 +221,8 @@
                 x = att[wide]
                 inverse = lax.rsqrt(jnp.mean(x * x, axis=-1, keepdims=True) + epsilon)
                 unit = x * inverse
-                grad_unit = p[t][here].astype(f32) * gain[:, wide[1]].astype(f32)
+                at = slice(shifts[t] + here[1].start, shifts[t] + here[1].stop)
+                grad_unit = p[t][0, here[0], at].astype(f32) * gain[:, wide[1]].astype(f32)
                 along = jnp.mean(grad_unit * unit, axis=-1, keepdims=True)
                 grads.append((inverse * (grad_unit - unit * along)).astype(bf16))
                 g[near] = grads[-1]
@@ -221,14 +257,15 @@
     )
 
 
-def later_grads(query, key, value, scores, g, grad_scores, after, into, chunk, cols, steps):
+def later_grads(query, key, value, scores, g, grad_scores, arrived, into, chunk, cols, steps):
     tokens, width = query.shape
     tile, heads = tokens // steps, cols // HDIM
     first = chunk * cols
 
     def body(*refs):
-        q, k, v, s, g, gs, after = refs[:7]
-        gk_hbm, gv_hbm, gk, gv, sems = refs[7 + (2 if into else 0) :]
+        q, k, v, s, g, gs = refs[:6]
+        after, refs = outside(refs[6 : 6 + len(arrived)], True), refs[6 + len(arrived) :]
+        gk_hbm, gv_hbm, gk, gv, sems = refs[len(into) :]
         copies = Copies(sems)
         stores, run = [], [after[h] for h in range(heads)]
         for t in reversed(range(steps)):
@@ -255,7 +292,7 @@
     local = (tokens, cols)
     return run_kernel(
         body,
-        (query, key, value, scores, g, grad_scores, after),
+        (query, key, value, scores, g, grad_scores, *arrived),
         [((tokens, width), bf16)] * 2,
         [(local, bf16)] * 2,
         2 * steps,
@@ -265,43 +302,48 @@
     )
 
 
-def project(pieces, xs, w_out, acc, chunks, kind):
-    rows, cols = xs[0].shape
+def project(dists, xs, w_out, acc, kind, hand_on=False, after=()):
+    _, rows, width = xs[0].shape
     model = w_out.shape[1]
     tile = min(512, model)
-    steps, n = model // tile, len(pieces)
+    steps, n = model // tile, len(dists)
+    final = kind == bf16
 
     def body(*refs):
         x, w, refs = refs[:n], refs[n], refs[n + 1 :]
+        acc_ref, refs = (refs[0], refs[1:]) if acc is not None else (None, refs)
         me = lax.axis_index("head")
-        deep = jnp.concatenate([ref[...] for ref in x], axis=1)
-        rows_of = [span((me ^ dist) * chunks + c, cols) for dist, c in pieces]
+        if hand_on:
+            refs[1][0] = x[0][1]
+        deep = jnp.concatenate([ref[0] for ref in x], axis=1)
+        rows_of = [span(me ^ dist, width) for dist in dists]
         stores = []
         for j in range(steps):
             at = slice(j * tile, (j + 1) * tile)
             total = mm(deep, jnp.concatenate([w[r, at] for r in rows_of], axis=0), 1, 0)
             if acc is not None:
-                total = total + refs[0][:, at]
-            if kind == f32:
-                refs[-1][:, at] = total
-            else:
-                o_hbm, o, sems = refs[-3:]
+                total = total + acc_ref[:, at]
+            if final:
+                o_hbm, o, sems = refs
                 o[:, at] = total.astype(kind)
                 stores.append(pltpu.make_async_copy(o.at[:, at], o_hbm.at[:, at], sems.at[j]))
                 stores[-1].start()
+            else:
+                refs[0][:, at] = total
         for copy in stores:
             copy.wait()
 
-    final = kind == bf16
-    return run_kernel(
+    outs = run_kernel(
         body,
         (*xs, w_out) + (() if acc is None else (acc,)),
-        [((rows, model), kind)],
+        [((rows, model), kind)] + [((1, rows, width), bf16)] * hand_on,
         [((rows, model), kind)] if final else [],
         steps if final else 0,
         "project",
         sent=int(final),
-    )[0]
+        after=after,
+    )
+    return outs if hand_on else outs[0]
 
 
 def on_device(nctx, nhead, query, key, value, gain, w_out, d_out):
@@ -309,46 +351,65 @@
     local_heads = width // HDIM
     chunks = 2 if local_heads % 2 == 0 else 1
     cols = width // chunks
-    place = lax.axis_index("ctx")
     gain = gain.reshape(1, width)
 
     def swap(array, dist):
-        if dist == 0:
-            return array
         return lax.ppermute(array, "head", [(i, i ^ dist) for i in range(nhead)])
 
-    def others(total, rounded, later):
-        outside = jnp.zeros_like(total)
+    pairs_of = [(d, d + 1) for d in range(2, nhead, 2)]
+    near = [(d,) for d in range(min(nhead, 2))]
+    groups = pairs_of + near
+
+    def scan(total, rounded):
+        arrived = []
         dist = 1
         while dist < nctx:
-            got = lax.ppermute(rounded, "ctx", [(i, i ^ dist) for i in range(nctx)]).astype(f32)
-            wanted = ((place & dist) == 0) == later
-            outside = outside + jnp.where(wanted, got, 0.0)
-            total = total + got
-            rounded = total.astype(bf16)
+            arrived.append(lax.ppermute(rounded, "ctx", [(i, i ^ dist) for i in range(nctx)]))
             dist *= 2
-        return outside
-
-    far = [d for d in range(nhead - 1, 0, -1) if d > 1]
-    near = [d for d in range(nhead) if d <= 1]
-    sent = {}
+            if dist < nctx:
+                total = total + arrived[-1].astype(f32)
+                rounded = total.astype(bf16)
+        return arrived
+
+    pieces = [{} for _ in range(chunks)]
+    sent = grad_rows(d_out, w_out, pairs_of, width, chunks) if pairs_of else []
+
+    def send_far(c, after):
+        for i, group in enumerate(pairs_of):
+            out = sent[c * len(pairs_of) + i]
+            pieces[c][group[0]] = swap(held_back(out, after) if after else out, group[0])
+
+    def hand_on(c, after):
+        for group in pairs_of:
+            pieces[c][group[1]] = swap(second_part(pieces[c][group[0]], after), 1)
+
+    send_far(0, ())
+    total, rounded = total_state(key, value, sent)
+    arrived = scan(total, rounded)
+    mine = []
+    for group, out in zip(near, grad_rows(d_out, w_out, near, width, 1, (rounded,), (query, value))):
+        mine.append(swap(out, group[0]) if group[0] else out)
+        for c in range(chunks):
+            pieces[c][group[0]] = mine[-1]
+    for c in range(1, chunks):
+        send_far(c, [pieces[c - 1][group[0]] for group in pairs_of] + arrived[1:2] + mine[:1])
+    normed, (attended, scores, states) = forward(
+        query, key, value, gain, arrived, groups, mine[:1]
+    )
+    normed = {group: swap(x, group[0]) if group[0] else x for group, x in zip(groups, normed)}
+    out = project(
+        [d for d, in near],
+        [normed[group] for group in near],
+        w_out,
+        None,
+        f32 if pairs_of else bf16,
+    )
+
+    grad_query, carried, afters = [], [], []
     for c in range(chunks):
-        pieces = [(d, c) for d in far]
-        if far:
-            sent.update(zip(pieces, grad_rows(d_out, w_out, pieces, chunks, cols)))
-    pieces = [(d, c) for d in near for c in range(chunks)]
-    sent.update(zip(pieces, grad_rows(d_out, w_out, pieces, chunks, cols)))
-    got = {(d, c): swap(sent[d, c], d) for c in range(chunks) for d in reversed(range(nhead))}
-
-    before = others(*total_state(key, value), False)
-
-    normed, (attended, scores, states) = forward(query, key, value, gain, before, chunks, nhead)
-    normed = {(d, c): swap(normed[d, c], d) for c in range(chunks) for d in reversed(range(nhead))}
-
-    grad_query, carried = None, []
-    for c in range(chunks):
-        grad_query, g, grad_scores, total, rounded = backward(
-            [got[d, c] for d in range(nhead)],
+        hand_on(c, [attended])
+        query_part, g, grad_scores, total, rounded = backward(
+            [pieces[c][d] for d in range(nhead)],
             query,
             key,
             value,
@@ -359,18 +420,21 @@
             c,
             cols,
         )
-        grad_query = [grad_query]
-        carried.append((g, grad_scores, others(total, rounded, True)))
-    grads = None
+        grad_query = [query_part]
+        afters.append(scan(total, rounded))
+        carried.append((g, grad_scores))
+    grads = []
     for c in range(chunks):
-        grads = later_grads(query, key, value, scores, *carried[c], grads, c, cols, nhead)
-
-    last = [(d, chunks - 1) for d in far]
-    first = [p for p in normed if p not in last]
-    out = project(first, [normed[p] for p in first], w_out, None, chunks, f32 if last else bf16)
-    if last:
-        out = project(last, [normed[p] for p in last], w_out, out, chunks, bf16)
-    return out, grad_query[0], grads[0], grads[1]
+        grads = later_grads(
+            query, key, value, scores, *carried[c], afters[c], grads, c, cols, nhead
+        )
+
+    for group in pairs_of:
+        out, second = project(group[:1], [normed[group]], w_out, out, f32, True, [a[-1] for a in afters])
+        out = project(
+            group[1:], [swap(second, 1)], w_out, out, bf16 if group == pairs_of[-1] else f32
+        )
+    return out, grad_query[0], *grads
 
 
 def solution(mesh):

time: 81.1 us -> 72.2 us (0.89)
  Pallas kernels: 31.6 us -> 28.2 us
  local copies, waits for them, and re-layouts: 9.78 us -> 6.59 us
  waiting for transfers between devices: 17.3 us -> 15.1 us
  other arithmetic: 1.28 us -> 0.17 us
  starting transfers between devices: 19.7 us -> 20.8 us
    pallas_call x11 -> x14, Pallas kernels: 31.6 us -> 28.2 us  [run_kernel(): pl.pallas_call(lambda *refs: body(*refs[skip:]), in_specs=[anywhere] * sk...]
    unnamed x26 -> x18, local copies, waits for them, and re-layouts: 9.77 us -> 6.58 us
    ppermute x9, starting transfers between devices: 12.2 us -> 15.3 us  [scan(): lax.ppermute(rounded, 'ctx', [(i, i ^ dist) for i in range(nctx)])]
    ppermute x12 -> x8, starting transfers between devices: 7.53 us -> 5.54 us  [swap(): return lax.ppermute(array, 'head', [(i, i ^ dist) for i in range(nhead)])]
    ppermute x9, waiting for transfers between devices: 14.2 us -> 12.7 us  [scan(): lax.ppermute(rounded, 'ctx', [(i, i ^ dist) for i in range(nctx)])]
    add x2 -> x0, other arithmetic: 1.11 us -> none  [others(): outside = outside + jnp.where(wanted, got, 0.0)]
    ppermute x12 -> x8, waiting for transfers between devices: 3.05 us -> 2.38 us  [swap(): return lax.ppermute(array, 'head', [(i, i ^ dist) for i in range(nhead)])]
  transfers between devices with their start and end apart: 21 -> 17, of which waited for: 8 -> 7; matrix products, arithmetic and copies ran while one was open for 2% -> 0% of each run, Pallas kernels for 31% -> 31%
where the time goes in v3:
time: 72.2 us; the launch traced here: 71.9 us
  Pallas kernels  28.2 us (39%)
  starting transfers between devices  20.8 us (29%)
  waiting for transfers between devices  15.1 us (21%)
  local copies, waits for them, and re-layouts  6.59 us (9%)
  between operations  0.99 us (1%)
    pallas_call x14, Pallas kernels, run_kernel(): pl.pallas_call(lambda *refs: body(*refs[skip:]), in_specs=[anywhere] * sk...  28.2 us
    ppermute x9, starting transfers between devices, scan(): lax.ppermute(rounded, 'ctx', [(i, i ^ dist) for i in range(nctx)])  15.3 us
    ppermute x9, waiting for transfers between devices, scan(): lax.ppermute(rounded, 'ctx', [(i, i ^ dist) for i in range(nctx)])  12.7 us
    unnamed x18, local copies, waits for them, and re-layouts  6.58 us
    ppermute x8, starting transfers between devices, swap(): return lax.ppermute(array, 'head', [(i, i ^ dist) for i in range(nhead)])  5.54 us
    ppermute x8, waiting for transfers between devices, swap(): return lax.ppermute(array, 'head', [(i, i ^ dist) for i in range(nhead)])  2.38 us
  transfers between devices with their start and end apart: 17, of which 7 were waited for; matrix products, arithmetic and copies ran while one was open for 0% of the time, Pallas kernels for 31%

profile of v3, /device:TPU:0, one launch (start us, length us, event | category | flops | bytes accessed | tf_op | source)
XLA Modules:
  0.0 71.9 jit_solution(15711302582875844186)
XLA Ops:
  0.6 3.4 %copy-done = bf16[2048,2048]{1,0:T(8,128)(2,1)S(1)} copy-done((bf16[2048,2048]{1,0:T(8,128)(2,1)S(1)}, bf16[2048,2048]{1,0:T(8,128)(2,1)}, u32[]{:S(2)}) %copy-start) | copy-done | bytes 8388632
  4.0 1.6 %copy-done.6 = bf16[512,2048]{1,0:T(8,128)(2,1)S(1)} copy-done((bf16[512,2048]{1,0:T(8,128)(2,1)S(1)}, bf16[512,2048]{1,0:T(8,128)(2,1)}, u32[]{:S(2)}) %copy-start.6) | copy-done | bytes 2097176
  5.6 2.4 %grad_rows.2 = (bf16[2,512,256]{2,1,0:T(8,128)(2,1)S(1)}, bf16[2,512,256]{2,1,0:T(8,128)(2,1)S(1)}) custom-call(bf16[512,2048]{1,0:T(8,128)(2,1)S(1)} %copy-done.6, bf16[2048,2048]{1,0:T(8,128)(2,1)S(1)} %copy-done), custom_call_target="tpu_custom_call" | custom-call | flops 553680000 | tf_op jit(solution)/shard_map/grad_rows/pallas_call | solution.py:67
  8.0 3.0 %collective-permute-start.1 = (bf16[2,512,256]{2,1,0:T(8,128)(2,1)S(1)}, bf16[2,512,256]{2,1,0:T(8,128)(2,1)S(1)}, u32[]{:S(2)}, u32[]{:S(2)}) collective-permute-start(bf16[2,512,256]{2,1,0:T(8,128)(2,1)S(1)} %get-tuple-element.32.refs_0_), channel_id=1, source_target_pairs={{0,2},{1,3},{2,0},{3,1},{4,6},{5,7},{6,4},{7,5},{8,10},{9,11},{10,... | collective-permute-start | bytes 1572872 | tf_op jit(solution)/shard_map/ppermute | solution.py:357
  11.0 1.6 %copy-done.3 = bf16[2048,512]{1,0:T(8,128)(2,1)S(1)} copy-done((bf16[2048,512]{1,0:T(8,128)(2,1)S(1)}, bf16[2048,512]{1,0:T(8,128)(2,1)}, u32[]{:S(2)}) %copy-start.3) | copy-done | bytes 2097176
  13.4 1.6 %collective-permute-start.2 = (bf16[4,128,128]{2,1,0:T(8,128)(2,1)S(1)}, bf16[4,128,128]{2,1,0:T(8,128)(2,1)S(1)}, u32[]{:S(2)}, u32[]{:S(2)}) collective-permute-start(bf16[4,128,128]{2,1,0:T(8,128)(2,1)S(1)} %get-tuple-element.34.refs_0_), channel_id=1, source_target_pairs={{0,4},{4,0},{8,12},{12,8},{16,20},{20,16},{24,28},{28,24},{1,5},{5... | collective-permute-start | bytes 393224 | tf_op jit(solution)/shard_map/ppermute | solution.py:367
  15.0 3.4 %collective-permute-done.2.refs_5_ = bf16[4,128,128]{2,1,0:T(8,128)(2,1)S(1)} collective-permute-done((bf16[4,128,128]{2,1,0:T(8,128)(2,1)S(1)}, bf16[4,128,128]{2,1,0:T(8,128)(2,1)S(1)}, u32[]{:S(2)}, u32[]{:S(2)}) %collective-permute-start.2) | collective-permute-done | bytes 131104 | tf_op jit(solution)/shard_map/ppermute | solution.py:367
  18.4 1.6 %collective-permute-start.3 = (bf16[4,128,128]{2,1,0:T(8,128)(2,1)S(1)}, bf16[4,128,128]{2,1,0:T(8,128)(2,1)S(1)}, u32[]{:S(2)}, u32[]{:S(2)}) collective-permute-start(bf16[4,128,128]{2,1,0:T(8,128)(2,1)S(1)} %fusion), channel_id=1, source_target_pairs={{0,8},{4,12},{8,0},{12,4},{16,24},{20,28},{24,16},{28,20},{1,9},{5... | collective-permute-start | bytes 393224 | tf_op jit(solution)/shard_map/ppermute | solution.py:367
  20.1 2.4 %grad_rows.3 = (bf16[1,512,512]{2,1,0:T(8,128)(2,1)S(1)}, bf16[1,512,512]{2,1,0:T(8,128)(2,1)S(1)}) custom-call(bf16[4,128,128]{2,1,0:T(8,128)(2,1)S(1)} %get-tuple-element.34.refs_0_, bf16[512,2048]{1,0:T(8,128)(2,1)S(1)} %copy-done.7, bf16[2048,2048]{1,0:T(8,128)(2,1)S(1)} %copy-done.1, bf16[2048,512]{1,0:T(8,128)(2,1)S(1)} %copy-done.5, ...), custom_call_target="tpu_custom_call" | custom-call | flops 553680000 | tf_op jit(solution)/shard_map/grad_rows/pallas_call | solution.py:67
  24.8 2.7 %collective-permute-start.4 = (bf16[4,128,128]{2,1,0:T(8,128)(2,1)S(1)}, bf16[4,128,128]{2,1,0:T(8,128)(2,1)S(1)}, u32[]{:S(2)}, u32[]{:S(2)}) collective-permute-start(bf16[4,128,128]{2,1,0:T(8,128)(2,1)S(1)} %add_convert_fusion), channel_id=1, source_target_pairs={{0,16},{4,20},{8,24},{12,28},{16,0},{20,4},{24,8},{28,12},{1,17},{... | collective-permute-start | bytes 393224 | tf_op jit(solution)/shard_map/ppermute | solution.py:367
  27.5 5.2 %collective-permute-done.4.refs_7_ = bf16[4,128,128]{2,1,0:T(8,128)(2,1)S(1)} collective-permute-done((bf16[4,128,128]{2,1,0:T(8,128)(2,1)S(1)}, bf16[4,128,128]{2,1,0:T(8,128)(2,1)S(1)}, u32[]{:S(2)}, u32[]{:S(2)}) %collective-permute-start.4) | collective-permute-done | bytes 131104 | tf_op jit(solution)/shard_map/ppermute | solution.py:367
  32.7 3.9 %forward.1 = (bf16[2,512,512]{2,1,0:T(8,128)(2,1)S(1)}, bf16[1,512,512]{2,1,0:T(8,128)(2,1)S(1)}, bf16[1,512,512]{2,1,0:T(8,128)(2,1)S(1)}, f32[2048,512]{1,0:T(...) custom-call(bf16[1,512,512]{2,1,0:T(8,128)(2,1)S(1)} %get-tuple-element.35.refs_0_.refs_2_, ...), custom_call_target="tpu_custom_call" | custom-call | flops 1349595008 | tf_op jit(solution)/shard_map/forward/pallas_call | solution.py:67
  38.2 3.5 %backward.2 = (bf16[2048,512]{1,0:T(8,128)(2,1)}, bf16[2048,256]{1,0:T(8,128)(2,1)S(1)}, bf16[2048,256]{1,0:T(8,128)(2,1)S(1)}, f32[2,128,128]{2,1,0:T(8,128)S(1)}, bf16[2,128,128]{2,1,0:T(8,128)(2,1)S(1)}) custom-call(bf16[1,512,512]{2,1,0:T(8,128)(2,1)S(1)} %get-tuple-element.35.refs_0_.refs_2_, bf16[1,512,512]{2,1,0:T(8,128)(2,1)S(1)} %collective-permute-done.refs_1_, ...), custom_call_target="tpu_custom_call" | custom-call | flops 1280385024 | tf_op jit(solution)/shard_map/backward/pallas_call | solution.py:67
  41.7 1.6 %collective-permute-start.6 = (bf16[2,128,128]{2,1,0:T(8,128)(2,1)S(1)}, bf16[2,128,128]{2,1,0:T(8,128)(2,1)S(1)}, u32[]{:S(2)}, u32[]{:S(2)}) collective-permute-start(bf16[2,128,128]{2,1,0:T(8,128)(2,1)S(1)} %get-tuple-element.41), channel_id=1, source_target_pairs={{0,4},{4,0},{8,12},{12,8},{16,20},{20,16},{24,28},{28,24},{1,5},{5... | collective-permute-start | bytes 196616 | tf_op jit(solution)/shard_map/ppermute | solution.py:367
  43.3 3.7 %backward.3 = (bf16[2048,512]{1,0:T(8,128)(2,1)}, bf16[2048,256]{1,0:T(8,128)(2,1)S(1)}, bf16[2048,256]{1,0:T(8,128)(2,1)S(1)}, f32[2,128,128]{2,1,0:T(8,128)S(1)}, bf16[2,128,128]{2,1,0:T(8,128)(2,1)S(1)}) custom-call(bf16[1,512,512]{2,1,0:T(8,128)(2,1)S(1)} %get-tuple-element.35.refs_0_.refs_2_, ...), custom_call_target="tpu_custom_call", output_to_operand_aliasing={{0}: (10, {})} | custom-call | flops 1280385024 | tf_op jit(solution)/shard_map/backward/pallas_call | solution.py:67
  48.9 2.4 %collective-permute-done.11.refs_6_ = bf16[2,128,128]{2,1,0:T(8,128)(2,1)S(1)} collective-permute-done((bf16[2,128,128]{2,1,0:T(8,128)(2,1)S(1)}, bf16[2,128,128]{2,1,0:T(8,128)(2,1)S(1)}, u32[]{:S(2)}, u32[]{:S(2)}) %collective-permute-start.11) | collective-permute-done | bytes 65568 | tf_op jit(solution)/shard_map/ppermute | solution.py:367
  52.7 2.9 %collective-permute-start.8 = (bf16[2,128,128]{2,1,0:T(8,128)(2,1)S(1)}, bf16[2,128,128]{2,1,0:T(8,128)(2,1)S(1)}, u32[]{:S(2)}, u32[]{:S(2)}) collective-permute-start(bf16[2,128,128]{2,1,0:T(8,128)(2,1)S(1)} %add_convert_fusion.2), channel_id=1, source_target_pairs={{0,16},{4,20},{8,24},{12,28},{16,0},{20,4},{24,8},{28,12},{1,17},{... | collective-permute-start | bytes 196616 | tf_op jit(solution)/shard_map/ppermute | solution.py:367
  56.2 1.8 %collective-permute-start.13 = (bf16[2,128,128]{2,1,0:T(8,128)(2,1)S(1)}, bf16[2,128,128]{2,1,0:T(8,128)(2,1)S(1)}, u32[]{:S(2)}, u32[]{:S(2)}) collective-permute-start(bf16[2,128,128]{2,1,0:T(8,128)(2,1)S(1)} %add_convert_fusion.1), channel_id=1, source_target_pairs={{0,16},{4,20},{8,24},{12,28},{16,0},{20,4},{24,8},{28,12},{1,17},{... | collective-permute-start | bytes 196616 | tf_op jit(solution)/shard_map/ppermute | solution.py:367
  58.0 2.3 %project.3.refs_4_ = f32[512,2048]{1,0:T(8,128)S(1)} custom-call(bf16[1,512,512]{2,1,0:T(8,128)(2,1)S(1)} %get-tuple-element.46.refs_0_, bf16[1,512,512]{2,1,0:T(8,128)(2,1)S(1)} %collective-permute-done.15.refs_1_, bf16[2048,2048]{1,0:T(8,128)(2,1)S(1)} %copy-done.1), custom_call_target="tpu_custom_call" | custom-call | flops 692099968 | tf_op jit(solution)/shard_map/project/pallas_call | solution.py:67
  60.4 2.0 %collective-permute-done.14.refs_2_ = bf16[2,512,512]{2,1,0:T(8,128)(2,1)S(1)} collective-permute-done((bf16[2,512,512]{2,1,0:T(8,128)(2,1)S(1)}, bf16[2,512,512]{2,1,0:T(8,128)(2,1)S(1)}, u32[]{:S(2)}, u32[]{:S(2)}) %collective-permute-start.14) | collective-permute-done | bytes 1048608 | tf_op jit(solution)/shard_map/ppermute | solution.py:357
  62.4 1.3 %project.4 = (f32[512,2048]{1,0:T(8,128)S(1)}, bf16[1,512,512]{2,1,0:T(8,128)(2,1)S(1)}) custom-call(bf16[2,128,128]{2,1,0:T(8,128)(2,1)S(1)} %collective-permute-done.8.refs_0_.refs_8_, bf16[2,128,128]{2,1,0:T(8,128)(2,1)S(1)} %collective-permute-done.13.refs_1_.refs_8_, bf16[2,512,512]{2,1,0:T(8,128)(2,1)S(1)} %collective-permute-done.14.refs_2_, ...), custom_call_target="tpu_custom_call" | custom-call | flops 692099968 | tf_op jit(solution)/shard_map/project/pallas_call | solution.py:67
  63.9 2.9 %later_grads.2 = (bf16[2048,512]{1,0:T(8,128)(2,1)}, bf16[2048,512]{1,0:T(8,128)(2,1)}) custom-call(bf16[2048,512]{1,0:T(8,128)(2,1)S(1)} %copy-done.5, bf16[2048,512]{1,0:T(8,128)(2,1)S(1)} %copy-done.4, bf16[2048,512]{1,0:T(8,128)(2,1)S(1)} %copy-done.2, bf16[2048,512]{1,0:T(8,128)(2,1)S(1)} %get-tuple-element.51.refs_3_, ...), custom_call_target="tpu_custom_call" | custom-call | flops 986242496 | tf_op jit(solution)/shard_map/later_grads/pallas_call | solution.py:67
  66.7 2.9 %later_grads.3 = (bf16[2048,512]{1,0:T(8,128)(2,1)}, bf16[2048,512]{1,0:T(8,128)(2,1)}) custom-call(bf16[2048,512]{1,0:T(8,128)(2,1)S(1)} %copy-done.5, bf16[2048,512]{1,0:T(8,128)(2,1)S(1)} %copy-done.4, bf16[2048,512]{1,0:T(8,128)(2,1)S(1)} %copy-done.2, ...), custom_call_target="tpu_custom_call", output_to_operand_aliasing={{0}: (9, {}), {1}: (10, {})} | custom-call | flops 986242496 | tf_op jit(solution)/shard_map/later_grads/pallas_call | solution.py:67
  69.6 2.1 %project.5 = bf16[512,2048]{1,0:T(8,128)(2,1)} custom-call(bf16[1,512,512]{2,1,0:T(8,128)(2,1)S(1)} %collective-permute-done.16.refs_0_, bf16[2048,2048]{1,0:T(8,128)(2,1)S(1)} %copy-done.1, f32[512,2048]{1,0:T(8,128)S(1)} %get-tuple-element.49.refs_2_), custom_call_target="tpu_custom_call" | custom-call | flops 692099968 | tf_op jit(solution)/shard_map/project/pallas_call | solution.py:67
  (49 shorter events, 8.8 us)
Async XLA Ops:
  0.6 3.4 %copy-start = (bf16[2048,2048]{1,0:T(8,128)(2,1)S(1)}, bf16[2048,2048]{1,0:T(8,128)(2,1)}, u32[]{:S(2)}) copy-start(bf16[2048,2048]{1,0:T(8,128)(2,1)} %refs_1_.9) | copy-start | bytes 25165828
  5.6 5.4 %copy-start.2 = (bf16[2048,512]{1,0:T(8,128)(2,1)S(1)}, bf16[2048,512]{1,0:T(8,128)(2,1)}, u32[]{:S(2)}) copy-start(bf16[2048,512]{1,0:T(8,128)(2,1)} %refs_2_.11) | copy-start | bytes 6291460
  5.6 14.5 %copy-start.1 = (bf16[2048,2048]{1,0:T(8,128)(2,1)S(1)}, bf16[2048,2048]{1,0:T(8,128)(2,1)}, u32[]{:S(2)}) copy-start(bf16[2048,2048]{1,0:T(8,128)(2,1)} %refs_1_.9) | copy-start | bytes 25165828
  8.0 15.5 %collective-permute-start.1 = (bf16[2,512,256]{2,1,0:T(8,128)(2,1)S(1)}, bf16[2,512,256]{2,1,0:T(8,128)(2,1)S(1)}, u32[]{:S(2)}, u32[]{:S(2)}) collective-permute-start(bf16[2,512,256]{2,1,0:T(8,128)(2,1)S(1)} %get-tuple-element.32.refs_0_), channel_id=1, source_target_pairs={{0,2},{1,3},{2,0},{3,1},{4,6},{5,7},{6,4},{7,5},{8,10},{9,11},{10,... | collective-permute-start | bytes 1572872 | tf_op jit(solution)/shard_map/ppermute | solution.py:357
  12.6 7.5 %copy-start.5 = (bf16[2048,512]{1,0:T(8,128)(2,1)S(1)}, bf16[2048,512]{1,0:T(8,128)(2,1)}, u32[]{:S(2)}) copy-start(bf16[2048,512]{1,0:T(8,128)(2,1)} %refs_0_.5) | copy-start | bytes 6291460
  12.6 7.5 %copy-start.7 = (bf16[512,2048]{1,0:T(8,128)(2,1)S(1)}, bf16[512,2048]{1,0:T(8,128)(2,1)}, u32[]{:S(2)}) copy-start(bf16[512,2048]{1,0:T(8,128)(2,1)} %refs_1_.7) | copy-start | bytes 6291460
  13.4 5.0 %collective-permute-start.2 = (bf16[4,128,128]{2,1,0:T(8,128)(2,1)S(1)}, bf16[4,128,128]{2,1,0:T(8,128)(2,1)S(1)}, u32[]{:S(2)}, u32[]{:S(2)}) collective-permute-start(bf16[4,128,128]{2,1,0:T(8,128)(2,1)S(1)} %get-tuple-element.34.refs_0_), channel_id=1, source_target_pairs={{0,4},{4,0},{8,12},{12,8},{16,20},{20,16},{24,28},{28,24},{1,5},{5... | collective-permute-start | bytes 393224 | tf_op jit(solution)/shard_map/ppermute | solution.py:367
  18.4 5.0 %collective-permute-start.3 = (bf16[4,128,128]{2,1,0:T(8,128)(2,1)S(1)}, bf16[4,128,128]{2,1,0:T(8,128)(2,1)S(1)}, u32[]{:S(2)}, u32[]{:S(2)}) collective-permute-start(bf16[4,128,128]{2,1,0:T(8,128)(2,1)S(1)} %fusion), channel_id=1, source_target_pairs={{0,8},{4,12},{8,0},{12,4},{16,24},{20,28},{24,16},{28,20},{1,9},{5... | collective-permute-start | bytes 393224 | tf_op jit(solution)/shard_map/ppermute | solution.py:367
  22.5 5.0 %copy-start.8 = (bf16[512]{0:T(512)(128)(2,1)S(1)}, bf16[512]{0:T(512)(128)(2,1)}, u32[]{:S(2)}) copy-start(bf16[512]{0:T(512)(128)(2,1)} %param.9) | copy-start | bytes 3076
  22.5 10.2 %copy-start.4 = (bf16[2048,512]{1,0:T(8,128)(2,1)S(1)}, bf16[2048,512]{1,0:T(8,128)(2,1)}, u32[]{:S(2)}) copy-start(bf16[2048,512]{1,0:T(8,128)(2,1)} %refs_1_.11) | copy-start | bytes 6291460
  23.5 13.2 %collective-permute-start.9 = (bf16[2,512,256]{2,1,0:T(8,128)(2,1)S(1)}, bf16[2,512,256]{2,1,0:T(8,128)(2,1)S(1)}, u32[]{:S(2)}, u32[]{:S(2)}) collective-permute-start(bf16[2,512,256]{2,1,0:T(8,128)(2,1)S(1)} %held_back.1), channel_id=1, source_target_pairs={{0,2},{1,3},{2,0},{3,1},{4,6},{5,7},{6,4},{7,5},{8,10},{9,11},{10,... | collective-permute-start | bytes 1572872 | tf_op jit(solution)/shard_map/ppermute | solution.py:357
  24.8 7.9 %collective-permute-start.4 = (bf16[4,128,128]{2,1,0:T(8,128)(2,1)S(1)}, bf16[4,128,128]{2,1,0:T(8,128)(2,1)S(1)}, u32[]{:S(2)}, u32[]{:S(2)}) collective-permute-start(bf16[4,128,128]{2,1,0:T(8,128)(2,1)S(1)} %add_convert_fusion), channel_id=1, source_target_pairs={{0,16},{4,20},{8,24},{12,28},{16,0},{20,4},{24,8},{28,12},{1,17},{... | collective-permute-start | bytes 393224 | tf_op jit(solution)/shard_map/ppermute | solution.py:367
  27.5 10.4 %collective-permute-start = (bf16[1,512,512]{2,1,0:T(8,128)(2,1)S(1)}, bf16[1,512,512]{2,1,0:T(8,128)(2,1)S(1)}, u32[]{:S(2)}, u32[]{:S(2)}) collective-permute-start(bf16[1,512,512]{2,1,0:T(8,128)(2,1)S(1)} %get-tuple-element.36), channel_id=1, source_target_pairs={{0,1},{1,0},{2,3},{3,2},{4,5},{5,4},{6,7},{7,6},{8,9},{9,8},{10,11... | collective-permute-start | bytes 1572872 | tf_op jit(solution)/shard_map/ppermute | solution.py:357
  36.6 1.6 %collective-permute-start.5 = (bf16[1,512,256]{2,1,0:T(8,128)(2,1)S(1)}, bf16[1,512,256]{2,1,0:T(8,128)(2,1)S(1)}, u32[]{:S(2)}, u32[]{:S(2)}) collective-permute-start(bf16[1,512,256]{2,1,0:T(8,128)(2,1)S(1)} %second_part.2), channel_id=1, source_target_pairs={{0,1},{1,0},{2,3},{3,2},{4,5},{5,4},{6,7},{7,6},{8,9},{9,8},{10,11... | collective-permute-start | bytes 786440 | tf_op jit(solution)/shard_map/ppermute | solution.py:357
  36.7 6.6 %collective-permute-start.10 = (bf16[1,512,256]{2,1,0:T(8,128)(2,1)S(1)}, bf16[1,512,256]{2,1,0:T(8,128)(2,1)S(1)}, u32[]{:S(2)}, u32[]{:S(2)}) collective-permute-start(bf16[1,512,256]{2,1,0:T(8,128)(2,1)S(1)} %second_part.3), channel_id=1, source_target_pairs={{0,1},{1,0},{2,3},{3,2},{4,5},{5,4},{6,7},{7,6},{8,9},{9,8},{10,11... | collective-permute-start | bytes 786440 | tf_op jit(solution)/shard_map/ppermute | solution.py:357
  37.3 25.1 %collective-permute-start.14 = (bf16[2,512,512]{2,1,0:T(8,128)(2,1)S(1)}, bf16[2,512,512]{2,1,0:T(8,128)(2,1)S(1)}, u32[]{:S(2)}, u32[]{:S(2)}) collective-permute-start(bf16[2,512,512]{2,1,0:T(8,128)(2,1)S(1)} %get-tuple-element.45), channel_id=1, source_target_pairs={{0,2},{1,3},{2,0},{3,1},{4,6},{5,7},{6,4},{7,5},{8,10},{9,11},{10,... | collective-permute-start | bytes 3145736 | tf_op jit(solution)/shard_map/ppermute | solution.py:357
  37.9 20.1 %collective-permute-start.15 = (bf16[1,512,512]{2,1,0:T(8,128)(2,1)S(1)}, bf16[1,512,512]{2,1,0:T(8,128)(2,1)S(1)}, u32[]{:S(2)}, u32[]{:S(2)}) collective-permute-start(bf16[1,512,512]{2,1,0:T(8,128)(2,1)S(1)} %get-tuple-element.47), channel_id=1, source_target_pairs={{0,1},{1,0},{2,3},{3,2},{4,5},{5,4},{6,7},{7,6},{8,9},{9,8},{10,11... | collective-permute-start | bytes 1572872 | tf_op jit(solution)/shard_map/ppermute | solution.py:357
  41.7 5.8 %collective-permute-start.6 = (bf16[2,128,128]{2,1,0:T(8,128)(2,1)S(1)}, bf16[2,128,128]{2,1,0:T(8,128)(2,1)S(1)}, u32[]{:S(2)}, u32[]{:S(2)}) collective-permute-start(bf16[2,128,128]{2,1,0:T(8,128)(2,1)S(1)} %get-tuple-element.41), channel_id=1, source_target_pairs={{0,4},{4,0},{8,12},{12,8},{16,20},{20,16},{24,28},{28,24},{1,5},{5... | collective-permute-start | bytes 196616 | tf_op jit(solution)/shard_map/ppermute | solution.py:367
  47.0 4.3 %collective-permute-start.11 = (bf16[2,128,128]{2,1,0:T(8,128)(2,1)S(1)}, bf16[2,128,128]{2,1,0:T(8,128)(2,1)S(1)}, u32[]{:S(2)}, u32[]{:S(2)}) collective-permute-start(bf16[2,128,128]{2,1,0:T(8,128)(2,1)S(1)} %get-tuple-element.44), channel_id=1, source_target_pairs={{0,4},{4,0},{8,12},{12,8},{16,20},{20,16},{24,28},{28,24},{1,5},{5... | collective-permute-start | bytes 196616 | tf_op jit(solution)/shard_map/ppermute | solution.py:367
  47.6 5.1 %collective-permute-start.7 = (bf16[2,128,128]{2,1,0:T(8,128)(2,1)S(1)}, bf16[2,128,128]{2,1,0:T(8,128)(2,1)S(1)}, u32[]{:S(2)}, u32[]{:S(2)}) collective-permute-start(bf16[2,128,128]{2,1,0:T(8,128)(2,1)S(1)} %fusion.1), channel_id=1, source_target_pairs={{0,8},{4,12},{8,0},{12,4},{16,24},{20,28},{24,16},{28,20},{1,9},{5... | collective-permute-start | bytes 196616 | tf_op jit(solution)/shard_map/ppermute | solution.py:367
  51.3 4.9 %collective-permute-start.12 = (bf16[2,128,128]{2,1,0:T(8,128)(2,1)S(1)}, bf16[2,128,128]{2,1,0:T(8,128)(2,1)S(1)}, u32[]{:S(2)}, u32[]{:S(2)}) collective-permute-start(bf16[2,128,128]{2,1,0:T(8,128)(2,1)S(1)} %fusion.2), channel_id=1, source_target_pairs={{0,8},{4,12},{8,0},{12,4},{16,24},{20,28},{24,16},{28,20},{1,9},{5... | collective-permute-start | bytes 196616 | tf_op jit(solution)/shard_map/ppermute | solution.py:367
  52.7 7.7 %collective-permute-start.8 = (bf16[2,128,128]{2,1,0:T(8,128)(2,1)S(1)}, bf16[2,128,128]{2,1,0:T(8,128)(2,1)S(1)}, u32[]{:S(2)}, u32[]{:S(2)}) collective-permute-start(bf16[2,128,128]{2,1,0:T(8,128)(2,1)S(1)} %add_convert_fusion.2), channel_id=1, source_target_pairs={{0,16},{4,20},{8,24},{12,28},{16,0},{20,4},{24,8},{28,12},{1,17},{... | collective-permute-start | bytes 196616 | tf_op jit(solution)/shard_map/ppermute | solution.py:367
  56.2 6.2 %collective-permute-start.13 = (bf16[2,128,128]{2,1,0:T(8,128)(2,1)S(1)}, bf16[2,128,128]{2,1,0:T(8,128)(2,1)S(1)}, u32[]{:S(2)}, u32[]{:S(2)}) collective-permute-start(bf16[2,128,128]{2,1,0:T(8,128)(2,1)S(1)} %add_convert_fusion.1), channel_id=1, source_target_pairs={{0,16},{4,20},{8,24},{12,28},{16,0},{20,4},{24,8},{28,12},{1,17},{... | collective-permute-start | bytes 196616 | tf_op jit(solution)/shard_map/ppermute | solution.py:367
  63.8 5.8 %collective-permute-start.16 = (bf16[1,512,512]{2,1,0:T(8,128)(2,1)S(1)}, bf16[1,512,512]{2,1,0:T(8,128)(2,1)S(1)}, u32[]{:S(2)}, u32[]{:S(2)}) collective-permute-start(bf16[1,512,512]{2,1,0:T(8,128)(2,1)S(1)} %get-tuple-element.48), channel_id=1, source_target_pairs={{0,1},{1,0},{2,3},{3,2},{4,5},{5,4},{6,7},{7,6},{8,9},{9,8},{10,11... | collective-permute-start | bytes 1572872 | tf_op jit(solution)/shard_map/ppermute | solution.py:357
  (2 other events, 3.2 us)

commit v4 on v3

--- a/solution.py
+++ b/solution.py
@@ -265,7 +265,8 @@
     def body(*refs):
         q, k, v, s, g, gs = refs[:6]
         after, refs = outside(refs[6 : 6 + len(arrived)], True), refs[6 + len(arrived) :]
-        gk_hbm, gv_hbm, gk, gv, sems = refs[len(into) :]
+        gk_hbm, gv_hbm, token, gk, gv, sems = refs[len(into) :]
+        token[...] = jnp.zeros_like(token)
         copies = Copies(sems)
         stores, run = [], [after[h] for h in range(heads)]
         for t in reversed(range(steps)):
@@ -293,7 +294,7 @@
     return run_kernel(
         body,
         (query, key, value, scores, g, grad_scores, *arrived),
-        [((tokens, width), bf16)] * 2,
+        [((tokens, width), bf16)] * 2 + [((8, HDIM), f32)],
         [(local, bf16)] * 2,
         2 * steps,
         "later_grads",
@@ -423,14 +424,15 @@
         grad_query = [query_part]
         afters.append(scan(total, rounded))
         carried.append((g, grad_scores))
-    grads = []
+    grads, tokens_out = [], []
     for c in range(chunks):
-        grads = later_grads(
+        *grads, token = later_grads(
             query, key, value, scores, *carried[c], afters[c], grads, c, cols, nhead
         )
+        tokens_out.append(token)
 
     for group in pairs_of:
-        out, second = project(group[:1], [normed[group]], w_out, out, f32, True, [a[-1] for a in afters])
+        out, second = project(group[:1], [normed[group]], w_out, out, f32, True, [a[-1] for a in afters] + tokens_out[:1])
         out = project(
             group[1:], [swap(second, 1)], w_out, out, bf16 if group == pairs_of[-1] else f32
         )

time: 72.2 us -> 71.9 us (level)
  starting transfers between devices: 20.8 us -> 18.9 us
  Pallas kernels: 28.2 us -> 29.5 us
    ppermute x9, starting transfers between devices: 15.3 us -> 13.4 us  [scan(): lax.ppermute(rounded, 'ctx', [(i, i ^ dist) for i in range(nctx)])]
    ppermute x9, waiting for transfers between devices: 12.7 us -> 14.5 us  [scan(): lax.ppermute(rounded, 'ctx', [(i, i ^ dist) for i in range(nctx)])]
    ppermute x8, waiting for transfers between devices: 2.38 us -> 1.03 us  [swap(): return lax.ppermute(array, 'head', [(i, i ^ dist) for i in range(nhead)])]
    pallas_call x14, Pallas kernels: 28.2 us -> 29.5 us  [run_kernel(): pl.pallas_call(lambda *refs: body(*refs[skip:]), in_specs=[anywhere] * sk...]
  transfers between devices with their start and end apart: 17 -> 17, of which waited for: 7 -> 8; matrix products, arithmetic and copies ran while one was open for 0% -> 0% of each run, Pallas kernels for 31% -> 33%
where the time goes in v4:
time: 71.9 us; the launch traced here: 71.7 us
  Pallas kernels  29.5 us (41%)
  starting transfers between devices  18.9 us (26%)
  waiting for transfers between devices  15.5 us (22%)
  local copies, waits for them, and re-layouts  6.59 us (9%)
  between operations  0.99 us (1%)
    pallas_call x14, Pallas kernels, run_kernel(): pl.pallas_call(lambda *refs: body(*refs[skip:]), in_specs=[anywhere] * sk...  29.5 us
    ppermute x9, waiting for transfers between devices, scan(): lax.ppermute(rounded, 'ctx', [(i, i ^ dist) for i in range(nctx)])  14.5 us
    ppermute x9, starting transfers between devices, scan(): lax.ppermute(rounded, 'ctx', [(i, i ^ dist) for i in range(nctx)])  13.4 us
    unnamed x18, local copies, waits for them, and re-layouts  6.58 us
    ppermute x8, starting transfers between devices, swap(): return lax.ppermute(array, 'head', [(i, i ^ dist) for i in range(nhead)])  5.55 us
  transfers between devices with their start and end apart: 17, of which 8 were waited for; matrix products, arithmetic and copies ran while one was open for 0% of the time, Pallas kernels for 33%

profile of v4, /device:TPU:0, one launch (start us, length us, event | category | flops | bytes accessed | tf_op | source)
XLA Modules:
  0.0 71.7 jit_solution(110924864863816783)
XLA Ops:
  0.6 3.4 %copy-done = bf16[2048,2048]{1,0:T(8,128)(2,1)S(1)} copy-done((bf16[2048,2048]{1,0:T(8,128)(2,1)S(1)}, bf16[2048,2048]{1,0:T(8,128)(2,1)}, u32[]{:S(2)}) %copy-start) | copy-done | bytes 8388632
  4.0 1.6 %copy-done.6 = bf16[512,2048]{1,0:T(8,128)(2,1)S(1)} copy-done((bf16[512,2048]{1,0:T(8,128)(2,1)S(1)}, bf16[512,2048]{1,0:T(8,128)(2,1)}, u32[]{:S(2)}) %copy-start.6) | copy-done | bytes 2097176
  5.6 2.4 %grad_rows.2 = (bf16[2,512,256]{2,1,0:T(8,128)(2,1)S(1)}, bf16[2,512,256]{2,1,0:T(8,128)(2,1)S(1)}) custom-call(bf16[512,2048]{1,0:T(8,128)(2,1)S(1)} %copy-done.6, bf16[2048,2048]{1,0:T(8,128)(2,1)S(1)} %copy-done), custom_call_target="tpu_custom_call" | custom-call | flops 553680000 | tf_op jit(solution)/shard_map/grad_rows/pallas_call | solution.py:67
  8.0 3.0 %collective-permute-start.1 = (bf16[2,512,256]{2,1,0:T(8,128)(2,1)S(1)}, bf16[2,512,256]{2,1,0:T(8,128)(2,1)S(1)}, u32[]{:S(2)}, u32[]{:S(2)}) collective-permute-start(bf16[2,512,256]{2,1,0:T(8,128)(2,1)S(1)} %get-tuple-element.33.refs_0_), channel_id=1, source_target_pairs={{0,2},{1,3},{2,0},{3,1},{4,6},{5,7},{6,4},{7,5},{8,10},{9,11},{10,... | collective-permute-start | bytes 1572872 | tf_op jit(solution)/shard_map/ppermute | solution.py:358
  11.0 1.6 %copy-done.3 = bf16[2048,512]{1,0:T(8,128)(2,1)S(1)} copy-done((bf16[2048,512]{1,0:T(8,128)(2,1)S(1)}, bf16[2048,512]{1,0:T(8,128)(2,1)}, u32[]{:S(2)}) %copy-start.3) | copy-done | bytes 2097176
  13.4 1.6 %collective-permute-start.2 = (bf16[4,128,128]{2,1,0:T(8,128)(2,1)S(1)}, bf16[4,128,128]{2,1,0:T(8,128)(2,1)S(1)}, u32[]{:S(2)}, u32[]{:S(2)}) collective-permute-start(bf16[4,128,128]{2,1,0:T(8,128)(2,1)S(1)} %get-tuple-element.35.refs_0_), channel_id=1, source_target_pairs={{0,4},{4,0},{8,12},{12,8},{16,20},{20,16},{24,28},{28,24},{1,5},{5... | collective-permute-start | bytes 393224 | tf_op jit(solution)/shard_map/ppermute | solution.py:368
  15.0 3.5 %collective-permute-done.2.refs_5_ = bf16[4,128,128]{2,1,0:T(8,128)(2,1)S(1)} collective-permute-done((bf16[4,128,128]{2,1,0:T(8,128)(2,1)S(1)}, bf16[4,128,128]{2,1,0:T(8,128)(2,1)S(1)}, u32[]{:S(2)}, u32[]{:S(2)}) %collective-permute-start.2) | collective-permute-done | bytes 131104 | tf_op jit(solution)/shard_map/ppermute | solution.py:368
  18.4 1.6 %collective-permute-start.3 = (bf16[4,128,128]{2,1,0:T(8,128)(2,1)S(1)}, bf16[4,128,128]{2,1,0:T(8,128)(2,1)S(1)}, u32[]{:S(2)}, u32[]{:S(2)}) collective-permute-start(bf16[4,128,128]{2,1,0:T(8,128)(2,1)S(1)} %fusion), channel_id=1, source_target_pairs={{0,8},{4,12},{8,0},{12,4},{16,24},{20,28},{24,16},{28,20},{1,9},{5... | collective-permute-start | bytes 393224 | tf_op jit(solution)/shard_map/ppermute | solution.py:368
  20.1 2.4 %grad_rows.3 = (bf16[1,512,512]{2,1,0:T(8,128)(2,1)S(1)}, bf16[1,512,512]{2,1,0:T(8,128)(2,1)S(1)}) custom-call(bf16[4,128,128]{2,1,0:T(8,128)(2,1)S(1)} %get-tuple-element.35.refs_0_, bf16[512,2048]{1,0:T(8,128)(2,1)S(1)} %copy-done.7, bf16[2048,2048]{1,0:T(8,128)(2,1)S(1)} %copy-done.1, bf16[2048,512]{1,0:T(8,128)(2,1)S(1)} %copy-done.5, ...), custom_call_target="tpu_custom_call" | custom-call | flops 553680000 | tf_op jit(solution)/shard_map/grad_rows/pallas_call | solution.py:67
  23.5 1.2 %collective-permute-start.9 = (bf16[2,512,256]{2,1,0:T(8,128)(2,1)S(1)}, bf16[2,512,256]{2,1,0:T(8,128)(2,1)S(1)}, u32[]{:S(2)}, u32[]{:S(2)}) collective-permute-start(bf16[2,512,256]{2,1,0:T(8,128)(2,1)S(1)} %held_back.1), channel_id=1, source_target_pairs={{0,2},{1,3},{2,0},{3,1},{4,6},{5,7},{6,4},{7,5},{8,10},{9,11},{10,... | collective-permute-start | bytes 1572872 | tf_op jit(solution)/shard_map/ppermute | solution.py:358
  24.8 2.7 %collective-permute-start.4 = (bf16[4,128,128]{2,1,0:T(8,128)(2,1)S(1)}, bf16[4,128,128]{2,1,0:T(8,128)(2,1)S(1)}, u32[]{:S(2)}, u32[]{:S(2)}) collective-permute-start(bf16[4,128,128]{2,1,0:T(8,128)(2,1)S(1)} %add_convert_fusion), channel_id=1, source_target_pairs={{0,16},{4,20},{8,24},{12,28},{16,0},{20,4},{24,8},{28,12},{1,17},{... | collective-permute-start | bytes 393224 | tf_op jit(solution)/shard_map/ppermute | solution.py:368
  27.5 5.2 %collective-permute-done.4.refs_7_ = bf16[4,128,128]{2,1,0:T(8,128)(2,1)S(1)} collective-permute-done((bf16[4,128,128]{2,1,0:T(8,128)(2,1)S(1)}, bf16[4,128,128]{2,1,0:T(8,128)(2,1)S(1)}, u32[]{:S(2)}, u32[]{:S(2)}) %collective-permute-start.4) | collective-permute-done | bytes 131104 | tf_op jit(solution)/shard_map/ppermute | solution.py:368
  32.7 4.2 %forward.1 = (bf16[2,512,512]{2,1,0:T(8,128)(2,1)S(1)}, bf16[1,512,512]{2,1,0:T(8,128)(2,1)S(1)}, bf16[1,512,512]{2,1,0:T(8,128)(2,1)S(1)}, f32[2048,512]{1,0:T(...) custom-call(bf16[1,512,512]{2,1,0:T(8,128)(2,1)S(1)} %get-tuple-element.36.refs_0_.refs_2_, ...), custom_call_target="tpu_custom_call" | custom-call | flops 1349595008 | tf_op jit(solution)/shard_map/forward/pallas_call | solution.py:67
  38.5 3.7 %backward.2 = (bf16[2048,512]{1,0:T(8,128)(2,1)}, bf16[2048,256]{1,0:T(8,128)(2,1)S(1)}, bf16[2048,256]{1,0:T(8,128)(2,1)S(1)}, f32[2,128,128]{2,1,0:T(8,128)S(1)}, bf16[2,128,128]{2,1,0:T(8,128)(2,1)S(1)}) custom-call(bf16[1,512,512]{2,1,0:T(8,128)(2,1)S(1)} %get-tuple-element.36.refs_0_.refs_2_, bf16[1,512,512]{2,1,0:T(8,128)(2,1)S(1)} %collective-permute-done.refs_1_, ...), custom_call_target="tpu_custom_call" | custom-call | flops 1280385024 | tf_op jit(solution)/shard_map/backward/pallas_call | solution.py:67
  42.2 1.6 %collective-permute-start.6 = (bf16[2,128,128]{2,1,0:T(8,128)(2,1)S(1)}, bf16[2,128,128]{2,1,0:T(8,128)(2,1)S(1)}, u32[]{:S(2)}, u32[]{:S(2)}) collective-permute-start(bf16[2,128,128]{2,1,0:T(8,128)(2,1)S(1)} %get-tuple-element.42), channel_id=1, source_target_pairs={{0,4},{4,0},{8,12},{12,8},{16,20},{20,16},{24,28},{28,24},{1,5},{5... | collective-permute-start | bytes 196616 | tf_op jit(solution)/shard_map/ppermute | solution.py:368
  43.8 3.8 %backward.3 = (bf16[2048,512]{1,0:T(8,128)(2,1)}, bf16[2048,256]{1,0:T(8,128)(2,1)S(1)}, bf16[2048,256]{1,0:T(8,128)(2,1)S(1)}, f32[2,128,128]{2,1,0:T(8,128)S(1)}, bf16[2,128,128]{2,1,0:T(8,128)(2,1)S(1)}) custom-call(bf16[1,512,512]{2,1,0:T(8,128)(2,1)S(1)} %get-tuple-element.36.refs_0_.refs_2_, ...), custom_call_target="tpu_custom_call", output_to_operand_aliasing={{0}: (10, {})} | custom-call | flops 1280385024 | tf_op jit(solution)/shard_map/backward/pallas_call | solution.py:67
  49.2 2.7 %collective-permute-done.11.refs_6_ = bf16[2,128,128]{2,1,0:T(8,128)(2,1)S(1)} collective-permute-done((bf16[2,128,128]{2,1,0:T(8,128)(2,1)S(1)}, bf16[2,128,128]{2,1,0:T(8,128)(2,1)S(1)}, u32[]{:S(2)}, u32[]{:S(2)}) %collective-permute-start.11) | collective-permute-done | bytes 65568 | tf_op jit(solution)/shard_map/ppermute | solution.py:368
  53.0 3.1 %collective-permute-start.8 = (bf16[2,128,128]{2,1,0:T(8,128)(2,1)S(1)}, bf16[2,128,128]{2,1,0:T(8,128)(2,1)S(1)}, u32[]{:S(2)}, u32[]{:S(2)}) collective-permute-start(bf16[2,128,128]{2,1,0:T(8,128)(2,1)S(1)} %add_convert_fusion.2), channel_id=1, source_target_pairs={{0,16},{4,20},{8,24},{12,28},{16,0},{20,4},{24,8},{28,12},{1,17},{... | collective-permute-start | bytes 196616 | tf_op jit(solution)/shard_map/ppermute | solution.py:368
  56.2 2.4 %project.3.refs_5_ = f32[512,2048]{1,0:T(8,128)S(1)} custom-call(bf16[1,512,512]{2,1,0:T(8,128)(2,1)S(1)} %get-tuple-element.51.refs_0_, bf16[1,512,512]{2,1,0:T(8,128)(2,1)S(1)} %collective-permute-done.15.refs_1_, bf16[2048,2048]{1,0:T(8,128)(2,1)S(1)} %copy-done.1), custom_call_target="tpu_custom_call" | custom-call | flops 692099968 | tf_op jit(solution)/shard_map/project/pallas_call | solution.py:67
  59.1 2.9 %later_grads.2 = (bf16[2048,512]{1,0:T(8,128)(2,1)}, bf16[2048,512]{1,0:T(8,128)(2,1)}, f32[8,128]{1,0:T(8,128)S(1)}) custom-call(bf16[2048,512]{1,0:T(8,128)(2,1)S(1)} %copy-done.5, bf16[2048,512]{1,0:T(8,128)(2,1)S(1)} %copy-done.4, bf16[2048,512]{1,0:T(8,128)(2,1)S(1)} %copy-done.2, bf16[2048,512]{1,0:T(8,128)(2,1)S(1)} %get-tuple-element.46.refs_3_, ...), custom_call_target="tpu_custom_call" | custom-call | flops 986242496 | tf_op jit(solution)/shard_map/later_grads/pallas_call | solution.py:67
  62.7 1.7 %collective-permute-done.13.refs_1_.refs_8_ = bf16[2,128,128]{2,1,0:T(8,128)(2,1)S(1)} collective-permute-done((bf16[2,128,128]{2,1,0:T(8,128)(2,1)S(1)}, bf16[2,128,128]{2,1,0:T(8,128)(2,1)S(1)}, u32[]{:S(2)}, u32[]{:S(2)}) %collective-permute-start.13) | collective-permute-done | bytes 65568 | tf_op jit(solution)/shard_map/ppermute | solution.py:368
  64.4 1.3 %project.4 = (f32[512,2048]{1,0:T(8,128)S(1)}, bf16[1,512,512]{2,1,0:T(8,128)(2,1)S(1)}) custom-call(bf16[2,128,128]{2,1,0:T(8,128)(2,1)S(1)} %collective-permute-done.8.refs_8_.refs_0_, bf16[2,128,128]{2,1,0:T(8,128)(2,1)S(1)} %collective-permute-done.13.refs_1_.refs_8_, f32[8,128]{1,0:T(8,128)S(1)} %get-tuple-element.49.refs_2_, ...), custom_call_target="tpu_custom_call" | custom-call | flops 692099968 | tf_op jit(solution)/shard_map/project/pallas_call | solution.py:67
  65.9 3.5 %later_grads.3 = (bf16[2048,512]{1,0:T(8,128)(2,1)}, bf16[2048,512]{1,0:T(8,128)(2,1)}, f32[8,128]{1,0:T(8,128)}) custom-call(bf16[2048,512]{1,0:T(8,128)(2,1)S(1)} %copy-done.5, bf16[2048,512]{1,0:T(8,128)(2,1)S(1)} %copy-done.4, bf16[2048,512]{1,0:T(8,128)(2,1)S(1)} %copy-done.2, ...), custom_call_target="tpu_custom_call", output_to_operand_aliasing={{0}: (9, {}), {1}: (10, {})} | custom-call | flops 986242496 | tf_op jit(solution)/shard_map/later_grads/pallas_call | solution.py:67
  69.3 2.1 %project.5 = bf16[512,2048]{1,0:T(8,128)(2,1)} custom-call(bf16[1,512,512]{2,1,0:T(8,128)(2,1)S(1)} %collective-permute-done.16.refs_0_, bf16[2048,2048]{1,0:T(8,128)(2,1)S(1)} %copy-done.1, f32[512,2048]{1,0:T(8,128)S(1)} %get-tuple-element.54.refs_2_), custom_call_target="tpu_custom_call" | custom-call | flops 692099968 | tf_op jit(solution)/shard_map/project/pallas_call | solution.py:67
  (49 shorter events, 7.6 us)
Async XLA Ops:
  0.6 3.4 %copy-start = (bf16[2048,2048]{1,0:T(8,128)(2,1)S(1)}, bf16[2048,2048]{1,0:T(8,128)(2,1)}, u32[]{:S(2)}) copy-start(bf16[2048,2048]{1,0:T(8,128)(2,1)} %refs_1_.10) | copy-start | bytes 25165828
  5.6 5.4 %copy-start.2 = (bf16[2048,512]{1,0:T(8,128)(2,1)S(1)}, bf16[2048,512]{1,0:T(8,128)(2,1)}, u32[]{:S(2)}) copy-start(bf16[2048,512]{1,0:T(8,128)(2,1)} %refs_2_.11) | copy-start | bytes 6291460
  5.6 14.5 %copy-start.1 = (bf16[2048,2048]{1,0:T(8,128)(2,1)S(1)}, bf16[2048,2048]{1,0:T(8,128)(2,1)}, u32[]{:S(2)}) copy-start(bf16[2048,2048]{1,0:T(8,128)(2,1)} %refs_1_.10) | copy-start | bytes 25165828
  8.0 15.5 %collective-permute-start.1 = (bf16[2,512,256]{2,1,0:T(8,128)(2,1)S(1)}, bf16[2,512,256]{2,1,0:T(8,128)(2,1)S(1)}, u32[]{:S(2)}, u32[]{:S(2)}) collective-permute-start(bf16[2,512,256]{2,1,0:T(8,128)(2,1)S(1)} %get-tuple-element.33.refs_0_), channel_id=1, source_target_pairs={{0,2},{1,3},{2,0},{3,1},{4,6},{5,7},{6,4},{7,5},{8,10},{9,11},{10,... | collective-permute-start | bytes 1572872 | tf_op jit(solution)/shard_map/ppermute | solution.py:358
  12.6 7.5 %copy-start.5 = (bf16[2048,512]{1,0:T(8,128)(2,1)S(1)}, bf16[2048,512]{1,0:T(8,128)(2,1)}, u32[]{:S(2)}) copy-start(bf16[2048,512]{1,0:T(8,128)(2,1)} %refs_0_.5) | copy-start | bytes 6291460
  12.6 7.5 %copy-start.7 = (bf16[512,2048]{1,0:T(8,128)(2,1)S(1)}, bf16[512,2048]{1,0:T(8,128)(2,1)}, u32[]{:S(2)}) copy-start(bf16[512,2048]{1,0:T(8,128)(2,1)} %refs_1_.7) | copy-start | bytes 6291460
  13.4 5.0 %collective-permute-start.2 = (bf16[4,128,128]{2,1,0:T(8,128)(2,1)S(1)}, bf16[4,128,128]{2,1,0:T(8,128)(2,1)S(1)}, u32[]{:S(2)}, u32[]{:S(2)}) collective-permute-start(bf16[4,128,128]{2,1,0:T(8,128)(2,1)S(1)} %get-tuple-element.35.refs_0_), channel_id=1, source_target_pairs={{0,4},{4,0},{8,12},{12,8},{16,20},{20,16},{24,28},{28,24},{1,5},{5... | collective-permute-start | bytes 393224 | tf_op jit(solution)/shard_map/ppermute | solution.py:368
  18.4 5.0 %collective-permute-start.3 = (bf16[4,128,128]{2,1,0:T(8,128)(2,1)S(1)}, bf16[4,128,128]{2,1,0:T(8,128)(2,1)S(1)}, u32[]{:S(2)}, u32[]{:S(2)}) collective-permute-start(bf16[4,128,128]{2,1,0:T(8,128)(2,1)S(1)} %fusion), channel_id=1, source_target_pairs={{0,8},{4,12},{8,0},{12,4},{16,24},{20,28},{24,16},{28,20},{1,9},{5... | collective-permute-start | bytes 393224 | tf_op jit(solution)/shard_map/ppermute | solution.py:368
  22.5 5.0 %copy-start.8 = (bf16[512]{0:T(512)(128)(2,1)S(1)}, bf16[512]{0:T(512)(128)(2,1)}, u32[]{:S(2)}) copy-start(bf16[512]{0:T(512)(128)(2,1)} %param.9) | copy-start | bytes 3076
  22.5 10.2 %copy-start.4 = (bf16[2048,512]{1,0:T(8,128)(2,1)S(1)}, bf16[2048,512]{1,0:T(8,128)(2,1)}, u32[]{:S(2)}) copy-start(bf16[2048,512]{1,0:T(8,128)(2,1)} %refs_1_.11) | copy-start | bytes 6291460
  23.5 13.5 %collective-permute-start.9 = (bf16[2,512,256]{2,1,0:T(8,128)(2,1)S(1)}, bf16[2,512,256]{2,1,0:T(8,128)(2,1)S(1)}, u32[]{:S(2)}, u32[]{:S(2)}) collective-permute-start(bf16[2,512,256]{2,1,0:T(8,128)(2,1)S(1)} %held_back.1), channel_id=1, source_target_pairs={{0,2},{1,3},{2,0},{3,1},{4,6},{5,7},{6,4},{7,5},{8,10},{9,11},{10,... | collective-permute-start | bytes 1572872 | tf_op jit(solution)/shard_map/ppermute | solution.py:358
  24.8 7.9 %collective-permute-start.4 = (bf16[4,128,128]{2,1,0:T(8,128)(2,1)S(1)}, bf16[4,128,128]{2,1,0:T(8,128)(2,1)S(1)}, u32[]{:S(2)}, u32[]{:S(2)}) collective-permute-start(bf16[4,128,128]{2,1,0:T(8,128)(2,1)S(1)} %add_convert_fusion), channel_id=1, source_target_pairs={{0,16},{4,20},{8,24},{12,28},{16,0},{20,4},{24,8},{28,12},{1,17},{... | collective-permute-start | bytes 393224 | tf_op jit(solution)/shard_map/ppermute | solution.py:368
  27.5 10.7 %collective-permute-start = (bf16[1,512,512]{2,1,0:T(8,128)(2,1)S(1)}, bf16[1,512,512]{2,1,0:T(8,128)(2,1)S(1)}, u32[]{:S(2)}, u32[]{:S(2)}) collective-permute-start(bf16[1,512,512]{2,1,0:T(8,128)(2,1)S(1)} %get-tuple-element.37), channel_id=1, source_target_pairs={{0,1},{1,0},{2,3},{3,2},{4,5},{5,4},{6,7},{7,6},{8,9},{9,8},{10,11... | collective-permute-start | bytes 1572872 | tf_op jit(solution)/shard_map/ppermute | solution.py:358
  36.9 1.6 %collective-permute-start.5 = (bf16[1,512,256]{2,1,0:T(8,128)(2,1)S(1)}, bf16[1,512,256]{2,1,0:T(8,128)(2,1)S(1)}, u32[]{:S(2)}, u32[]{:S(2)}) collective-permute-start(bf16[1,512,256]{2,1,0:T(8,128)(2,1)S(1)} %second_part.2), channel_id=1, source_target_pairs={{0,1},{1,0},{2,3},{3,2},{4,5},{5,4},{6,7},{7,6},{8,9},{9,8},{10,11... | collective-permute-start | bytes 786440 | tf_op jit(solution)/shard_map/ppermute | solution.py:358
  37.0 6.7 %collective-permute-start.10 = (bf16[1,512,256]{2,1,0:T(8,128)(2,1)S(1)}, bf16[1,512,256]{2,1,0:T(8,128)(2,1)S(1)}, u32[]{:S(2)}, u32[]{:S(2)}) collective-permute-start(bf16[1,512,256]{2,1,0:T(8,128)(2,1)S(1)} %second_part.3), channel_id=1, source_target_pairs={{0,1},{1,0},{2,3},{3,2},{4,5},{5,4},{6,7},{7,6},{8,9},{9,8},{10,11... | collective-permute-start | bytes 786440 | tf_op jit(solution)/shard_map/ppermute | solution.py:358
  37.6 25.1 %collective-permute-start.14 = (bf16[2,512,512]{2,1,0:T(8,128)(2,1)S(1)}, bf16[2,512,512]{2,1,0:T(8,128)(2,1)S(1)}, u32[]{:S(2)}, u32[]{:S(2)}) collective-permute-start(bf16[2,512,512]{2,1,0:T(8,128)(2,1)S(1)} %get-tuple-element.50), channel_id=1, source_target_pairs={{0,2},{1,3},{2,0},{3,1},{4,6},{5,7},{6,4},{7,5},{8,10},{9,11},{10,... | collective-permute-start | bytes 3145736 | tf_op jit(solution)/shard_map/ppermute | solution.py:358
  38.2 18.0 %collective-permute-start.15 = (bf16[1,512,512]{2,1,0:T(8,128)(2,1)S(1)}, bf16[1,512,512]{2,1,0:T(8,128)(2,1)S(1)}, u32[]{:S(2)}, u32[]{:S(2)}) collective-permute-start(bf16[1,512,512]{2,1,0:T(8,128)(2,1)S(1)} %get-tuple-element.52), channel_id=1, source_target_pairs={{0,1},{1,0},{2,3},{3,2},{4,5},{5,4},{6,7},{7,6},{8,9},{9,8},{10,11... | collective-permute-start | bytes 1572872 | tf_op jit(solution)/shard_map/ppermute | solution.py:358
  42.2 6.0 %collective-permute-start.6 = (bf16[2,128,128]{2,1,0:T(8,128)(2,1)S(1)}, bf16[2,128,128]{2,1,0:T(8,128)(2,1)S(1)}, u32[]{:S(2)}, u32[]{:S(2)}) collective-permute-start(bf16[2,128,128]{2,1,0:T(8,128)(2,1)S(1)} %get-tuple-element.42), channel_id=1, source_target_pairs={{0,4},{4,0},{8,12},{12,8},{16,20},{20,16},{24,28},{28,24},{1,5},{5... | collective-permute-start | bytes 196616 | tf_op jit(solution)/shard_map/ppermute | solution.py:368
  47.6 4.3 %collective-permute-start.11 = (bf16[2,128,128]{2,1,0:T(8,128)(2,1)S(1)}, bf16[2,128,128]{2,1,0:T(8,128)(2,1)S(1)}, u32[]{:S(2)}, u32[]{:S(2)}) collective-permute-start(bf16[2,128,128]{2,1,0:T(8,128)(2,1)S(1)} %get-tuple-element.45), channel_id=1, source_target_pairs={{0,4},{4,0},{8,12},{12,8},{16,20},{20,16},{24,28},{28,24},{1,5},{5... | collective-permute-start | bytes 196616 | tf_op jit(solution)/shard_map/ppermute | solution.py:368
  48.2 4.8 %collective-permute-start.7 = (bf16[2,128,128]{2,1,0:T(8,128)(2,1)S(1)}, bf16[2,128,128]{2,1,0:T(8,128)(2,1)S(1)}, u32[]{:S(2)}, u32[]{:S(2)}) collective-permute-start(bf16[2,128,128]{2,1,0:T(8,128)(2,1)S(1)} %fusion.1), channel_id=1, source_target_pairs={{0,8},{4,12},{8,0},{12,4},{16,24},{20,28},{24,16},{28,20},{1,9},{5... | collective-permute-start | bytes 196616 | tf_op jit(solution)/shard_map/ppermute | solution.py:368
  52.0 6.6 %collective-permute-start.12 = (bf16[2,128,128]{2,1,0:T(8,128)(2,1)S(1)}, bf16[2,128,128]{2,1,0:T(8,128)(2,1)S(1)}, u32[]{:S(2)}, u32[]{:S(2)}) collective-permute-start(bf16[2,128,128]{2,1,0:T(8,128)(2,1)S(1)} %fusion.2), channel_id=1, source_target_pairs={{0,8},{4,12},{8,0},{12,4},{16,24},{20,28},{24,16},{28,20},{1,9},{5... | collective-permute-start | bytes 196616 | tf_op jit(solution)/shard_map/ppermute | solution.py:368
  53.0 6.1 %collective-permute-start.8 = (bf16[2,128,128]{2,1,0:T(8,128)(2,1)S(1)}, bf16[2,128,128]{2,1,0:T(8,128)(2,1)S(1)}, u32[]{:S(2)}, u32[]{:S(2)}) collective-permute-start(bf16[2,128,128]{2,1,0:T(8,128)(2,1)S(1)} %add_convert_fusion.2), channel_id=1, source_target_pairs={{0,16},{4,20},{8,24},{12,28},{16,0},{20,4},{24,8},{28,12},{1,17},{... | collective-permute-start | bytes 196616 | tf_op jit(solution)/shard_map/ppermute | solution.py:368
  58.6 5.9 %collective-permute-start.13 = (bf16[2,128,128]{2,1,0:T(8,128)(2,1)S(1)}, bf16[2,128,128]{2,1,0:T(8,128)(2,1)S(1)}, u32[]{:S(2)}, u32[]{:S(2)}) collective-permute-start(bf16[2,128,128]{2,1,0:T(8,128)(2,1)S(1)} %add_convert_fusion.1), channel_id=1, source_target_pairs={{0,16},{4,20},{8,24},{12,28},{16,0},{20,4},{24,8},{28,12},{1,17},{... | collective-permute-start | bytes 196616 | tf_op jit(solution)/shard_map/ppermute | solution.py:368
  65.8 3.6 %collective-permute-start.16 = (bf16[1,512,512]{2,1,0:T(8,128)(2,1)S(1)}, bf16[1,512,512]{2,1,0:T(8,128)(2,1)S(1)}, u32[]{:S(2)}, u32[]{:S(2)}) collective-permute-start(bf16[1,512,512]{2,1,0:T(8,128)(2,1)S(1)} %get-tuple-element.53), channel_id=1, source_target_pairs={{0,1},{1,0},{2,3},{3,2},{4,5},{5,4},{6,7},{7,6},{8,9},{9,8},{10,11... | collective-permute-start | bytes 1572872 | tf_op jit(solution)/shard_map/ppermute | solution.py:358
  (2 other events, 3.2 us)
